TPU v7x, 32 devices: a whole 2x2x4 slice. The times are simulated.
32 devices in a mesh: dp: 16 (over z, y, core), tensor: 2 (over x).
Axes of the slice: x: 2, y: 2, z: 4, core: 2. Of those that a mesh axis runs over, the one named last changes fastest.
Arguments:
- tokens: bfloat16 [25088, 512], P(('dp', 'tensor')), may hold values from -6 to 6
- cotangent: bfloat16 [25088, 512], P(('dp', 'tensor')), may hold values from -6 to 6
- image_counts: int32 [16], replicated, may hold values from 2 to 8, as said below
- w_in: float32 [512, 1536], P(None, 'tensor'), may hold values from -0.25 to 0.25
- m_in: float32 [512, 1536], P(None, 'tensor'), may hold values from -448 to 448
- v_in: float32 [512, 1536], P(None, 'tensor'), may hold values from 2007.04 to 8028.16
- w_out: float32 [512, 512], P('tensor'), may hold values from -1.5 to 1.5
- m_out: float32 [512, 512], P('tensor'), may hold values from -168 to 168
- v_out: float32 [512, 512], P('tensor'), may hold values from 282.24 to 1128.96
- w_up: float32 [512, 2048], P(None, 'tensor'), may hold values from -0.25 to 0.25
- m_up: float32 [512, 2048], P(None, 'tensor'), may hold values from -336 to 336
- v_up: float32 [512, 2048], P(None, 'tensor'), may hold values from 1128.96 to 4515.84
- w_down: float32 [2048, 512], P('tensor'), may hold values from -0.125 to 0.125
- m_down: float32 [2048, 512], P('tensor'), may hold values from -672 to 672
- v_down: float32 [2048, 512], P('tensor'), may hold values from 4515.84 to 18063.36
- kernel: float32 [9, 512], P(None, 'tensor'), may hold values from -12 to 12
- m_kernel: float32 [9, 512], P(None, 'tensor'), may hold values from -224 to 224
- v_kernel: float32 [9, 512], P(None, 'tensor'), may hold values from 501.76 to 2007.04
- up_bias: float32 [2048], P('tensor'), may hold values from -1.5 to 1.5
- m_bias: float32 [2048], P('tensor'), may hold values from -336 to 336
- v_bias: float32 [2048], P('tensor'), may hold values from 1128.96 to 4515.84
- vectors: float32 [7, 512], replicated, may hold values from -0.9 to 1.45
- m_vectors: float32 [7, 512], P(None, 'tensor'), may hold values from -784 to 784
- v_vectors: float32 [7, 512], P(None, 'tensor'), may hold values from 6146.56 to 24586.24
Outputs:
- output: bfloat16 [25088, 512], P(('dp', 'tensor'))
- grad_in: float32 [25088, 512], P(('dp', 'tensor'))
- new_w_in: float32 [512, 1536], P(None, 'tensor')
- new_m_in: float32 [512, 1536], P(None, 'tensor')
- new_v_in: float32 [512, 1536], P(None, 'tensor')
- copy_w_in: bfloat16 [512, 1536], P(None, 'tensor')
- new_w_out: float32 [512, 512], P('tensor')
- new_m_out: float32 [512, 512], P('tensor')
- new_v_out: float32 [512, 512], P('tensor')
- copy_w_out: bfloat16 [512, 512], P('tensor')
- new_w_up: float32 [512, 2048], P(None, 'tensor')
- new_m_up: float32 [512, 2048], P(None, 'tensor')
- new_v_up: float32 [512, 2048], P(None, 'tensor')
- copy_w_up: bfloat16 [512, 2048], P(None, 'tensor')
- new_w_down: float32 [2048, 512], P('tensor')
- new_m_down: float32 [2048, 512], P('tensor')
- new_v_down: float32 [2048, 512], P('tensor')
- copy_w_down: bfloat16 [2048, 512], P('tensor')
- new_kernel: float32 [9, 512], P(None, 'tensor')
- new_m_kernel: float32 [9, 512], P(None, 'tensor')
- new_v_kernel: float32 [9, 512], P(None, 'tensor')
- new_up_bias: float32 [2048], P('tensor')
- new_m_bias: float32 [2048], P('tensor')
- new_v_bias: float32 [2048], P('tensor')
- new_vectors: float32 [7, 512], P(None, 'tensor')
- new_m_vectors: float32 [7, 512], P(None, 'tensor')
- new_v_vectors: float32 [7, 512], P(None, 'tensor')
Inputs may be any that keep to these rules, and one draw needn't show every extreme that they name: image_counts[i] images of dp group i are live, in its first slots; some group has all 8 slots live and some group the fewest.
All inputs are finite; a program needn't handle non-finite values.
Results may differ from a plain program's by a relative error of at most 0.01145.
The roundings to bfloat16 on the way count: a program that leaves them out, or rounds other values in their place, can miss the bound.
Values may be sent and summed in bfloat16 or wider, within the bound.
A program may use at most 192 MiB of HBM per device.

v0:
```python
import jax
import jax.numpy as jnp
from jax import lax
from jax.sharding import PartitionSpec as P

D = 512
HD = 32
FF = 2048
SIDE = 14
STEP = 5


beta_one = 0.5
beta_two = 0.5
epsilon = 1e-08
decay = 0.05
norm_eps = 1e-05


def narrow(values):
    return values.astype(jnp.bfloat16)


def product(left_side, right_side):
    return jnp.dot(left_side, right_side, preferred_element_type=jnp.float32)


def grad_product(left_side, right_side):
    return lax.dot_general(
        left_side, right_side, (((0,), (0,)), ((), ())), preferred_element_type=jnp.float32
    )


def layer_norm(values, gain_row, shift_row):
    centred = values - jnp.mean(values, axis=-1, keepdims=True)
    variance = jnp.mean(centred * centred, axis=-1, keepdims=True)
    return centred * lax.rsqrt(variance + norm_eps) * gain_row + shift_row


def spatial(grid_field, tap_table):
    padded = jnp.pad(grid_field, ((0, 0), (1, 1), (1, 1), (0, 0)))
    summed = jnp.zeros_like(grid_field)
    for row_step in range(3):
        for col_step in range(3):
            summed = (
                summed
                + tap_table[3 * row_step + col_step]
                * padded[:, row_step : row_step + SIDE, col_step : col_step + SIDE, :]
            )
    return summed


def generate(gen_pre, kernel):
    image_count, window, channels = gen_pre.shape
    grid_field = jax.nn.gelu(gen_pre).reshape(image_count, SIDE, SIDE, channels)
    convolved = spatial(grid_field, kernel)
    pooled = spatial(convolved, jnp.full((9, channels), 1.0 / 9.0, jnp.float32))
    return pooled.reshape(image_count, window, channels) * HD ** (-0.5)


def rates():
    return (
        (D ** (-0.5), decay),
        ((D // 32) ** (-0.5), decay),
        (D ** (-0.5), decay),
        (FF ** (-0.5), decay),
        (2.0, decay),
        (0.3, 0.0),
        (0.3, 0.0),
    )


def adam_step(weight, first_moment, second, gradient, setting):
    step_rate, shrink = setting
    first_moment = beta_one * first_moment + (1.0 - beta_one) * gradient
    second = beta_two * second + (1.0 - beta_two) * gradient * gradient
    first_hat = first_moment / (1.0 - beta_one**STEP)
    second_hat = second / (1.0 - beta_two**STEP)
    weight = weight - step_rate * (first_hat / (jnp.sqrt(second_hat) + epsilon) + shrink * weight)
    return (weight, first_moment, second)


def local(
    tokens,
    cotangent,
    image_counts,
    w_in,
    m_in,
    v_in,
    w_out,
    m_out,
    v_out,
    w_up,
    m_up,
    v_up,
    w_down,
    m_down,
    v_down,
    kernel,
    m_kernel,
    v_kernel,
    up_bias,
    m_bias,
    v_bias,
    vectors,
    m_vectors,
    v_vectors,
):
    row_count = tokens.shape[0]
    window = SIDE * SIDE
    tensor_place = lax.axis_index("tensor")
    row_index = tensor_place * row_count + jnp.arange(row_count, dtype=jnp.int32)
    live_rows = (row_index // window < image_counts[lax.axis_index("dp")]).astype(jnp.float32)[
        :, None
    ]
    inputs = tokens.astype(jnp.float32)
    cotan_rows = cotangent.astype(jnp.float32) * live_rows
    norm_a = narrow(layer_norm(inputs, vectors[0], vectors[1]))
    low_in, low_out, low_up, low_down = (
        lax.all_gather(narrow(w_in), "tensor", axis=1, tiled=True),
        lax.all_gather(narrow(w_out), "tensor", axis=0, tiled=True),
        lax.all_gather(narrow(w_up), "tensor", axis=1, tiled=True),
        lax.all_gather(narrow(w_down), "tensor", axis=0, tiled=True),
    )
    taps_in, bias_in = (
        lax.all_gather(kernel, "tensor", axis=1, tiled=True),
        lax.all_gather(up_bias, "tensor", axis=0, tiled=True),
    )
    image_count = norm_a.shape[0] // window
    local_heads = low_in.shape[1] // (3 * HD)
    width = local_heads * HD
    proj = product(norm_a, low_in).reshape(image_count, window, local_heads, 3, HD)
    gen_pre = proj[:, :, :, 0, :].reshape(image_count, window, width)
    keys = narrow(proj[:, :, :, 1, :])
    values = narrow(proj[:, :, :, 2, :])
    queries = narrow(generate(gen_pre, taps_in)).reshape(image_count, window, local_heads, HD)
    scores = jnp.einsum("nqhc,nkhc->nhqk", queries, keys, preferred_element_type=jnp.float32)
    top_score = jnp.max(scores, axis=-1, keepdims=True)
    exp_scores = jnp.exp(scores - top_score)
    totals = jnp.sum(exp_scores, axis=-1, keepdims=True)
    log_total = top_score + jnp.log(totals)
    probs = narrow(exp_scores / totals)
    mixed = narrow(
        jnp.einsum("nhqk,nkhc->nqhc", probs, values, preferred_element_type=jnp.float32)
    ).reshape(image_count * window, width)
    attn = product(mixed, low_out)
    after_attn = inputs + vectors[4] * attn
    norm_b = narrow(layer_norm(after_attn, vectors[2], vectors[3]))
    pre_hidden = product(norm_b, low_up) + bias_in
    hidden = narrow(jax.nn.gelu(pre_hidden))
    branch = product(hidden, low_down)
    finished = after_attn + vectors[5] * (branch + vectors[6])
    result = narrow(finished * live_rows)
    d_branch = vectors[5] * cotan_rows
    grad_mlp_scale = jnp.sum(cotan_rows * (branch + vectors[6]), axis=0)
    grad_down_bias = jnp.sum(d_branch, axis=0)
    low_branch = narrow(d_branch)
    d_hidden = product(low_branch, low_down.T)
    grad_w_down = grad_product(hidden, low_branch)
    gelu_pull = jax.vjp(jax.nn.gelu, pre_hidden)[1]
    d_pre = narrow(gelu_pull(d_hidden)[0])
    grad_up_bias = jnp.sum(d_pre, axis=0, dtype=jnp.float32)
    grad_w_up = grad_product(norm_b, d_pre)
    d_norm_b = product(d_pre, low_up.T)
    second_pull = jax.vjp(layer_norm, after_attn, vectors[2], vectors[3])[1]
    d_after_norm, grad_gain_b, grad_shift_b = second_pull(d_norm_b)
    d_after = cotan_rows + d_after_norm
    grad_attn_scale = jnp.sum(d_after * attn, axis=0)
    low_attn = narrow(vectors[4] * d_after)
    d_mixed = narrow(product(low_attn, low_out.T)).reshape(image_count, window, local_heads, HD)
    grad_w_out = grad_product(mixed, low_attn)
    again = jnp.einsum("nqhc,nkhc->nhqk", queries, keys, preferred_element_type=jnp.float32)
    soft_probs = jnp.exp(again - log_total)
    d_probs = jnp.einsum("nqhc,nkhc->nhqk", d_mixed, values, preferred_element_type=jnp.float32)
    d_values = jnp.einsum("nhqk,nqhc->nkhc", probs, d_mixed, preferred_element_type=jnp.float32)
    inner = jnp.sum(soft_probs * d_probs, axis=-1, keepdims=True)
    d_scores = narrow(soft_probs * (d_probs - inner))
    d_queries = jnp.einsum("nhqk,nkhc->nqhc", d_scores, keys, preferred_element_type=jnp.float32)
    d_keys = jnp.einsum("nhqk,nqhc->nkhc", d_scores, queries, preferred_element_type=jnp.float32)
    gen_pull = jax.vjp(generate, gen_pre, taps_in)[1]
    d_gen, grad_kernel = gen_pull(d_queries.reshape(image_count, window, width))
    d_proj = narrow(
        jnp.stack([d_gen.reshape(image_count, window, local_heads, HD), d_keys, d_values], axis=3)
    ).reshape(image_count * window, 3 * width)
    grad_w_in = grad_product(norm_a, d_proj)
    d_norm_a = product(d_proj, low_in.T)
    first_pull = jax.vjp(layer_norm, inputs, vectors[0], vectors[1])[1]
    d_input_norm, grad_gain_a, grad_shift_a = first_pull(d_norm_a)
    grad_in = d_after + d_input_norm
    vector_grads = jnp.stack(
        [
            grad_gain_a,
            grad_shift_a,
            grad_gain_b,
            grad_shift_b,
            grad_attn_scale,
            grad_mlp_scale,
            grad_down_bias,
        ]
    )
    owned = (
        lax.psum_scatter(grad_w_in, "tensor", scatter_dimension=1, tiled=True),
        lax.psum_scatter(grad_w_out, "tensor", scatter_dimension=0, tiled=True),
        lax.psum_scatter(grad_w_up, "tensor", scatter_dimension=1, tiled=True),
        lax.psum_scatter(grad_w_down, "tensor", scatter_dimension=0, tiled=True),
        lax.psum_scatter(grad_kernel, "tensor", scatter_dimension=1, tiled=True),
        lax.psum_scatter(grad_up_bias, "tensor", scatter_dimension=0, tiled=True),
        lax.psum_scatter(vector_grads, "tensor", scatter_dimension=1, tiled=True),
    )
    g_in, g_out, g_up, g_down, g_kernel, g_bias, g_vectors = lax.psum(
        (owned[0], owned[1], owned[2], owned[3], owned[4], owned[5], owned[6]), "dp"
    )
    vector_width = m_vectors.shape[1]
    own_vectors = lax.dynamic_slice_in_dim(vectors, tensor_place * vector_width, vector_width, 1)
    rate_table = rates()
    new_w_in, new_m_in, new_v_in = adam_step(w_in, m_in, v_in, g_in, rate_table[0])
    new_w_out, new_m_out, new_v_out = adam_step(w_out, m_out, v_out, g_out, rate_table[1])
    new_w_up, new_m_up, new_v_up = adam_step(w_up, m_up, v_up, g_up, rate_table[2])
    new_w_down, new_m_down, new_v_down = adam_step(w_down, m_down, v_down, g_down, rate_table[3])
    new_kernel, new_m_kernel, new_v_kernel = adam_step(
        kernel, m_kernel, v_kernel, g_kernel, rate_table[4]
    )
    new_up_bias, new_m_bias, new_v_bias = adam_step(up_bias, m_bias, v_bias, g_bias, rate_table[5])
    new_vectors, new_m_vectors, new_v_vectors = adam_step(
        own_vectors, m_vectors, v_vectors, g_vectors, rate_table[6]
    )
    return (
        result,
        grad_in,
        new_w_in,
        new_m_in,
        new_v_in,
        narrow(new_w_in),
        new_w_out,
        new_m_out,
        new_v_out,
        narrow(new_w_out),
        new_w_up,
        new_m_up,
        new_v_up,
        narrow(new_w_up),
        new_w_down,
        new_m_down,
        new_v_down,
        narrow(new_w_down),
        new_kernel,
        new_m_kernel,
        new_v_kernel,
        new_up_bias,
        new_m_bias,
        new_v_bias,
        new_vectors,
        new_m_vectors,
        new_v_vectors,
    )


def solution(mesh):
    placed = (
        P(("dp", "tensor"), None),
        P(("dp", "tensor"), None),
        P(),
        P(None, "tensor"),
        P(None, "tensor"),
        P(None, "tensor"),
        P("tensor", None),
        P("tensor", None),
        P("tensor", None),
        P(None, "tensor"),
        P(None, "tensor"),
        P(None, "tensor"),
        P("tensor", None),
        P("tensor", None),
        P("tensor", None),
        P(None, "tensor"),
        P(None, "tensor"),
        P(None, "tensor"),
        P("tensor"),
        P("tensor"),
        P("tensor"),
        P(),
        P(None, "tensor"),
        P(None, "tensor"),
    )
    return jax.shard_map(
        local,
        mesh=mesh,
        in_specs=placed,
        out_specs=(
            P(("dp", "tensor"), None),
            P(("dp", "tensor"), None),
            P(None, "tensor"),
            P(None, "tensor"),
            P(None, "tensor"),
            P(None, "tensor"),
            P("tensor", None),
            P("tensor", None),
            P("tensor", None),
            P("tensor", None),
            P(None, "tensor"),
            P(None, "tensor"),
            P(None, "tensor"),
            P(None, "tensor"),
            P("tensor", None),
            P("tensor", None),
            P("tensor", None),
            P("tensor", None),
            P(None, "tensor"),
            P(None, "tensor"),
            P(None, "tensor"),
            P("tensor"),
            P("tensor"),
            P("tensor"),
            P(None, "tensor"),
            P(None, "tensor"),
            P(None, "tensor"),
        ),
        check_vma=False,
    )
```

profile of v0, /device:TPU:0, one launch (start us, length us, event | category | flops | bytes accessed | tf_op | source)
XLA Modules:
  0.0 607.0 jit_solution(1674829801840698082)
XLA Ops:
  15.2 5.3 all_gather.19
  20.6 14.7 %all_gather.20 = bf16[512,512]{1,0:T(8,128)(2,1)} all-gather(bf16[256,512]{1,0:T(8,128)(2,1)S(1)} %convert_element_type.111), channel_id=1, replica_groups=mesh['dp'=16,'tensor'=2] {'tensor'}, dimensions={0}, use_global_device_ids=true | all-gather | bytes 786432 | tf_op jit(solution)/shard_map/all_gather | solution.py:121
  35.3 4.4 all_gather.22
  40.9 4.7 all-gather.4.cloned.1.call-done
  45.6 5.9 fusion.69
  51.5 9.3 %reshape.225 = f32[4,196,16,3,32]{1,0,4,3,2:T(4,128)} reshape(f32[784,1536]{0,1:T(8,128)} %fusion.69) | data formatting | bytes 9633792 | tf_op jit(solution)/shard_map/reshape | solution.py:132
  60.8 4.0 copy.78
  69.2 5.4 copy.80
  74.6 4.8 reshape_squeeze.3
  89.1 4.7 copy.81
  93.8 3.2 fusion.90
  97.0 4.7 copy-done
  104.7 11.0 %divide_convert_fusion = bf16[4,16,196,196]{2,3,1,0:T(8,128)(2,1)} fusion(f32[4,16,196,196]{2,3,1,0:T(8,128)} %copy-done, f32[4,16,196]{2,1,0:T(8,128)S(1)} %fusion, f32[4,16,196]{2,1,0:T(8,128)S(1)} %get-tuple-element.110), kind=kLoop, calls=%fused_computation.3 | loop fusion | flops 7375872 | bytes 14852096 | tf_op jit(solution)/shard_map/convert_element_type | solution.py:21
  115.6 4.5 fusion.47
  122.8 3.4 fusion.87
  127.0 7.4 %multiply_convert_fusion.1 = (bf16[784,2048]{1,0:T(8,128)(2,1)}, f32[784,2048]{1,0:T(8,128)}) fusion(f32[2048]{0:T(1024)S(1)} %all_gather.22, bf16[512,2048]{1,0:T(8,128)(2,1)} %all-gather.6.cloned.1.call-done, f32[784,512]{1,0:T(8,128)S(1)} %get-tuple-element.82, f32[512]{0:T(512)S(1)} %bitcast.106, f32[512]{0:T(512)S(1)} %bitcast.102, ...), kind=kOutput, calls=%fused_computation.16 | convolution fusion | flops 1662230528 | bytes 13355136 | tf_op jit(solution)/shard_map/dot_general | solution.py:25
  134.4 8.7 %convert_reduce_fusion = (f32[2048]{0:T(1024)S(1)}, bf16[784,2048]{1,0:T(8,128)(2,1)S(1)}) fusion(f32[784,2048]{1,0:T(8,128)} %get-tuple-element.115, f32[2048]{0:T(1024)S(1)} %all_gather.22, bf16[2048,512]{1,0:T(8,128)(2,1)} %all-gather.8.cloned.1.call-done, bf16[784,512]{1,0:T(8,128)(2,1)} %param.25, f32[784]{0:T(1024)S(1)} %fusion.63, f32[512]{0:T(512)S(1)} %bitcast.144), kind=kOutput, calls=%fused_computation.15 | convolution fusion | flops 1682700288 | bytes 12555328 | tf_op jit(solution)/shard_map/dot_general | solution.py:25
  152.4 4.1 reshape.227
  156.5 13.2 %multiply_reduce_fusion = (f32[4,16,196]{2,1,0:T(8,128)S(1)}, f32[4,16,196,196]{2,3,1,0:T(8,128)}) fusion(f32[4,16,196,196]{2,3,1,0:T(8,128)} %copy-done, f32[4,16,196]{2,1,0:T(8,128)S(1)} %log_add_fusion, bf16[4,196,16,3,32]{1,4,2,0,3:T(8,128)(2,1)} %copy.105, bf16[4,196,16,32]{1,0,3,2:T(4,128)(2,1)} %reshape.227), kind=kOutput, calls=%fused_computation.1 | convolution fusion | flops 164715264 | bytes 25139200 | tf_op jit(solution)/shard_map/nqhc,nkhc->nhqk/dot_general | solution.py:174
  169.7 6.3 %multiply_convert_fusion = bf16[4,16,196,196]{2,3,1,0:T(8,128)(2,1)S(1)} fusion(f32[4,16,196,196]{2,3,1,0:T(8,128)} %get-tuple-element.117, f32[4,16,196,196]{2,3,1,0:T(8,128)S(1)} %bitcast.101, f32[4,16,196]{2,1,0:T(8,128)S(1)} %get-tuple-element.116, f32[4,16,196]{2,1,0:T(8,128)S(1)} %log_add_fusion), kind=kLoop, calls=%fused_computation | loop fusion | flops 9834496 | bytes 24686592 | tf_op jit(solution)/shard_map/convert_element_type | solution.py:21
  178.8 3.9 multiply_bitcast_fusion
  182.6 6.7 %copy.87 = f32[4,196,16,32]{3,2,0,1:T(8,128)} copy(f32[4,196,16,32]{1,3,2,0:T(8,128)} %multiply_bitcast_fusion) | data formatting | bytes 3211264 | tf_op jit(solution)/shard_map/transpose(jvp())/mul | solution.py:47
  189.3 5.7 mul.791
  195.0 3.5 pad_add_fusion.1
  198.5 5.8 multiply_reduce_fusion.12
  204.4 3.8 broadcast_multiply_fusion
  211.9 5.6 reshape.228
  217.5 6.2 %copy.88 = f32[4,196,16,1,32]{1,4,2,0,3:T(8,128)} copy(f32[4,196,16,1,32]{4,2,0,1,3:T(8,128)} %reshape.228) | data formatting | bytes 3211264 | tf_op jit(solution)/shard_map/transpose(jvp())/reshape | solution.py:55
  223.8 5.2 fusion.49
  229.0 5.3 fusion.48
  238.1 4.7 copy.94
  242.8 6.8 %convert_element_type.124 = bf16[784,1536]{0,1:T(8,128)(2,1)} reshape(bf16[4,196,16,3,32]{1,0,4,3,2:T(4,128)(2,1)} %copy.94) | data formatting | bytes 4816896 | tf_op jit(solution)/shard_map/convert_element_type | solution.py:21
  249.6 5.7 fusion.67
  255.8 6.8 %fusion.72 = f32[512,2048]{1,0:T(8,128)} fusion(bf16[784,2048]{1,0:T(8,128)(2,1)} %copy-done.15, f32[784,512]{1,0:T(8,128)S(1)} %get-tuple-element.82, f32[512]{0:T(512)S(1)} %bitcast.107, f32[512]{0:T(512)S(1)} %bitcast.105, f32[784]{0:T(1024)S(1)} %fusion.66, f32[784]{0:T(1024)S(1)} %broadcast_multiply_fusion.9), kind=kOutput, calls=%fused_computation.190 | convolution fusion | flops 1646174208 | bytes 9021568 | tf_op jit(solution)/shard_map/dot_general | solution.py:29
  262.7 6.6 %fusion.56 = f32[2048,512]{1,0:T(8,128)} fusion(bf16[784,2048]{1,0:T(8,128)(2,1)} %get-tuple-element.114, bf16[784,512]{1,0:T(8,128)(2,1)} %param.25, f32[784]{0:T(1024)S(1)} %fusion.63, f32[512]{0:T(512)S(1)} %bitcast.145), kind=kOutput, calls=%fused_computation.154 | convolution fusion | flops 1645772800 | bytes 8213568 | tf_op jit(solution)/shard_map/dot_general | solution.py:29
  269.4 4.3 fusion.74
  275.4 3.9 fusion.44
  280.7 18.3 %reduce-scatter.7.cloned.1.call-done = f32[512,768]{1,0:T(8,128)} async-done(((f32[512,1536]{1,0:T(8,128)}), f32[512,768]{1,0:T(8,128)}) %reduce-scatter.7.cloned.1.call-update) | async-done | bytes 1572880 | tf_op jit(solution)/shard_map/reduce_scatter | solution.py:202
  299.0 56.5 %reduce-scatter.11.cloned.1.call-done = f32[512,1024]{1,0:T(8,128)} async-done(((f32[512,2048]{1,0:T(8,128)}), f32[512,1024]{1,0:T(8,128)}) %reduce-scatter.11.cloned.1.call-update) | async-done | bytes 2097168 | tf_op jit(solution)/shard_map/reduce_scatter | solution.py:204
  355.5 56.7 %reduce-scatter.13.cloned.1.call-done = f32[1024,512]{1,0:T(8,128)} async-done(((f32[2048,512]{1,0:T(8,128)}), f32[1024,512]{1,0:T(8,128)}) %reduce-scatter.13.cloned.1.call-update) | async-done | bytes 2097168 | tf_op jit(solution)/shard_map/reduce_scatter | solution.py:205
  414.2 5.0 all-reduce.29
  419.2 5.7 reduce-scatter.17.cloned.1.call-done
  424.8 12.6 %reduce-scatter.15.cloned.1.call-done = f32[9,256]{1,0:T(8,128)} async-done(((f32[9,512]{1,0:T(8,128)}), f32[9,256]{1,0:T(8,128)}) %reduce-scatter.15.cloned.1.call-update) | async-done | bytes 9232 | tf_op jit(solution)/shard_map/reduce_scatter | solution.py:206
  437.4 63.4 %all-reduce.30 = (f32[9,256]{1,0:T(8,128)S(1)}, f32[1024]{0:T(1024)S(1)}, f32[7,256]{1,0:T(8,128)S(1)}) all-reduce(f32[9,256]{1,0:T(8,128)} %reduce-scatter.15.cloned.1.call-done, f32[1024]{0:T(1024)S(1)} %dynamic-slice.1, f32[7,256]{1,0:T(8,128)} %reduce-scatter.17.cloned.1.call-done), channel_id=1, replica_groups=mesh['dp'=16,'tensor'=2] {'dp'}, use_global_device_ids=true, to_apply=%region_29.30 | all-reduce | flops 5120 | bytes 40960 | tf_op jit(solution)/shard_map/psum | solution.py:210
  502.8 79.2 %all-reduce.34.cloned.1.call-done = (f32[512,768]{1,0:T(8,128)}, f32[256,512]{1,0:T(8,128)}, f32[512,1024]{1,0:T(8,128)}, f32[1024,512]{1,0:T(8,128)}) async-done(((f32[512,768]{1,0:T(8,128)}, f32[256,512]{1,0:T(8,128)}, f32[512,1024]{1,0:T(8,128)}, f32[1024,512]{1,0:T(8,128)}), (f32[512,768]{1,0:T(8,128)}, f32[256,512]{1,0:T(8,128)}, f32[512,1024]{1,0:T(8,128)}, ...) | async-done | bytes 6291472 | tf_op jit(solution)/shard_map/psum | solution.py:210
  582.0 5.3 fusion.84
  589.8 4.5 fusion.80
  595.8 4.1 fusion.78
  (186 shorter events, 59.9 us)
Async XLA Ops:
  7.2 38.4 %all-gather.4.cloned.1.call-start = ((), (), s32[]{:S(2)}) async-start(), calls=%async_computation.6 | async-start | bytes 2359296 | tf_op jit(solution)/shard_map/all_gather | solution.py:120
  9.8 117.2 %all-gather.6.cloned.1.call-start = ((), (), s32[]{:S(2)}) async-start(), calls=%async_computation.7 | async-start | bytes 3145728 | tf_op jit(solution)/shard_map/all_gather | solution.py:122
  11.0 123.4 %all-gather.8.cloned.1.call-start = ((), (), s32[]{:S(2)}) async-start(), calls=%async_computation.8 | async-start | bytes 3145728 | tf_op jit(solution)/shard_map/all_gather | solution.py:123
  13.8 6.7 %copy-start.22 = (f32[256,512]{1,0:T(8,128)S(1)}, f32[256,512]{1,0:T(8,128)}, u32[]{:S(2)}) copy-start(f32[256,512]{1,0:T(8,128)} %param.30) | copy-start | bytes 1572868
  13.9 266.8 %reduce-scatter.9.cloned.1.call-start = ((), (), s32[]{:S(2)}) async-start(), calls=%async_computation.10 | async-start | bytes 1572864 | tf_op jit(solution)/shard_map/reduce_scatter | solution.py:203
  14.5 20.8 %copy-start.40 = (f32[1024]{0:T(1024)S(1)}, f32[1024]{0:T(1024)}, u32[]{:S(2)}) copy-start(f32[1024]{0:T(1024)} %param.42) | copy-start | bytes 12292
  14.5 25.2 %copy-start.51 = (s32[16]{0:T(128)S(1)}, s32[16]{0:T(128)}, u32[]{:S(2)}) copy-start(s32[16]{0:T(128)} %param.26) | copy-start | bytes 196
  15.2 36.3 %copy-start.34 = (f32[784]{0:T(1024)}, f32[784]{0:T(1024)S(1)}, u32[]{:S(2)}) copy-start(f32[784]{0:T(1024)S(1)} %fusion.34) | copy-start | bytes 9412
  60.8 4.6 copy-start.2
  97.0 4.7 copy-start
  134.4 8.7 %copy-start.48 = (bf16[512,2048]{1,0:T(8,128)(2,1)S(1)}, bf16[512,2048]{1,0:T(8,128)(2,1)}, u32[]{:S(2)}) copy-start(bf16[512,2048]{1,0:T(8,128)(2,1)} %all-gather.6.cloned.1.call-done) | copy-start | bytes 6291460
  152.4 17.3 %slice-start = ((s8[13107200]{0:T(1024)(128)(4,1)}), s8[524288]{0:T(1024)(128)(4,1)S(1)}, s32[]{:S(2)}) async-start(s8[13107200]{0:T(1024)(128)(4,1)} %bitcast.100), calls=%async_computation.16 | async-start | bytes 1048576
  156.5 13.2 %slice-start.1 = ((s8[13107200]{0:T(1024)(128)(4,1)}), s8[4194304]{0:T(1024)(128)(4,1)S(1)}, s32[]{:S(2)}) async-start(s8[13107200]{0:T(1024)(128)(4,1)} %bitcast.100), calls=%async_computation.17 | async-start | bytes 8388608
  156.5 13.2 %slice-start.2 = ((s8[13107200]{0:T(1024)(128)(4,1)}), s8[4194304]{0:T(1024)(128)(4,1)S(1)}, s32[]{:S(2)}) async-start(s8[13107200]{0:T(1024)(128)(4,1)} %bitcast.100), calls=%async_computation.18 | async-start | bytes 8388608
  156.5 13.2 %slice-start.3 = ((s8[13107200]{0:T(1024)(128)(4,1)}), s8[4194304]{0:T(1024)(128)(4,1)S(1)}, s32[]{:S(2)}) async-start(s8[13107200]{0:T(1024)(128)(4,1)} %bitcast.100), calls=%async_computation.19 | async-start | bytes 8388608
  223.7 75.3 %reduce-scatter.7.cloned.1.call-start = ((), (), s32[]{:S(2)}) async-start(), calls=%async_computation.9 | async-start | bytes 4718592 | tf_op jit(solution)/shard_map/reduce_scatter | solution.py:202
  229.0 5.4 copy-start.12
  242.8 6.8 %copy-start.8 = (bf16[784,512]{1,0:T(8,128)(2,1)S(1)}, bf16[784,512]{1,0:T(8,128)(2,1)}, u32[]{:S(2)}) copy-start(bf16[784,512]{1,0:T(8,128)(2,1)} %param.24) | copy-start | bytes 2408452
  255.3 100.2 %reduce-scatter.11.cloned.1.call-start = ((), (), s32[]{:S(2)}) async-start(), calls=%async_computation.11 | async-start | bytes 6291456 | tf_op jit(solution)/shard_map/reduce_scatter | solution.py:204
  262.6 149.7 %reduce-scatter.13.cloned.1.call-start = ((), (), s32[]{:S(2)}) async-start(), calls=%async_computation.12 | async-start | bytes 6291456 | tf_op jit(solution)/shard_map/reduce_scatter | solution.py:205
  269.3 155.5 %reduce-scatter.17.cloned.1.call-start = ((), (), s32[]{:S(2)}) async-start(), calls=%async_computation.14 | async-start | bytes 24576 | tf_op jit(solution)/shard_map/reduce_scatter | solution.py:208
  269.4 5.3 copy-start.27
  269.4 5.3 copy-start.47
  269.4 5.3 copy-start.53
  279.9 157.5 %reduce-scatter.15.cloned.1.call-start = ((), (), s32[]{:S(2)}) async-start(), calls=%async_computation.13 | async-start | bytes 49152 | tf_op jit(solution)/shard_map/reduce_scatter | solution.py:206
  280.6 301.3 %all-reduce.34.cloned.1.call-start = ((), (), s32[]{:S(2)}) async-start(), calls=%async_computation.15 | async-start | bytes 12582912 | tf_op jit(solution)/shard_map/psum | solution.py:210
  412.3 88.6 %copy-start.41 = (f32[1024]{0:T(1024)S(1)}, f32[1024]{0:T(1024)}, u32[]{:S(2)}) copy-start(f32[1024]{0:T(1024)} %param.42) | copy-start | bytes 12292
  412.3 88.6 %copy-start.44 = (f32[1024]{0:T(1024)S(1)}, f32[1024]{0:T(1024)}, u32[]{:S(2)}) copy-start(f32[1024]{0:T(1024)} %param.43) | copy-start | bytes 12292
  412.3 88.6 %copy-start.45 = (f32[1024]{0:T(1024)S(1)}, f32[1024]{0:T(1024)}, u32[]{:S(2)}) copy-start(f32[1024]{0:T(1024)} %param.44) | copy-start | bytes 12292
  412.3 89.2 %copy-start.37 = (f32[7,512]{1,0:T(8,128)S(1)}, f32[7,512]{1,0:T(8,128)}, u32[]{:S(2)}) copy-start(f32[7,512]{1,0:T(8,128)} %param.45) | copy-start | bytes 43012
  412.3 89.2 %copy-start.42 = (f32[7,256]{1,0:T(8,128)S(1)}, f32[7,256]{1,0:T(8,128)}, u32[]{:S(2)}) copy-start(f32[7,256]{1,0:T(8,128)} %param.46) | copy-start | bytes 21508
  412.3 89.2 %copy-start.43 = (f32[7,256]{1,0:T(8,128)S(1)}, f32[7,256]{1,0:T(8,128)}, u32[]{:S(2)}) copy-start(f32[7,256]{1,0:T(8,128)} %param.47) | copy-start | bytes 21508
  412.3 89.8 %copy-start.33 = (f32[9,256]{1,0:T(8,128)S(1)}, f32[9,256]{1,0:T(8,128)}, u32[]{:S(2)}) copy-start(f32[9,256]{1,0:T(8,128)} %param.39) | copy-start | bytes 27652
  412.3 89.8 %copy-start.38 = (f32[9,256]{1,0:T(8,128)S(1)}, f32[9,256]{1,0:T(8,128)}, u32[]{:S(2)}) copy-start(f32[9,256]{1,0:T(8,128)} %param.40) | copy-start | bytes 27652
  412.3 89.8 %copy-start.39 = (f32[9,256]{1,0:T(8,128)S(1)}, f32[9,256]{1,0:T(8,128)}, u32[]{:S(2)}) copy-start(f32[9,256]{1,0:T(8,128)} %param.41) | copy-start | bytes 27652
  412.3 169.6 %copy-start.13 = (f32[512,768]{1,0:T(8,128)S(1)}, f32[512,768]{1,0:T(8,128)}, u32[]{:S(2)}) copy-start(f32[512,768]{1,0:T(8,128)} %param.27) | copy-start | bytes 4718596
  412.4 169.6 %copy-start.28 = (f32[512,768]{1,0:T(8,128)S(1)}, f32[512,768]{1,0:T(8,128)}, u32[]{:S(2)}) copy-start(f32[512,768]{1,0:T(8,128)} %param.28) | copy-start | bytes 4718596
  582.0 5.4 copy-start.23
  582.0 5.4 copy-start.29
  582.0 5.4 copy-start.30
  582.0 5.4 copy-start.31
  582.0 6.9 %copy-start.16 = (f32[512,1024]{1,0:T(8,128)S(1)}, f32[512,1024]{1,0:T(8,128)}, u32[]{:S(2)}) copy-start(f32[512,1024]{1,0:T(8,128)} %param.34) | copy-start | bytes 6291460
  582.0 6.9 %copy-start.17 = (f32[512,1024]{1,0:T(8,128)S(1)}, f32[512,1024]{1,0:T(8,128)}, u32[]{:S(2)}) copy-start(f32[512,1024]{1,0:T(8,128)} %param.35) | copy-start | bytes 6291460
  582.0 6.9 %copy-start.21 = (f32[512,1024]{1,0:T(8,128)S(1)}, f32[512,1024]{1,0:T(8,128)}, u32[]{:S(2)}) copy-start(f32[512,1024]{1,0:T(8,128)} %get-tuple-element.51) | copy-start | bytes 6291460
  589.8 4.5 copy-start.11
  589.8 4.5 copy-start.18
  589.8 5.3 copy-start.19
  589.8 6.0 copy-start.20
  (20 other events, 47.5 us)
Sparse Core Ops, SparseCore 0:
  10.2 35.4 all-gather.3
  47.8 33.2 all-gather.5
  83.2 33.1 all-gather.7
  223.9 20.4 reduce-scatter.8
  255.5 43.5 reduce-scatter.6
  301.2 54.3 reduce-scatter.10
  357.9 54.3 reduce-scatter.12
  415.0 9.7 reduce-scatter.16
  427.6 9.8 reduce-scatter.14
  441.2 140.6 all-reduce.33
where the time goes:
time: 612 us; the launch traced here: 607 us
  waiting for transfers between devices  234 us (38%)
  local copies, waits for them, and re-layouts  93.9 us (15%)
  matrix products  93.7 us (15%)
  blocking collectives  92.8 us (15%)
  other arithmetic  75.7 us (12%)
  between operations  15.7 us (3%)
    psum x1, waiting for transfers between devices, local(): lax.psum((owned[0], owned[1], owned[2], owned[3], owned[4], owned[5], own...  79.2 us
    psum x1, blocking collectives, local(): lax.psum((owned[0], owned[1], owned[2], owned[3], owned[4], owned[5], own...  63.4 us
    reduce_scatter x1, waiting for transfers between devices, local(): lax.psum_scatter(grad_w_down, 'tensor', scatter_dimension=0, tiled=True)  56.7 us
    reduce_scatter x1, waiting for transfers between devices, local(): lax.psum_scatter(grad_w_up, 'tensor', scatter_dimension=1, tiled=True)  56.5 us
    convert_element_type x11, other arithmetic, narrow(): return values.astype(jnp.bfloat16)  42.1 us
    dot_general x8, matrix products, product(): return jnp.dot(left_side, right_side, preferred_element_type=jnp.float32)  37.4 us
    dot_general x4, matrix products, grad_product(): lax.dot_general(left_side, right_side, (((0,), (0,)), ((), ())), preferre...  21 us
    reduce_scatter x1, waiting for transfers between devices, local(): lax.psum_scatter(grad_w_in, 'tensor', scatter_dimension=1, tiled=True)  18.3 us
  transfers between devices with their start and end apart: 10, of which 8 were waited for; matrix products, arithmetic and copies ran while one was open for 24% of the time, Pallas kernels for 0%

commit v1 on v0

v1 whole, which is shorter than its diff:
```python
import functools
import jax
import jax.numpy as jnp
from jax import lax
from jax.experimental import pallas as pl
from jax.experimental.pallas import tpu as pltpu
from jax.sharding import PartitionSpec as P

D = 512
HD = 32
FF = 2048
SIDE = 14
WIDE = 16
WIN = SIDE * SIDE
ROWS = SIDE * WIDE
KEYS = 256
GROUPS = D // 128
STEP = 5
DOWN, UP, OUT, IN, GROWS = 0, 2048, 4096, 4608, 6144
MESH = pl.DeviceIdType.MESH
eps = 1e-05
f32 = jnp.float32
bf16 = jnp.bfloat16
C0 = 0.7978845608028654
C1 = 0.044715


def nn(a, b):
    return lax.dot_general(a, b, (((1,), (0,)), ((), ())), preferred_element_type=f32)


def nt(a, b):
    return lax.dot_general(a, b, (((1,), (1,)), ((), ())), preferred_element_type=f32)


def tn(a, b):
    return lax.dot_general(a, b, (((0,), (0,)), ((), ())), preferred_element_type=f32)


def normed(x):
    c = x - jnp.mean(x, axis=-1, keepdims=True)
    r = lax.rsqrt(jnp.mean(c * c, axis=-1, keepdims=True) + eps)
    return c * r, r


def norm_back(u, xhat, r):
    return r * (
        u
        - jnp.mean(u, axis=-1, keepdims=True)
        - xhat * jnp.mean(u * xhat, axis=-1, keepdims=True)
    )


def gelu_pair(x):
    x2 = x * x
    t = jnp.tanh(x * (C0 + (C0 * C1) * x2))
    h = 0.5 + 0.5 * t
    slope = h + (0.5 * x) * ((1.0 - t * t) * (C0 + (3.0 * C0 * C1) * x2))
    return x * h, slope


def gelu(x):
    return x * (0.5 + 0.5 * jnp.tanh(x * (C0 + (C0 * C1) * (x * x))))


def row_sum(x):
    return jnp.sum(x, axis=0, keepdims=True)


def shift_rows(x, by):
    z = jnp.zeros((abs(by), x.shape[1]), x.dtype)
    if by > 0:
        return jnp.concatenate([z, x[:-by]], axis=0)
    return jnp.concatenate([x[-by:], z], axis=0)


def roll1(x, by):
    return pltpu.roll(x, by % x.shape[0], 0)


def pool(c):
    s = c + roll1(c, 1) + roll1(c, -1)
    return s + shift_rows(s, WIDE) + shift_rows(s, -WIDE)


def block_kernel(images, lim, tok, cot, wi, wo, wu, wd, small, vecs,
           out, gin, grads, gsmall,
           x_s, co_s, gp_s, at_s, af_s, da_s, na_s, q_s, mx_s, nb_s, lb_s, la_s, dm_s,
           k_s, v_s, hd_s, dp_s, pj_s, p_s, mf_s, taps):
    limit = lim[0]
    v0, v1, v2, v3, v4, v5, v6 = (vecs[i : i + 1, :] for i in range(7))
    gsmall[...] = jnp.zeros_like(gsmall)
    for t in range(2):
        taps[:, t * 256 : (t + 1) * 256] = small[t]

    gin[...] = tok[...].astype(f32)
    pad = jnp.zeros((WIDE - SIDE, D), f32)
    for i in range(images * SIDE):
        x_s[i * WIDE : i * WIDE + SIDE, :] = gin[i * SIDE : (i + 1) * SIDE, :]
        x_s[i * WIDE + SIDE : (i + 1) * WIDE, :] = pad
    gin[...] = cot[...].astype(f32)
    for n in range(images):
        live = (n < limit).astype(f32)
        for i in range(n * SIDE, (n + 1) * SIDE):
            co_s[i * WIDE : i * WIDE + SIDE, :] = gin[i * SIDE : (i + 1) * SIDE, :] * live
            co_s[i * WIDE + SIDE : (i + 1) * WIDE, :] = pad

    cell = lax.broadcasted_iota(jnp.int32, (ROWS, 1), 0)
    inside = lax.rem(cell, WIDE) < SIDE
    lane = lax.broadcasted_iota(jnp.int32, (1, 128), 1)
    head_masks = [(lane // HD) == h for h in range(4)]
    key_row = lax.broadcasted_iota(jnp.int32, (KEYS, 128), 0)
    key_lane = lax.broadcasted_iota(jnp.int32, (KEYS, 128), 1)
    key_pad = (lax.rem(key_row, WIDE) >= SIDE) | (key_row >= ROWS)
    key_block = jnp.where(key_pad & (key_lane == 0), -1e30, 0.0).astype(bf16)
    one_block = jnp.where(
        lax.broadcasted_iota(jnp.int32, (ROWS, 128), 1) == 0, 1.0, 0.0
    ).astype(bf16)

    def forward(n, carry):
        rows = pl.ds(pl.multiple_of(n * ROWS, WIDE), ROWS)
        krows = pl.ds(pl.multiple_of(n * KEYS, WIDE), ROWS)
        kall = pl.ds(pl.multiple_of(n * KEYS, WIDE), KEYS)
        kend = pl.ds(pl.multiple_of(n * KEYS + ROWS, WIDE), KEYS - ROWS)
        x = x_s[rows, :]
        xhat, _ = normed(x)
        na = (xhat * v0 + v1).astype(bf16)
        na_s[rows, :] = na
        for t in range(2):
            ts = slice(t * 256, (t + 1) * 256)
            k_s[krows, ts] = nn(na, wi[t, 1]).astype(bf16)
            v_s[krows, ts] = nn(na, wi[t, 2]).astype(bf16)
        k_s[kend, :] = jnp.zeros((KEYS - ROWS, D), bf16)
        v_s[kend, :] = jnp.zeros((KEYS - ROWS, D), bf16)
        for g in range(GROUPS):
            ls = slice(g * 128, (g + 1) * 128)
            gp = nn(na, wi[g // 2, 0, :, (g % 2) * 128 : (g % 2 + 1) * 128])
            gp_s[rows, ls] = gp
            field = jnp.where(inside, gelu(gp), 0.0)
            back, ahead = roll1(field, 1), roll1(field, -1)
            conv = None
            for a in range(3):
                part = (
                    taps[3 * a : 3 * a + 1, ls] * back
                    + taps[3 * a + 1 : 3 * a + 2, ls] * field
                    + taps[3 * a + 2 : 3 * a + 3, ls] * ahead
                )
                if a != 1:
                    part = shift_rows(part, WIDE * (1 - a))
                conv = part if conv is None else conv + part
            pooled = pool(jnp.where(inside, conv, 0.0)) * (HD ** (-0.5) / 9.0)
            qg = pooled.astype(bf16)
            q_s[rows, ls] = qg
            qa = jnp.concatenate([qg, one_block], axis=1)
            kg = k_s[kall, ls]
            vg = v_s[kall, ls]
            acc = None
            for h in range(4):
                kh = jnp.concatenate(
                    [jnp.where(head_masks[h], kg, jnp.zeros_like(kg)), key_block], axis=1
                )
                s = nt(qa, kh)
                e = jnp.exp(s - jnp.max(s, axis=-1, keepdims=True))
                p = (e * (1.0 / jnp.sum(e, axis=-1, keepdims=True))).astype(bf16)
                p_s[n * 16 + (g * 4 + h)] = p
                o = nn(p, jnp.where(head_masks[h], vg, jnp.zeros_like(vg)))
                acc = o if acc is None else acc + o
            mx_s[rows, ls] = acc.astype(bf16)
            mf_s[rows, ls] = acc
        attn = nn(mx_s[rows, :], wo[...])
        at_s[rows, :] = attn
        after = x + v4 * attn
        af_s[rows, :] = after
        xhat_b, _ = normed(after)
        nb_s[rows, :] = (xhat_b * v2 + v3).astype(bf16)
        return carry

    lax.fori_loop(0, images, forward, 0)

    def feed(n, carry):
        rows = pl.ds(pl.multiple_of(n * ROWS, WIDE), ROWS)
        co = co_s[rows, :]
        d_br = v5 * co
        lb = d_br.astype(bf16)
        lb_s[rows, :] = lb
        nb = nb_s[rows, :]
        branch = None
        for c in range(4):
            cs = slice(c * 512, (c + 1) * 512)
            us = slice((c % 2) * 512, (c % 2 + 1) * 512)
            unit_bias = jnp.concatenate(
                [small[c // 2, 9 + (c % 2) * 2 + j : 10 + (c % 2) * 2 + j, :] for j in range(2)],
                axis=1,
            )
            pre = nn(nb, wu[c // 2, :, us]) + unit_bias
            value, slope = gelu_pair(pre)
            hid = value.astype(bf16)
            hd_s[rows, cs] = hid
            br = nn(hid, wd[cs, :])
            d_hid = nt(lb, wd[cs, :])
            dp = (slope * d_hid).astype(bf16)
            dp_s[rows, cs] = dp
            dn = nt(dp, wu[c // 2, :, us])
            gsmall[16 + c : 17 + c, :] += row_sum(dp.astype(f32))
            branch = br if branch is None else branch + br
            d_nb = dn if c == 0 else d_nb + dn
        after = af_s[rows, :]
        xhat, r = normed(after)
        moved = branch + v6
        live = (n < limit).astype(f32)
        af_s[rows, :] = (after + v5 * moved) * live
        gsmall[14:15, :] += row_sum(co * moved)
        gsmall[15:16, :] += row_sum(d_br)
        gsmall[11:12, :] += row_sum(d_nb * xhat)
        gsmall[12:13, :] += row_sum(d_nb)
        d_after = co + norm_back(v2 * d_nb, xhat, r)
        da_s[rows, :] = d_after
        gsmall[13:14, :] += row_sum(d_after * at_s[rows, :])
        la = (v4 * d_after).astype(bf16)
        la_s[rows, :] = la
        dm_s[rows, :] = nt(la, wo[...]).astype(bf16)
        return carry

    lax.fori_loop(0, images, feed, 0)

    for i in range(images * SIDE):
        gin[i * SIDE : (i + 1) * SIDE, :] = af_s[i * WIDE : i * WIDE + SIDE, :]
    out[...] = gin[...].astype(bf16)

    for c in range(FF // 512):
        cs = slice(c * 512, (c + 1) * 512)
        up = tn(nb_s[...], dp_s[:, cs]).astype(bf16)
        down = tn(hd_s[:, cs], lb_s[...]).astype(bf16)
        for j in range(2):
            js = slice(j * 256, (j + 1) * 256)
            first = UP + ((c % 2) * 2 + j) * 512
            grads[c // 2, first : first + 512, :] = up[:, js]
            first = DOWN + j * 1024 + (c % 2) * 512
            grads[c // 2, first : first + 512, :] = down[:, js]
    g_out = tn(mx_s[...], la_s[...]).astype(bf16)
    for t in range(2):
        for j in range(2):
            first = OUT + j * 256
            grads[t, first : first + 256, :] = g_out[t * 256 : (t + 1) * 256, j * 256 : (j + 1) * 256]

    pick_row = lax.broadcasted_iota(jnp.int32, (256, 128), 0)
    pick_lane = lax.broadcasted_iota(jnp.int32, (256, 128), 1)
    pick = jnp.where(
        (lax.rem(pick_row, 128) // HD == lax.rem(pick_lane, 4)) & (pick_lane < 8), 1.0, 0.0
    ).astype(bf16)

    def split(a):
        high = a.astype(bf16)
        return high, (a - high.astype(f32)).astype(bf16)

    def inner_block(a):
        sums = nn(jnp.concatenate(split(a), axis=1), pick)
        high, low = split(sums)
        return jnp.where(lane < 4, high, low)

    def backward(n, carry):
        rows = pl.ds(pl.multiple_of(n * ROWS, WIDE), ROWS)
        kall = pl.ds(pl.multiple_of(n * KEYS, WIDE), KEYS)
        for g in range(GROUPS):
            ls = slice(g * 128, (g + 1) * 128)
            dmg = dm_s[rows, ls]
            qg = q_s[rows, ls]
            kg = k_s[kall, ls]
            vg = v_s[kall, ls]
            dmf = dmg.astype(f32)
            left = jnp.concatenate([dmg, inner_block(dmf * mf_s[rows, ls])], axis=1)
            dmt = jnp.transpose(dmf).astype(bf16)
            qt = jnp.transpose(qg.astype(f32)).astype(bf16)
            dq = None
            dks, dvs = [], []
            for h in range(4):
                minus = jnp.where((lane == h) | (lane == h + 4), -1.0, 0.0).astype(bf16)
                right = jnp.concatenate(
                    [
                        jnp.where(head_masks[h], vg, jnp.zeros_like(vg)),
                        jnp.broadcast_to(minus, (KEYS, 128)),
                    ],
                    axis=1,
                )
                p = p_s[n * 16 + (g * 4 + h)]
                ds = (p.astype(f32) * nt(left, right)).astype(bf16)
                hs = slice(h * HD, (h + 1) * HD)
                part = nn(ds, jnp.where(head_masks[h], kg, jnp.zeros_like(kg)))
                dq = part if dq is None else dq + part
                dvs.append(nn(dmt[hs, :], p))
                dks.append(nn(qt[hs, :], ds))
            dk = jnp.transpose(jnp.concatenate(dks, axis=0))[:ROWS]
            dv = jnp.transpose(jnp.concatenate(dvs, axis=0))[:ROWS]
            pj_s[rows, D + g * 128 : D + (g + 1) * 128] = dk.astype(bf16)
            pj_s[rows, 2 * D + g * 128 : 2 * D + (g + 1) * 128] = dv.astype(bf16)
            value, slope = gelu_pair(gp_s[rows, ls])
            field = jnp.where(inside, value, 0.0)
            d_conv = jnp.where(inside, pool(dq * (HD ** (-0.5) / 9.0)), 0.0)
            shifted = (roll1(field, 1), field, roll1(field, -1))
            d_cols = [None, None, None]
            for a in range(3):
                moved = d_conv if a == 1 else shift_rows(d_conv, WIDE * (a - 1))
                for b in range(3):
                    t = 3 * a + b
                    gsmall[t : t + 1, ls] += row_sum(moved * shifted[b])
                    term = taps[t : t + 1, ls] * moved
                    d_cols[b] = term if d_cols[b] is None else d_cols[b] + term
            d_field = roll1(d_cols[0], -1) + d_cols[1] + roll1(d_cols[2], 1)
            pj_s[rows, ls] = jnp.where(inside, slope * d_field, 0.0).astype(bf16)
        pj = pj_s[rows, :]
        d_na = None
        for part in range(3):
            for t in range(2):
                first = part * D + t * 256
                term = nt(pj[:, first : first + 256], wi[t, part])
                d_na = term if d_na is None else d_na + term
        xhat, r = normed(x_s[rows, :])
        gsmall[9:10, :] += row_sum(d_na * xhat)
        gsmall[10:11, :] += row_sum(d_na)
        co_s[rows, :] = da_s[rows, :] + norm_back(v0 * d_na, xhat, r)
        return carry

    lax.fori_loop(0, images, backward, 0)
    for i in range(images * SIDE):
        gin[i * SIDE : (i + 1) * SIDE, :] = co_s[i * WIDE : i * WIDE + SIDE, :]
    for part in range(3):
        g_in = tn(na_s[...], pj_s[:, part * D : (part + 1) * D]).astype(bf16)
        for t in range(2):
            first = IN + part * 512
            grads[t, first : first + 512, :] = g_in[:, t * 256 : (t + 1) * 256]


def block(lim, tok, cot, wi, wo, wu, wd, small, vecs):
    images = tok.shape[0] // WIN
    R = images * ROWS
    K = images * KEYS
    S = jax.ShapeDtypeStruct
    V = pltpu.VMEM
    return pl.pallas_call(
        functools.partial(block_kernel, images),
        out_shape=(
            S(tok.shape, bf16),
            S(tok.shape, f32),
            S((2, GROWS, 256), bf16),
            S((24, D), f32),
        ),
        in_specs=[pl.BlockSpec(memory_space=pltpu.SMEM)] + [pl.BlockSpec(memory_space=V)] * 8,
        out_specs=[pl.BlockSpec(memory_space=V)] * 4,
        scratch_shapes=[V((R, D), f32)] * 6
        + [V((R, D), bf16)] * 7
        + [V((K, D), bf16)] * 2
        + [V((R, FF), bf16)] * 2
        + [
            V((R, 3 * D), bf16),
            V((images * 16, ROWS, KEYS), bf16),
            V((R, D), f32),
            V((16, D), f32),
        ],
        compiler_params=pltpu.CompilerParams(vmem_limit_bytes=60 * 1024 * 1024),
    )(lim, tok, cot, wi, wo, wu, wd, small, vecs)


def tile_loop(rows, size, body):
    if rows <= size:
        body(0, rows)
        return

    def step(i, carry):
        body(pl.multiple_of(i * size, size), size)
        return carry

    lax.fori_loop(0, rows // size, step, 0)


def aligned(first, size):
    return pl.ds(pl.multiple_of(first, 16), size)


CHUNKS = ((DOWN, 2048), (UP, 2048), (OUT, 512), (IN, 1536))


def reduce_kernel(grads, gsmall, full, small_sum, *scratch):
    count = len(CHUNKS)
    r1s, s1s, rpxs, rqys, p1s, q1s, rpys, rqxs, p2s, q2s, zps, zqs = (
        scratch[i * count : (i + 1) * count] for i in range(12)
    )
    small_in, small_z, send, recv, ssend, srecv = scratch[12 * count :]
    dp, x = lax.axis_index("dp"), lax.axis_index("tensor")
    core = lax.rem(dp, 2)
    y = lax.rem(dp // 2, 2)
    z = dp // 4

    def at(zz, yy, cc, xx):
        return ((zz * 2 + yy) * 2 + cc, xx)

    core_mate = at(z, y, 1 - core, x)
    x_mate = at(z, y, core, 1 - x)
    y_mate = at(z, 1 - y, core, x)
    z_others = [lax.rem(z + k, 4) for k in range(1, 4)]
    z_mates = [at(o, y, core, x) for o in z_others]
    barrier = pltpu.get_barrier_semaphore()
    for mate in (core_mate, x_mate, y_mate, *z_mates):
        pl.semaphore_signal(barrier, inc=1, device_id=mate, device_id_type=MESH)
    pl.semaphore_wait(barrier, 6)

    def copy(src, dst, chunk, slot, mate):
        return pltpu.make_async_remote_copy(
            src_ref=src,
            dst_ref=dst,
            send_sem=send.at[chunk, slot],
            recv_sem=recv.at[chunk, slot],
            device_id=mate,
            device_id_type=MESH,
        )

    def small_copy(src, dst, slot, mate):
        return pltpu.make_async_remote_copy(
            src_ref=src,
            dst_ref=dst,
            send_sem=ssend.at[slot],
            recv_sem=srecv.at[slot],
            device_id=mate,
            device_id_type=MESH,
        )

    def add(target, one, two):
        target[...] = (one.astype(f32) + two.astype(f32)).astype(bf16)

    flights = {}

    def stage(c, s):
        base, R = CHUNKS[c]
        half, quarter, eighth, piece = R // 2, R // 4, R // 8, R // 32
        r1, s1, rpx, rqy, p1, q1, rpy, rqx, p2, q2, zp, zq = (
            group[c]
            for group in (r1s, s1s, rpxs, rqys, p1s, q1s, rpys, rqxs, p2s, q2s, zps, zqs)
        )
        for flight in flights.pop((c, s - 1), ()):
            flight.wait()
        go = []
        mine = base + core * half
        if s == 0:
            go = [copy(grads.at[:, aligned(base + (1 - core) * half, half), :], r1, c, 0, core_mate)]
        elif s == 1:

            def body(i, size):
                rows = pl.ds(i, size)
                own = aligned(mine + i, size)
                for t in range(2):
                    s1[t, rows, :] = (
                        grads[t, own, :].astype(f32) + r1[t, rows, :].astype(f32)
                    ).astype(bf16)

            tile_loop(half, 128, body)
            go = [
                copy(s1.at[1 - x, pl.ds(0, quarter), :], rpx, c, 1, x_mate),
                copy(s1.at[:, aligned(quarter + (1 - y) * eighth, eighth), :], rqy, c, 2, y_mate),
            ]
        elif s == 2:

            def body_p(i, size):
                rows = pl.ds(i, size)
                p1[rows, :] = (s1[x, rows, :].astype(f32) + rpx[rows, :].astype(f32)).astype(bf16)

            def body_q(i, size):
                rows = pl.ds(i, size)
                own = aligned(quarter + y * eighth + i, size)
                for t in range(2):
                    q1[t, rows, :] = (
                        s1[t, own, :].astype(f32) + rqy[t, rows, :].astype(f32)
                    ).astype(bf16)

            tile_loop(quarter, 128, body_p)
            tile_loop(eighth, 64, body_q)
            go = [
                copy(p1.at[aligned((1 - y) * eighth, eighth), :], rpy, c, 3, y_mate),
                copy(q1.at[1 - x], rqx, c, 4, x_mate),
            ]
        elif s == 3:

            def body(i, size):
                rows = pl.ds(i, size)
                own = aligned(y * eighth + i, size)
                p2[rows, :] = (p1[own, :].astype(f32) + rpy[rows, :].astype(f32)).astype(bf16)
                q2[rows, :] = (q1[x, rows, :].astype(f32) + rqx[rows, :].astype(f32)).astype(bf16)

            tile_loop(eighth, 64, body)
            for k in range(3):
                theirs = aligned(z_others[k] * piece, piece)
                go.append(copy(p2.at[theirs, :], zp.at[k], c, 5 + k, z_mates[k]))
                go.append(copy(q2.at[theirs, :], zq.at[k], c, 8 + k, z_mates[k]))
        elif s == 4:
            own = aligned(z * piece, piece)
            for j, (part, got) in enumerate(((p2, zp), (q2, zq))):
                total = part[own, :].astype(f32)
                for k in range(3):
                    total = total + got[k].astype(f32)
                place = aligned(mine + j * quarter + y * eighth + z * piece, piece)
                full[place, :] = total.astype(bf16)
                for k in range(3):
                    go.append(
                        copy(full.at[place, :], full.at[place, :], c, 11 + 3 * j + k, z_mates[k])
                    )
        elif s == 5:
            for j in range(2):
                place = aligned(mine + j * quarter + y * eighth, eighth)
                go.append(copy(full.at[place, :], full.at[place, :], c, 17 + j, y_mate))
        elif s == 6:
            place = aligned(mine, half)
            go = [copy(full.at[place, :], full.at[place, :], c, 19, core_mate)]
        for flight in go:
            flight.start()
        if go:
            flights[(c, s)] = go

    def small_stage(s):
        if s == 0:
            small_z[0] = gsmall[...]
        elif s <= 3:
            flights.pop(("s", s - 1))[0].wait()
            small_z[s] = small_z[s - 1] + small_in[s - 1]
        else:
            for flight in flights.pop(("s", 3)):
                flight.wait()
            total = None
            for k in range(4):
                part = small_z[4 + k]
                total = part if total is None else total + part
            small_sum[...] = total
            return
        if s < 3:
            mate = (core_mate, x_mate, y_mate)[s]
            go = [small_copy(small_z.at[s], small_in.at[s], s, mate)]
        else:
            small_z[4 + z] = small_z[3]
            go = [
                small_copy(small_z.at[3], small_z.at[4 + z], 3 + k, z_mates[k]) for k in range(3)
            ]
        for flight in go:
            flight.start()
        flights[("s", s)] = go

    for step in range(8 + count - 1):
        for c in range(count):
            if 0 <= step - c <= 7:
                stage(c, step - c)
        if 0 <= step <= 4:
            small_stage(step)


def reduce_gradients(grads, gsmall):
    S = jax.ShapeDtypeStruct
    V = pltpu.VMEM
    shapes = [
        lambda R: (2, R // 2, 256),
        lambda R: (2, R // 2, 256),
        lambda R: (R // 4, 256),
        lambda R: (2, R // 8, 256),
        lambda R: (R // 4, 256),
        lambda R: (2, R // 8, 256),
        lambda R: (R // 8, 256),
        lambda R: (R // 8, 256),
        lambda R: (R // 8, 256),
        lambda R: (R // 8, 256),
        lambda R: (3, R // 32, 256),
        lambda R: (3, R // 32, 256),
    ]
    count = len(CHUNKS)
    return pl.pallas_call(
        reduce_kernel,
        out_shape=(S((GROWS, 256), bf16), S((24, D), f32)),
        in_specs=[pl.BlockSpec(memory_space=V)] * 2,
        out_specs=[pl.BlockSpec(memory_space=V)] * 2,
        scratch_shapes=[V(shape(R), bf16) for shape in shapes for _, R in CHUNKS]
        + [
            V((3, 24, D), f32),
            V((8, 24, D), f32),
            pltpu.SemaphoreType.DMA((count, 20)),
            pltpu.SemaphoreType.DMA((count, 20)),
            pltpu.SemaphoreType.DMA((6,)),
            pltpu.SemaphoreType.DMA((6,)),
        ],
        compiler_params=pltpu.CompilerParams(
            collective_id=1, has_side_effects=True, vmem_limit_bytes=48 * 1024 * 1024
        ),
    )(grads, gsmall)


def spread(part, transposed):
    shape = (768, 256) if transposed else (256, 768)
    narrow_side, wide_side = (1, 0) if transposed else (0, 1)
    a = lax.broadcasted_iota(jnp.int32, shape, narrow_side)
    b = lax.broadcasted_iota(jnp.int32, shape, wide_side)
    return jnp.where(b == (a // HD) * (3 * HD) + part * HD + lax.rem(a, HD), 1.0, 0.0).astype(bf16)


def adam(w, m, v, g, rate, decay):
    m = 0.5 * m + 0.5 * g
    v = 0.5 * v + 0.5 * g * g
    scale = 1.0 / (1.0 - 0.5**STEP)
    w = w - rate * ((m * scale) / (jnp.sqrt(v * scale) + 1e-08) + decay * w)
    return w, m, v


MATRICES = (
    (1024, 512, FF**-0.5, 4),
    (512, 1024, D**-0.5, 4),
    (256, 512, (D // HD) ** -0.5, 1),
    (512, 768, D**-0.5, 2),
)


def adam_kernel(*refs):
    full, small_sum = refs[:2]
    mats = refs[2:14]
    smalls = refs[14:23]
    outs = refs[23:39]
    small_outs = refs[39:48]
    bufs = refs[48:60]
    lows = refs[60:64]
    in_sem, out_sem = refs[64:]
    loads = {}
    for i, (rows, cols, rate, pieces) in enumerate(MATRICES):
        size = rows // pieces
        for p in range(pieces):
            rs = pl.ds(p * size, size)
            for j in range(3):
                go = pltpu.make_async_copy(
                    mats[3 * i + j].at[rs, :], bufs[3 * i + j].at[rs, :], in_sem.at[i, p, j]
                )
                go.start()
                loads[i, p, j] = go
    stores = []
    for i, (rows, cols, rate, pieces) in enumerate(MATRICES):
        size = rows // pieces
        bw, bm, bv = bufs[3 * i : 3 * i + 3]
        low = lows[i]
        for p in range(pieces):
            for j in range(3):
                loads[i, p, j].wait()

            def body(first, tile, i=i, p=p, bw=bw, bm=bm, bv=bv, low=low, rate=rate, size=size):
                rs = pl.ds(p * size + first, tile)
                if i == 0:
                    g = [full[pl.ds(DOWN + j * 1024 + p * size + first, tile), :] for j in range(2)]
                elif i == 1:
                    g = [full[pl.ds(UP + j * 512 + p * size + first, tile), :] for j in range(4)]
                elif i == 2:
                    g = [full[pl.ds(OUT + j * 256 + p * size + first, tile), :] for j in range(2)]
                else:
                    g = None
                    for part in range(3):
                        own = full[pl.ds(IN + part * 512 + p * size + first, tile), :]
                        term = nn(own, spread(part, False))
                        g = term if g is None else g + term
                if i < 3:
                    g = jnp.concatenate(g, axis=1).astype(f32)
                w, m, v = adam(bw[rs, :], bm[rs, :], bv[rs, :], g, rate, 0.05)
                bw[rs, :] = w
                bm[rs, :] = m
                bv[rs, :] = v
                low[rs, :] = w.astype(bf16)

            tile_loop(size, 32, body)
            rs = pl.ds(p * size, size)
            for j, src in enumerate((bw, bm, bv, low)):
                go = pltpu.make_async_copy(
                    src.at[rs, :], outs[4 * i + j].at[rs, :], out_sem.at[i, p, j]
                )
                go.start()
                stores.append(go)
    x = lax.axis_index("tensor")
    mine = pl.ds(pl.multiple_of(x * 256, 256), 256)
    g_small = small_sum[:, mine]
    both = small_sum[16:20, :]
    first = jnp.where(x == 0, 1.0, 0.0)
    g_bias = jnp.concatenate(
        [
            (both[j : j + 1, :] * first + both[2 + j : 3 + j, :] * (1.0 - first))
            for j in range(2)
        ],
        axis=1,
    )
    for i, (g, rate, decay) in enumerate(
        ((g_small[0:9], 2.0, 0.05), (g_bias, 0.3, 0.0), (g_small[9:16], 0.3, 0.0))
    ):
        w = smalls[3 * i][...] if i < 2 else smalls[6][:, mine]
        new = adam(w, smalls[3 * i + 1][...], smalls[3 * i + 2][...], g, rate, decay)
        for j in range(3):
            small_outs[3 * i + j][...] = new[j]
    for go in stores:
        go.wait()


def adam_step(full, small_sum, mats, smalls):
    S = jax.ShapeDtypeStruct
    V = pltpu.VMEM
    mat_shapes = [(rows, cols) for rows, cols, _, _ in MATRICES]
    any_spec = pl.BlockSpec(memory_space=pl.ANY)
    vmem_spec = pl.BlockSpec(memory_space=V)
    small_shapes = [(9, 256)] * 3 + [(1, 1024)] * 3 + [(7, 256)] * 3
    return pl.pallas_call(
        adam_kernel,
        out_shape=tuple(
            S(shape, kind) for shape in mat_shapes for kind in (f32, f32, f32, bf16)
        )
        + tuple(S(shape, f32) for shape in small_shapes),
        in_specs=[vmem_spec] * 2 + [any_spec] * 12 + [vmem_spec] * 9,
        out_specs=[any_spec] * 16 + [vmem_spec] * 9,
        scratch_shapes=[V(shape, f32) for shape in mat_shapes for _ in range(3)]
        + [V(shape, bf16) for shape in mat_shapes]
        + [pltpu.SemaphoreType.DMA((4, 4, 3)), pltpu.SemaphoreType.DMA((4, 4, 4))],
        compiler_params=pltpu.CompilerParams(vmem_limit_bytes=48 * 1024 * 1024),
    )(full, small_sum, *mats, *smalls)


def gather_kernel(w_in, w_out, w_up, w_down, own_small, wi, wo, wu, wd, small, send, recv):
    dp, x = lax.axis_index("dp"), lax.axis_index("tensor")
    core = lax.rem(dp, 2)
    y = lax.rem(dp // 2, 2)
    z = dp // 4

    def at(yy, cc, xx):
        return ((z * 2 + yy) * 2 + cc, xx)

    core_mate, x_mate, y_mate = at(y, 1 - core, x), at(y, core, 1 - x), at(1 - y, core, x)
    barrier = pltpu.get_barrier_semaphore()
    for mate in (core_mate, x_mate, y_mate):
        pl.semaphore_signal(barrier, inc=1, device_id=mate, device_id_type=MESH)
    pl.semaphore_wait(barrier, 3)

    def copy(src, dst, item, slot, mate):
        go = pltpu.make_async_remote_copy(
            src_ref=src,
            dst_ref=dst,
            send_sem=send.at[item, slot],
            recv_sem=recv.at[item, slot],
            device_id=mate,
            device_id_type=MESH,
        )
        go.start()
        return go

    small[x] = own_small[...]
    extra = copy(small.at[x], small.at[x], 4, 0, x_mate)

    def view(item, half, yy, cc):
        quarter = yy * 2 + cc
        if item == 0:
            return wi.at[half, :, aligned(quarter * 128, 128), :]
        ref, size = ((wo, 64), (wu, 128), (wd, 256))[item - 1]
        return ref.at[half, aligned(quarter * size, size), :]

    crossing = []
    for item in range(4):
        if item == 0:
            spreads = [spread(part, True) for part in range(3)]

            def body(first, tile):
                rows = pl.ds(first, tile)
                low = w_in[rows, :].astype(bf16)
                for part in range(3):
                    wi[x, part, rows, :] = nn(low, spreads[part]).astype(bf16)

            tile_loop(512, 128, body)
        else:
            src, dst = ((w_out, wo), (w_up, wu), (w_down, wd))[item - 1]

            def body(first, tile, src=src, dst=dst):
                rows = pl.ds(first, tile)
                dst[x, rows, :] = src[rows, :].astype(bf16)

            tile_loop(src.shape[0], 64, body)
        mine = view(item, x, y, core)
        crossing.append(copy(mine, mine, item, 0, x_mate))

    flying = [extra]
    aside = {}
    for item in range(5):
        if item < 4:
            crossing[item].wait()
            got = view(item, 1 - x, y, core)
            flying.append(copy(got, got, item, 1, core_mate))
            aside[item] = copy(got, got, item, 2, y_mate)
        if item > 0:
            aside[item - 1].wait()
            got = view(item - 1, 1 - x, 1 - y, core)
            flying.append(copy(got, got, item - 1, 3, core_mate))
    for go in flying:
        go.wait()


def gather_weights(w_in, w_out, w_up, w_down, own_small):
    S = jax.ShapeDtypeStruct
    spec = pl.BlockSpec(memory_space=pltpu.VMEM)
    return pl.pallas_call(
        gather_kernel,
        out_shape=(
            S((2, 3, D, 256), bf16),
            S((2, 256, D), bf16),
            S((2, D, 1024), bf16),
            S((2, 1024, D), bf16),
            S((2, 16, 256), f32),
        ),
        in_specs=[spec] * 5,
        out_specs=[spec] * 5,
        scratch_shapes=[pltpu.SemaphoreType.DMA((5, 4)), pltpu.SemaphoreType.DMA((5, 4))],
        compiler_params=pltpu.CompilerParams(
            collective_id=2, has_side_effects=True, vmem_limit_bytes=40 * 1024 * 1024
        ),
    )(w_in, w_out, w_up, w_down, own_small)


def local(
    tokens, cotangent, image_counts,
    w_in, m_in, v_in, w_out, m_out, v_out, w_up, m_up, v_up, w_down, m_down, v_down,
    kernel, m_kernel, v_kernel, up_bias, m_bias, v_bias, vectors, m_vectors, v_vectors,
):
    images = tokens.shape[0] // WIN
    live = image_counts[lax.axis_index("dp")] - lax.axis_index("tensor") * images
    own_small = jnp.concatenate(
        [kernel, up_bias.reshape(4, 256), jnp.zeros((3, 256), f32)], axis=0
    )
    wi, wo, wu, wd, small = gather_weights(w_in, w_out, w_up, w_down, own_small)
    out, grad_in, grads, g_small = block(
        live.reshape(1), tokens, cotangent, wi, wo.reshape(D, D), wu, wd.reshape(FF, D), small, vectors
    )
    full, small_sum = reduce_gradients(grads, g_small)
    new = adam_step(
        full,
        small_sum,
        (w_down, m_down, v_down, w_up, m_up, v_up, w_out, m_out, v_out, w_in, m_in, v_in),
        (kernel, m_kernel, v_kernel)
        + tuple(a.reshape(1, -1) for a in (up_bias, m_bias, v_bias))
        + (vectors, m_vectors, v_vectors),
    )
    down, up, mid, first = new[:4], new[4:8], new[8:12], new[12:16]
    bias = tuple(a.reshape(-1) for a in new[19:22])
    return (out, grad_in, *first, *mid, *up, *down, *new[16:19], *bias, *new[22:25])


def general(
    tokens, cotangent, image_counts,
    w_in, m_in, v_in, w_out, m_out, v_out, w_up, m_up, v_up, w_down, m_down, v_down,
    kernel, m_kernel, v_kernel, up_bias, m_bias, v_bias, vectors, m_vectors, v_vectors,
):
    images = tokens.shape[0] // WIN
    place = lax.axis_index("tensor")
    live = image_counts[lax.axis_index("dp")] - place * images

    def whole(a, axis):
        return lax.all_gather(a, "tensor", axis=axis, tiled=True)

    wi = whole(w_in.astype(bf16), 1).reshape(D, 2, 8, 3, HD).transpose(1, 3, 0, 2, 4)
    wi = wi.reshape(2, 3, D, 256)
    wo, wd = whole(w_out.astype(bf16), 0), whole(w_down.astype(bf16), 0)
    wu = whole(w_up.astype(bf16), 1).reshape(D, 2, 1024).transpose(1, 0, 2)
    small = jnp.concatenate(
        [
            whole(kernel, 1).reshape(9, 2, 256).transpose(1, 0, 2),
            whole(up_bias, 0).reshape(2, 4, 256),
            jnp.zeros((2, 3, 256), f32),
        ],
        axis=1,
    )
    out, grad_in, grads, gs = block(
        live.reshape(1), tokens, cotangent, wi, wo, wu, wd, small, vectors
    )
    grads = grads.astype(f32)

    def columns(first, rows, count):
        part = grads[:, first : first + rows * count].reshape(2, count, rows, 256)
        return part

    g_down = columns(DOWN, 1024, 2).transpose(0, 2, 1, 3).reshape(FF, D)
    g_up = columns(UP, 512, 4).transpose(2, 0, 1, 3).reshape(D, FF)
    g_out = columns(OUT, 256, 2).transpose(0, 2, 1, 3).reshape(D, D)
    g_in = columns(IN, 512, 3).reshape(2, 3, D, 8, HD).transpose(2, 0, 3, 1, 4).reshape(D, 3 * D)

    def owned(a, axis):
        return lax.psum(lax.psum_scatter(a, "tensor", scatter_dimension=axis, tiled=True), "dp")

    g_in, g_out, g_up, g_down = owned(g_in, 1), owned(g_out, 0), owned(g_up, 1), owned(g_down, 0)
    g_kernel, g_bias, g_vectors = owned(gs[0:9], 1), owned(gs[16:20].reshape(-1), 0), owned(gs[9:16], 1)
    vector_width = m_vectors.shape[1]
    own_vectors = lax.dynamic_slice_in_dim(vectors, place * vector_width, vector_width, 1)
    results = [out, grad_in]
    for w, m, v, g, rate in (
        (w_in, m_in, v_in, g_in, D**-0.5),
        (w_out, m_out, v_out, g_out, (D // HD) ** -0.5),
        (w_up, m_up, v_up, g_up, D**-0.5),
        (w_down, m_down, v_down, g_down, FF**-0.5),
    ):
        new = adam(w, m, v, g, rate, 0.05)
        results += [*new, new[0].astype(bf16)]
    results += adam(kernel, m_kernel, v_kernel, g_kernel, 2.0, 0.05)
    results += adam(up_bias, m_bias, v_bias, g_bias, 0.3, 0.0)
    results += adam(own_vectors, m_vectors, v_vectors, g_vectors, 0.3, 0.0)
    return tuple(results)


def solution(mesh):
    rows, columns = P("tensor", None), P(None, "tensor")
    tokens = P(("dp", "tensor"), None)
    mats = (columns,) * 3 + (rows,) * 3 + (columns,) * 3 + (rows,) * 3
    news = (columns,) * 4 + (rows,) * 4 + (columns,) * 4 + (rows,) * 4
    pairs = mesh.shape["dp"] == 16 and mesh.shape["tensor"] == 2
    return jax.shard_map(
        local if pairs else general,
        mesh=mesh,
        in_specs=(tokens, tokens, P(), *mats)
        + (columns,) * 3
        + (P("tensor"),) * 3
        + (P(), columns, columns),
        out_specs=(tokens, tokens, *news) + (columns,) * 3 + (P("tensor"),) * 3 + (columns,) * 3,
        check_vma=False,
    )
```

time: 612 us -> 218 us (0.36)
  waiting for transfers between devices: 234 us -> 0 us
  Pallas kernels: 0 us -> 200 us
  matrix products: 93.7 us -> 0 us
  blocking collectives: 92.8 us -> 0 us
  local copies, waits for them, and re-layouts: 93.9 us -> 15.3 us
  other arithmetic: 75.7 us -> 0.79 us
  between operations: 15.7 us -> 1.71 us
    pallas_call x0 -> x4, Pallas kernels: none -> 200 us  [the longest x1 74.9 us: block(): pl.pallas_call(functools.partial(block_kernel, images), out_shape=(S(tok....]
    reduce_scatter x6 -> x0, waiting for transfers between devices: 150 us -> none  [the longest x1 56.7 us: local(): lax.psum_scatter(grad_w_down, 'tensor', scatter_dimension=0, tiled=True)]
    dot_general x18 -> x0, matrix products: 93.7 us -> none  [the longest x8 37.4 us: product(): return jnp.dot(left_side, right_side, preferred_element_type=jnp.float32)]
    psum x1 -> x0, waiting for transfers between devices: 79.2 us -> none  [local(): lax.psum((owned[0], owned[1], owned[2], owned[3], owned[4], owned[5], own...]
    psum x1 -> x0, blocking collectives: 63.4 us -> none  [local(): lax.psum((owned[0], owned[1], owned[2], owned[3], owned[4], owned[5], own...]
    convert_element_type x12 -> x0, other arithmetic: 42.8 us -> none  [the longest x11 42.1 us: narrow(): return values.astype(jnp.bfloat16)]
    reshape x7 -> x1, local copies, waits for them, and re-layouts: 34 us -> 0.69 us  [local(): up_bias.reshape(4, 256)]
    all_gather x3 -> x0, blocking collectives: 24.4 us -> none  [the longest x1 14.7 us: local(): lax.all_gather(narrow(w_out), 'tensor', axis=0, tiled=True)]
  transfers between devices with their start and end apart: 10 -> 0, of which waited for: 8 -> 0; matrix products, arithmetic and copies ran while one was open for 24% -> 0% of each run, Pallas kernels for 0% -> 0%
where the time goes in v1:
time: 218 us
  Pallas kernels  200 us (92%)
  local copies, waits for them, and re-layouts  15.3 us (7%)
    pallas_call x1, Pallas kernels, block(): pl.pallas_call(functools.partial(block_kernel, images), out_shape=(S(tok....  74.9 us
    pallas_call x1, Pallas kernels, reduce_gradients(): pl.pallas_call(reduce_kernel, out_shape=(S((GROWS, 256), bf16), S((24, D)...  71.6 us
    pallas_call x1, Pallas kernels, gather_weights(): pl.pallas_call(gather_kernel, out_shape=(S((2, 3, D, 256), bf16), S((2, 2...  31.8 us
    pallas_call x1, Pallas kernels, adam_step(): pl.pallas_call(adam_kernel, out_shape=tuple((S(shape, kind) for shape in...  21.7 us
    unnamed x50, local copies, waits for them, and re-layouts  13.3 us

profile of v1, /device:TPU:0, one launch (start us, length us, event | category | flops | bytes accessed | tf_op | source)
XLA Modules:
  0.0 217.8 jit_solution(3983399744663149711)
XLA Ops:
  0.7 1.2 dynamic_slice.3
  2.6 0.1 pad.2.clone
  2.7 0.7 reshape.85
  3.3 0.8 maximum_maximum_fusion.own_small
  4.1 0.0 copy-start
  4.1 1.6 copy-done
  5.7 0.0 copy-start.1
  5.7 1.6 copy-done.1
  7.3 0.0 copy-start.2
  7.3 1.4 copy-done.2
  8.7 1.0 copy-done.5
  9.8 31.8 %shard_map.439 = (bf16[2,3,512,256]{3,2,1,0:T(8,128)(2,1)S(1)}, bf16[2,256,512]{2,1,0:T(8,128)(2,1)S(1)}, bf16[2,512,1024]{2,1,0:T(8,128)(2,1)S(1)}, bf16[2,1024,512]{2,1,0:T(8,128)(2,1)S(1)}, f32[2,16,256]{2,1,0:T(8,128)S(1)}) custom-call(f32[512,768]{1,0:T(8,128)S(1)} %copy-done.2, f32[256,512]{1,0:T(8,128)S(1)} %copy-done.5, f32[512,1024]{1,0:T(8,128)S(1)} %copy-done, ...), custom_call_target="tpu_custom_call" | custom-call | tf_op jit(solution)/shard_map/pallas_call | solution.py:796
  41.5 0.0 copy-start.7
  41.6 1.3 copy-done.7
  42.9 1.3 copy-done.8
  44.2 1.1 copy-done.10
  45.3 0.8 copy-done.13
  46.1 0.6 copy-done.17
  46.7 74.9 %shard_map.440 = (bf16[784,512]{1,0:T(8,128)(2,1)}, f32[784,512]{1,0:T(8,128)}, bf16[2,6144,256]{2,1,0:T(8,128)(2,1)}, f32[24,512]{1,0:T(8,128)}) custom-call(s32[1]{0:T(128)} %bitcast.1.lim, bf16[784,512]{1,0:T(8,128)(2,1)} %tok.1, bf16[784,512]{1,0:T(8,128)(2,1)} %cot.1, bf16[2,3,512,256]{3,2,1,0:T(8,128)(2,1)} %copy-done.10, bf16[512,512]{1,0:T(8,128)(2,1)} %bitcast.11, ...), custom_call_target="tpu_custom_call" | custom-call | tf_op jit(solution)/shard_map/pallas_call | solution.py:339
  121.7 0.8 copy-done.16
  122.5 0.0 copy-start.12
  122.5 0.0 copy-start.14
  122.5 0.0 copy-start.15
  122.5 0.0 copy-start.18
  122.5 0.0 copy-start.19
  122.5 0.0 copy-start.20
  122.6 0.0 copy-start.21
  122.6 0.0 copy-start.22
  122.6 0.0 copy-start.23
  122.6 0.0 copy-start.24
  122.6 71.6 %shard_map.441 = (bf16[6144,256]{1,0:T(8,128)(2,1)S(1)}, f32[24,512]{1,0:T(8,128)S(1)}) custom-call(bf16[2,6144,256]{2,1,0:T(8,128)(2,1)} %get-tuple-element.70.grads, f32[24,512]{1,0:T(8,128)S(1)} %copy-done.16), custom_call_target="tpu_custom_call" | custom-call | tf_op jit(solution)/shard_map/pallas_call | solution.py:569
  194.2 0.0 copy-start.4
  194.2 1.6 copy-done.4
  195.9 0.0 copy-done.3
  195.9 0.0 copy-done.6
  195.9 0.0 copy-done.9
  195.9 0.0 copy-done.11
  195.9 0.0 copy-done.12
  195.9 0.0 copy-done.14
  195.9 0.0 copy-done.15
  195.9 0.0 copy-done.18
  195.9 0.0 copy-done.19
  195.9 0.0 copy-done.20
  195.9 0.0 copy-done.21
  195.9 0.0 copy-done.22
  195.9 0.0 copy-done.23
  196.0 0.0 copy-done.24
  196.0 21.7 %shard_map.442 = (f32[1024,512]{1,0:T(8,128)}, f32[1024,512]{1,0:T(8,128)}, f32[1024,512]{1,0:T(8,128)}, bf16[1024,512]{1,0:T(8,128)(2,1)}, f32[512,1024]{1,0:T(...) custom-call(bf16[6144,256]{1,0:T(8,128)(2,1)} %copy-done.4, ...), custom_call_target="tpu_custom_call" | custom-call | tf_op jit(solution)/shard_map/pallas_call | solution.py:702
  (11 shorter events, 0.0 us)
Async XLA Ops:
  4.1 1.6 copy-start
  5.7 1.6 copy-start.1
  7.3 1.4 copy-start.2
  8.7 1.0 copy-start.5
  41.5 1.3 copy-start.7
  42.9 1.3 copy-start.8
  44.2 1.1 copy-start.10
  45.3 0.8 copy-start.13
  46.1 0.6 copy-start.17
  121.7 0.8 copy-start.16
  122.5 73.4 %copy-start.3 = (f32[512,768]{1,0:T(8,128)S(1)}, f32[512,768]{1,0:T(8,128)}, u32[]{:S(2)}) copy-start(f32[512,768]{1,0:T(8,128)} %refs_11_.1) | copy-start | bytes 4718596
  122.5 73.4 %copy-start.6 = (f32[256,512]{1,0:T(8,128)S(1)}, f32[256,512]{1,0:T(8,128)}, u32[]{:S(2)}) copy-start(f32[256,512]{1,0:T(8,128)} %refs_8_.1) | copy-start | bytes 1572868
  122.5 73.4 %copy-start.9 = (f32[512,768]{1,0:T(8,128)S(1)}, f32[512,768]{1,0:T(8,128)}, u32[]{:S(2)}) copy-start(f32[512,768]{1,0:T(8,128)} %refs_12_.1) | copy-start | bytes 4718596
  122.5 73.4 %copy-start.11 = (f32[256,512]{1,0:T(8,128)S(1)}, f32[256,512]{1,0:T(8,128)}, u32[]{:S(2)}) copy-start(f32[256,512]{1,0:T(8,128)} %refs_9_.1) | copy-start | bytes 1572868
  122.5 73.4 %copy-start.12 = (f32[256,512]{1,0:T(8,128)S(1)}, f32[256,512]{1,0:T(8,128)}, u32[]{:S(2)}) copy-start(f32[256,512]{1,0:T(8,128)} %refs_10_.1) | copy-start | bytes 1572868
  122.5 73.4 %copy-start.14 = (f32[7,512]{1,0:T(8,128)S(1)}, f32[7,512]{1,0:T(8,128)}, u32[]{:S(2)}) copy-start(f32[7,512]{1,0:T(8,128)} %refs_20_.1) | copy-start | bytes 43012
  122.5 73.4 %copy-start.15 = (f32[9,256]{1,0:T(8,128)S(1)}, f32[9,256]{1,0:T(8,128)}, u32[]{:S(2)}) copy-start(f32[9,256]{1,0:T(8,128)} %refs_14_.1) | copy-start | bytes 27652
  122.5 73.4 %copy-start.18 = (f32[9,256]{1,0:T(8,128)S(1)}, f32[9,256]{1,0:T(8,128)}, u32[]{:S(2)}) copy-start(f32[9,256]{1,0:T(8,128)} %refs_15_.1) | copy-start | bytes 27652
  122.5 73.4 %copy-start.19 = (f32[9,256]{1,0:T(8,128)S(1)}, f32[9,256]{1,0:T(8,128)}, u32[]{:S(2)}) copy-start(f32[9,256]{1,0:T(8,128)} %refs_16_.1) | copy-start | bytes 27652
  122.5 73.4 %copy-start.20 = (f32[1024]{0:T(1024)S(1)}, f32[1024]{0:T(1024)}, u32[]{:S(2)}) copy-start(f32[1024]{0:T(1024)} %param.42) | copy-start | bytes 12292
  122.6 73.4 %copy-start.21 = (f32[7,256]{1,0:T(8,128)S(1)}, f32[7,256]{1,0:T(8,128)}, u32[]{:S(2)}) copy-start(f32[7,256]{1,0:T(8,128)} %refs_21_.1) | copy-start | bytes 21508
  122.6 73.4 %copy-start.22 = (f32[7,256]{1,0:T(8,128)S(1)}, f32[7,256]{1,0:T(8,128)}, u32[]{:S(2)}) copy-start(f32[7,256]{1,0:T(8,128)} %refs_22_.1) | copy-start | bytes 21508
  122.6 73.4 %copy-start.23 = (f32[1024]{0:T(1024)S(1)}, f32[1024]{0:T(1024)}, u32[]{:S(2)}) copy-start(f32[1024]{0:T(1024)} %param.43) | copy-start | bytes 12292
  122.6 73.4 %copy-start.24 = (f32[1024]{0:T(1024)S(1)}, f32[1024]{0:T(1024)}, u32[]{:S(2)}) copy-start(f32[1024]{0:T(1024)} %param.44) | copy-start | bytes 12292
  194.2 1.6 copy-start.4

commit v2 on v1

v2 whole, which is shorter than its diff:
```python
import functools
import jax
import jax.numpy as jnp
from jax import lax
from jax.experimental import pallas as pl
from jax.experimental.pallas import tpu as pltpu
from jax.sharding import PartitionSpec as P

D = 512
HD = 32
FF = 2048
SIDE = 14
WIDE = 16
WIN = SIDE * SIDE
ROWS = SIDE * WIDE
KEYS = 256
GROUPS = D // 128
STEP = 5
DOWN, UP, OUT, IN, GROWS = 0, 2048, 4096, 4608, 6144
MESH = pl.DeviceIdType.MESH
eps = 1e-05
f32 = jnp.float32
bf16 = jnp.bfloat16
C0 = 0.7978845608028654
C1 = 0.044715


def nn(a, b):
    return lax.dot_general(a, b, (((1,), (0,)), ((), ())), preferred_element_type=f32)


def nt(a, b):
    return lax.dot_general(a, b, (((1,), (1,)), ((), ())), preferred_element_type=f32)


def tn(a, b):
    return lax.dot_general(a, b, (((0,), (0,)), ((), ())), preferred_element_type=f32)


def normed(x):
    c = x - jnp.mean(x, axis=-1, keepdims=True)
    r = lax.rsqrt(jnp.mean(c * c, axis=-1, keepdims=True) + eps)
    return c * r, r


def norm_back(u, xhat, r):
    return r * (
        u
        - jnp.mean(u, axis=-1, keepdims=True)
        - xhat * jnp.mean(u * xhat, axis=-1, keepdims=True)
    )


def gelu_pair(x):
    x2 = x * x
    t = 0.5 * jnp.tanh(x * (C0 + (C0 * C1) * x2))
    h = 0.5 + t
    value = x * h
    return value, h + value * ((0.5 - t) * (2.0 * C0 + (6.0 * C0 * C1) * x2))


def gelu(x):
    return x * (0.5 + 0.5 * jnp.tanh(x * (C0 + (C0 * C1) * (x * x))))


def row_sum(x):
    return jnp.sum(x, axis=0, keepdims=True)


def shift_rows(x, by):
    z = jnp.zeros((abs(by), x.shape[1]), x.dtype)
    if by > 0:
        return jnp.concatenate([z, x[:-by]], axis=0)
    return jnp.concatenate([x[-by:], z], axis=0)


def roll1(x, by):
    return pltpu.roll(x, by % x.shape[0], 0)


def pool(c):
    s = c + roll1(c, 1) + roll1(c, -1)
    return s + shift_rows(s, WIDE) + shift_rows(s, -WIDE)


def block_body(images, limit, first_half, hooks, wi, wo, wu, wd, small, vecs,
               gin, grads, gsmall,
               x_s, co_s, at_s, af_s, da_s, gp_s, mf_s, na_s, nb_s, lb_s, la_s, mx_s,
               q_s, k_s, v_s, dm_s, hd_s, dp_s, pj_s, p_s, taps_s, ds_s):
    gain_a, shift_a, gain_b, shift_b, scale_a, scale_f, bias_f = (
        vecs[i : i + 1, :] for i in range(7)
    )
    gsmall[...] = jnp.zeros_like(gsmall)
    dn_s = at_s
    gtaps = taps_s
    gtaps[...] = jnp.zeros_like(gtaps)
    blank = jnp.zeros((KEYS - ROWS, 256), bf16)
    for ref in (q_s, k_s, v_s, dm_s):
        for t in range(2):
            for n in range(images):
                ref[t, n * KEYS + ROWS : (n + 1) * KEYS, :] = blank

    cell = lax.broadcasted_iota(jnp.int32, (ROWS, 1), 0)
    inside = lax.rem(cell, WIDE) < SIDE
    lane = lax.broadcasted_iota(jnp.int32, (1, 128), 1)
    head_masks = [(lane // HD) == h for h in range(4)]
    key_row = lax.broadcasted_iota(jnp.int32, (KEYS, 128), 0)
    key_lane = lax.broadcasted_iota(jnp.int32, (KEYS, 128), 1)
    key_pad = (lax.rem(key_row, WIDE) >= SIDE) | (key_row >= ROWS)
    key_block = jnp.where(key_pad & (key_lane == 0), -1e30, 0.0).astype(bf16)
    one_block = jnp.where(key_lane == 0, 1.0, 0.0).astype(bf16)

    def padded(n):
        return pl.ds(pl.multiple_of(n * ROWS, WIDE), ROWS)

    def held(n):
        return pl.ds(pl.multiple_of(n * KEYS, WIDE), ROWS)

    def whole(n):
        return pl.ds(pl.multiple_of(n * KEYS, WIDE), KEYS)

    def masked(h, a):
        return jnp.where(head_masks[h], a, jnp.zeros_like(a))

    def prepare(n, carry):
        rows = padded(n)
        xhat, _ = normed(x_s[rows, :].astype(f32))
        na_s[rows, :] = (xhat * gain_a + shift_a).astype(bf16)
        return carry

    def tap(t, i, ls):
        return small[t, pl.ds(i, 1), ls]

    def attend(t, n):
        rows = padded(n)
        na = na_s[rows, :]
        k_s[t, held(n), :] = nn(na, wi[t, 1]).astype(bf16)
        v_s[t, held(n), :] = nn(na, wi[t, 2]).astype(bf16)
        for g in range(2):
            ls = slice(g * 128, (g + 1) * 128)
            gp = nn(na, wi[t, 0, :, ls])
            gp_s[t, rows, ls] = gp
            field = jnp.where(inside, gelu(gp), 0.0)
            back, ahead = roll1(field, 1), roll1(field, -1)
            conv = None
            for a in range(3):
                part = (
                    tap(t, 3 * a, ls) * back
                    + tap(t, 3 * a + 1, ls) * field
                    + tap(t, 3 * a + 2, ls) * ahead
                )
                if a != 1:
                    part = shift_rows(part, WIDE * (1 - a))
                conv = part if conv is None else conv + part
            pooled = pool(jnp.where(inside, conv, 0.0)) * (HD ** (-0.5) / 9.0)
            q_s[t, held(n), ls] = pooled.astype(bf16)
        for g in range(2):
            ls = slice(g * 128, (g + 1) * 128)
            qa = jnp.concatenate([q_s[t, whole(n), ls], one_block], axis=1)
            kg = k_s[t, whole(n), ls]
            vt = jnp.transpose(v_s[t, whole(n), ls])
            mixed = []
            keys = jnp.concatenate(
                [jnp.concatenate([masked(h, kg), key_block], axis=1) for h in range(4)], axis=0
            )
            scores = nt(keys, qa)
            for h in range(4):
                hs = slice(h * KEYS, (h + 1) * KEYS)
                s = scores[hs]
                e = jnp.exp(s - jnp.max(s, axis=0, keepdims=True))
                p_s[t, n * 2 + g, :, hs] = (e * (1.0 / jnp.sum(e, axis=0, keepdims=True))).astype(bf16)
            for h in range(4):
                p = p_s[t, n * 2 + g, :, h * KEYS : (h + 1) * KEYS]
                mixed.append(nn(vt[h * HD : (h + 1) * HD], p))
            mix = jnp.transpose(jnp.concatenate(mixed, axis=0))[:ROWS]
            mf_s[t, rows, ls] = mix
            mx_s[t, rows, ls] = mix.astype(bf16)

    def finish(n, carry):
        rows = padded(n)
        attn = nn(mx_s[0, rows, :], wo[0]) + nn(mx_s[1, rows, :], wo[1])
        at_s[rows, :] = attn
        after = x_s[rows, :].astype(f32) + scale_a * attn
        af_s[rows, :] = after
        xhat, _ = normed(after)
        nb_s[rows, :] = (xhat * gain_b + shift_b).astype(bf16)
        return carry

    def feed(n, carry):
        rows = padded(n)
        co = co_s[rows, :].astype(f32)
        d_branch = scale_f * co
        lb = d_branch.astype(bf16)
        lb_s[rows, :] = lb
        nb = nb_s[rows, :]
        branch = None
        for c in range(4):
            cs = slice(c * 512, (c + 1) * 512)
            us = slice((c % 2) * 512, (c % 2 + 1) * 512)
            unit_bias = jnp.concatenate(
                [small[c // 2, 9 + (c % 2) * 2 + j : 10 + (c % 2) * 2 + j, :] for j in range(2)],
                axis=1,
            )
            pre = nn(nb, wu[c // 2, :, us]) + unit_bias
            value, slope = gelu_pair(pre)
            hid = value.astype(bf16)
            hd_s[rows, cs] = hid
            br = nn(hid, wd[c // 2, us, :])
            d_pre = slope * nt(lb, wd[c // 2, us, :])
            gsmall[16 + c : 17 + c, :] += row_sum(d_pre)
            dp = d_pre.astype(bf16)
            dp_s[rows, cs] = dp
            dn = nt(dp, wu[c // 2, :, us])
            branch = br if branch is None else branch + br
            d_nb = dn if c == 0 else d_nb + dn
        after = af_s[rows, :]
        xhat, r = normed(after)
        moved = branch + bias_f
        live = (n < limit).astype(f32)
        af_s[rows, :] = (after + scale_f * moved) * live
        gsmall[14:15, :] += row_sum(co * moved)
        gsmall[15:16, :] += row_sum(d_branch)
        gsmall[11:12, :] += row_sum(d_nb * xhat)
        gsmall[12:13, :] += row_sum(d_nb)
        d_after = co + norm_back(gain_b * d_nb, xhat, r)
        da_s[rows, :] = d_after
        gsmall[13:14, :] += row_sum(d_after * at_s[rows, :])
        la = (scale_a * d_after).astype(bf16)
        la_s[rows, :] = la
        for t in range(2):
            dm_s[t, held(n), :] = nt(la, wo[t]).astype(bf16)
        return carry

    pick_row = lax.broadcasted_iota(jnp.int32, (256, 128), 0)
    pick_lane = lax.broadcasted_iota(jnp.int32, (256, 128), 1)
    pick = jnp.where(
        (lax.rem(pick_row, 128) // HD == lax.rem(pick_lane, 4)) & (pick_lane < 8), 1.0, 0.0
    ).astype(bf16)

    def split(a):
        high = a.astype(bf16)
        return high, (a - high.astype(f32)).astype(bf16)

    def inner_block(a):
        sums = nn(jnp.concatenate(split(a), axis=1), pick)
        high, low = split(sums)
        return jnp.where(lane < 4, high, low)

    blank_rows = jnp.zeros((KEYS - ROWS, 128), bf16)

    minus = [
        jnp.where((lane == h) | (lane == h + 4), -1.0, 0.0).astype(bf16) for h in range(4)
    ]

    def recede(t, n):
        rows = padded(n)
        for g in range(2):
            ls = slice(g * 128, (g + 1) * 128)
            inner = inner_block(dm_s[t, held(n), ls].astype(f32) * mf_s[t, rows, ls])
            dmg = dm_s[t, whole(n), ls]
            left = jnp.concatenate(
                [dmg, jnp.concatenate([inner, blank_rows], axis=0)], axis=1
            )
            qg = q_s[t, whole(n), ls]
            kg = k_s[t, whole(n), ls]
            vg = v_s[t, whole(n), ls]
            kt = jnp.transpose(kg)
            dqs = []
            right = jnp.concatenate(
                [
                    jnp.concatenate([masked(h, vg), jnp.broadcast_to(minus[h], (KEYS, 128))], axis=1)
                    for h in range(4)
                ],
                axis=0,
            )
            d_probs = nt(right, left)
            for h in range(4):
                hs = slice(h * KEYS, (h + 1) * KEYS)
                e = p_s[t, n * 2 + g, :, hs]
                ds_s[:, hs] = (e.astype(f32) * d_probs[hs]).astype(bf16)
            dv = nn(
                p_s[t, n * 2 + g], jnp.concatenate([masked(h, dmg) for h in range(4)], axis=0)
            )
            dk = nn(ds_s[...], jnp.concatenate([masked(h, qg) for h in range(4)], axis=0))
            for h in range(4):
                dqs.append(nn(kt[h * HD : (h + 1) * HD], ds_s[:, h * KEYS : (h + 1) * KEYS]))
            dq = jnp.transpose(jnp.concatenate(dqs, axis=0))[:ROWS]
            pj_s[t, 1, rows, ls] = dk[:ROWS].astype(bf16)
            pj_s[t, 2, rows, ls] = dv[:ROWS].astype(bf16)
            value, slope = gelu_pair(gp_s[t, rows, ls])
            field = jnp.where(inside, value, 0.0)
            d_conv = jnp.where(inside, pool(dq * (HD ** (-0.5) / 9.0)), 0.0)
            shifted = (roll1(field, 1), field, roll1(field, -1))
            d_cols = [None, None, None]
            for a in range(3):
                moved = d_conv if a == 1 else shift_rows(d_conv, WIDE * (a - 1))
                for b in range(3):
                    i = 3 * a + b
                    gtaps[t, i : i + 1, ls] += row_sum(moved * shifted[b])
                    term = tap(t, i, ls) * moved
                    d_cols[b] = term if d_cols[b] is None else d_cols[b] + term
            d_field = roll1(d_cols[0], -1) + d_cols[1] + roll1(d_cols[2], 1)
            pj_s[t, 0, rows, ls] = jnp.where(inside, slope * d_field, 0.0).astype(bf16)
        d_na = None
        for part in range(3):
            term = nt(pj_s[t, part, rows, :], wi[t, part])
            d_na = term if d_na is None else d_na + term
        return d_na

    def rise(n, carry):
        rows = padded(n)
        d_na = dn_s[rows, :]
        xhat, r = normed(x_s[rows, :].astype(f32))
        gsmall[9:10, :] += row_sum(d_na * xhat)
        gsmall[10:11, :] += row_sum(d_na)
        da_s[rows, :] += norm_back(gain_a * d_na, xhat, r)
        return carry

    def narrow_rows(target, source):
        for i in range(images * SIDE):
            target[i * SIDE : (i + 1) * SIDE, :] = source[i * WIDE : i * WIDE + SIDE, :]

    def store_down(u):
        for t in range(2):
            cs = slice((2 * t + u) * 512, (2 * t + u + 1) * 512)
            down = tn(hd_s[:, cs], lb_s[...]).astype(bf16)
            for j in range(2):
                first = DOWN + (2 * u + j) * 512
                grads[t, first : first + 512, :] = down[:, j * 256 : (j + 1) * 256]

    def store_up(u):
        for t in range(2):
            cs = slice((2 * t + u) * 512, (2 * t + u + 1) * 512)
            up = tn(nb_s[...], dp_s[:, cs]).astype(bf16)
            for j in range(2):
                first = UP + (2 * u + j) * 512
                grads[t, first : first + 512, :] = up[:, j * 256 : (j + 1) * 256]

    def store_out():
        for t in range(2):
            g_out = tn(mx_s[t], la_s[...]).astype(bf16)
            for j in range(2):
                first = OUT + j * 256
                grads[t, first : first + 256, :] = g_out[:, j * 256 : (j + 1) * 256]

    def store_in(t, part):
        first = IN + part * 512
        grads[t, first : first + 512, :] = tn(na_s[...], pj_s[t, part]).astype(bf16)

    def widen(source, temp, spare, target, scaled):
        temp[0 : images * WIN, :] = source[0 : images * WIN, :].astype(f32)
        pad = jnp.zeros((WIDE - SIDE, D), f32)
        for n in range(images):
            for i in range(n * SIDE, (n + 1) * SIDE):
                cells = temp[i * SIDE : (i + 1) * SIDE, :]
                if scaled:
                    cells = cells * (n < limit).astype(f32)
                spare[i * WIDE : i * WIDE + SIDE, :] = cells
                spare[i * WIDE + SIDE : (i + 1) * WIDE, :] = pad
        target[...] = spare[...].astype(bf16)

    loop = lax.fori_loop
    hooks.tokens()
    widen(nb_s, at_s, af_s, x_s, False)
    loop(0, images, prepare, 0)
    hooks.weights()
    other_half = 1 - first_half

    def fore(i, carry):
        later = i // images
        attend(first_half + (other_half - first_half) * later, lax.rem(i, images))
        hooks.fore(i)
        return carry

    loop(0, 2 * images, fore, 0)
    hooks.cotangent()
    widen(lb_s, at_s, da_s, co_s, True)
    loop(0, images, finish, 0)
    hooks.arrived()
    loop(0, images, feed, 0)
    narrow_rows(gin, af_s)
    hooks.output()
    for u in range(2):
        store_down(u)
        hooks.point("D%d" % u)
    for u in range(2):
        store_up(u)
        hooks.point("U%d" % u)
    store_out()
    hooks.point("O")

    def aft(n, carry):
        dn_s[padded(n), :] = recede(other_half, n)
        hooks.back(n)
        return carry

    loop(0, images, aft, 0)
    for part in (2, 1, 0):
        store_in(other_half, part)
        hooks.point("A%d" % part)

    def aft2(n, carry):
        dn_s[padded(n), :] += recede(first_half, n)
        hooks.back(images + n)
        return carry

    loop(0, images, aft2, 0)
    for part in (2, 1, 0):
        store_in(first_half, part)
        hooks.point("B%d" % part)
    loop(0, images, rise, 0)
    narrow_rows(gin, da_s)
    for t in range(2):
        gsmall[0:9, t * 256 : (t + 1) * 256] = gtaps[t, 0:9, :]
    hooks.finished()


class Quiet:
    def __init__(self, tok, cot, nb_s, lb_s, out, gin):
        self.refs = tok, cot, nb_s, lb_s, out, gin

    def tokens(self):
        tok, cot, nb_s, lb_s, _, _ = self.refs
        rows = tok.shape[0]
        nb_s[0:rows, :] = tok[...]
        lb_s[0:rows, :] = cot[...]

    def output(self):
        _, _, _, _, out, gin = self.refs
        out[...] = gin[...].astype(bf16)

    def point(self, name):
        pass

    back = fore = point

    def weights(self):
        pass

    cotangent = arrived = finished = weights


def block_kernel(images, lim, tok, cot, wi, wo, wu, wd, small, vecs, out, gin, grads, gsmall, *scratch):
    quiet = Quiet(tok, cot, scratch[8], scratch[9], out, gin)
    block_body(images, lim[0], 0, quiet, wi, wo, wu, wd, small, vecs, gin, grads, gsmall, *scratch)


def block_scratch(images):
    R = images * ROWS
    K = images * KEYS
    V = pltpu.VMEM
    return (
        [V((R, D), bf16)] * 2
        + [V((R, D), f32)] * 3
        + [V((2, R, 256), f32)] * 2
        + [V((R, D), bf16)] * 4
        + [V((2, R, 256), bf16)]
        + [V((2, K, 256), bf16)] * 4
        + [V((R, FF), bf16)] * 2
        + [
            V((2, 3, R, 256), bf16),
            V((2, images * 2, KEYS, 4 * KEYS), bf16),
            V((2, 16, 256), f32),
            V((KEYS, 4 * KEYS), bf16),
        ]
    )


def block(lim, tok, cot, wi, wo, wu, wd, small, vecs):
    images = tok.shape[0] // WIN
    S = jax.ShapeDtypeStruct
    V = pltpu.VMEM
    return pl.pallas_call(
        functools.partial(block_kernel, images),
        out_shape=(
            S(tok.shape, bf16),
            S(tok.shape, f32),
            S((2, GROWS, 256), bf16),
            S((24, D), f32),
        ),
        in_specs=[pl.BlockSpec(memory_space=pltpu.SMEM)] + [pl.BlockSpec(memory_space=V)] * 8,
        out_specs=[pl.BlockSpec(memory_space=V)] * 4,
        scratch_shapes=block_scratch(images),
        compiler_params=pltpu.CompilerParams(vmem_limit_bytes=62 * 1024 * 1024),
    )(lim, tok, cot, wi, wo, wu, wd, small, vecs)


def tile_loop(rows, size, body):
    if rows <= size:
        body(0, rows)
        return

    def step(i, carry):
        body(pl.multiple_of(i * size, size), size)
        return carry

    lax.fori_loop(0, rows // size, step, 0)


def aligned(first, size):
    return pl.ds(pl.multiple_of(first, 16), size)


def spread(part, transposed):
    shape = (768, 256) if transposed else (256, 768)
    narrow_side, wide_side = (1, 0) if transposed else (0, 1)
    a = lax.broadcasted_iota(jnp.int32, shape, narrow_side)
    b = lax.broadcasted_iota(jnp.int32, shape, wide_side)
    return jnp.where(b == (a // HD) * (3 * HD) + part * HD + lax.rem(a, HD), 1.0, 0.0).astype(bf16)


def adam(w, m, v, g, rate, decay):
    m = 0.5 * m + 0.5 * g
    v = 0.5 * v + 0.5 * g * g
    scale = 1.0 / (1.0 - 0.5**STEP)
    w = w - rate * ((m * scale) / (jnp.sqrt(v * scale) + 1e-08) + decay * w)
    return w, m, v


MATRICES = (
    (1024, 512, FF**-0.5, 4),
    (512, 1024, D**-0.5, 4),
    (256, 512, (D // HD) ** -0.5, 1),
    (512, 768, D**-0.5, 2),
)


def adam_kernel(*refs):
    full, small_sum = refs[:2]
    mats = refs[2:14]
    smalls = refs[14:23]
    outs = refs[23:39]
    small_outs = refs[39:48]
    bufs = refs[48:60]
    lows = refs[60:64]
    in_sem, out_sem = refs[64:]
    loads = {}
    for i, (rows, cols, rate, pieces) in enumerate(MATRICES):
        size = rows // pieces
        for p in range(pieces):
            rs = pl.ds(p * size, size)
            for j in range(3):
                go = pltpu.make_async_copy(
                    mats[3 * i + j].at[rs, :], bufs[3 * i + j].at[rs, :], in_sem.at[i, p, j]
                )
                go.start()
                loads[i, p, j] = go
    stores = []
    for i, (rows, cols, rate, pieces) in enumerate(MATRICES):
        size = rows // pieces
        bw, bm, bv = bufs[3 * i : 3 * i + 3]
        low = lows[i]
        for p in range(pieces):
            for j in range(3):
                loads[i, p, j].wait()

            def body(first, tile, i=i, p=p, bw=bw, bm=bm, bv=bv, low=low, rate=rate, size=size):
                rs = pl.ds(p * size + first, tile)
                if i == 0:
                    g = [
                        full[pl.ds(DOWN + (p // 2 * 2 + j) * 512 + p % 2 * size + first, tile), :]
                        for j in range(2)
                    ]
                elif i == 1:
                    g = [full[pl.ds(UP + j * 512 + p * size + first, tile), :] for j in range(4)]
                elif i == 2:
                    g = [full[pl.ds(OUT + j * 256 + p * size + first, tile), :] for j in range(2)]
                else:
                    g = None
                    for part in range(3):
                        own = full[pl.ds(IN + part * 512 + p * size + first, tile), :]
                        term = nn(own, spread(part, False))
                        g = term if g is None else g + term
                if i < 3:
                    g = jnp.concatenate(g, axis=1).astype(f32)
                w, m, v = adam(bw[rs, :], bm[rs, :], bv[rs, :], g, rate, 0.05)
                bw[rs, :] = w
                bm[rs, :] = m
                bv[rs, :] = v
                low[rs, :] = w.astype(bf16)

            tile_loop(size, 32, body)
            rs = pl.ds(p * size, size)
            for j, src in enumerate((bw, bm, bv, low)):
                go = pltpu.make_async_copy(
                    src.at[rs, :], outs[4 * i + j].at[rs, :], out_sem.at[i, p, j]
                )
                go.start()
                stores.append(go)
    x = lax.axis_index("tensor")
    mine = pl.ds(pl.multiple_of(x * 256, 256), 256)
    g_small = small_sum[:, mine]
    both = small_sum[16:20, :]
    first = jnp.where(x == 0, 1.0, 0.0)
    g_bias = jnp.concatenate(
        [
            (both[j : j + 1, :] * first + both[2 + j : 3 + j, :] * (1.0 - first))
            for j in range(2)
        ],
        axis=1,
    )
    for i, (g, rate, decay) in enumerate(
        ((g_small[0:9], 2.0, 0.05), (g_bias, 0.3, 0.0), (g_small[9:16], 0.3, 0.0))
    ):
        w = smalls[3 * i][...] if i < 2 else smalls[6][:, mine]
        new = adam(w, smalls[3 * i + 1][...], smalls[3 * i + 2][...], g, rate, decay)
        for j in range(3):
            small_outs[3 * i + j][...] = new[j]
    for go in stores:
        go.wait()


def adam_step(full, small_sum, mats, smalls):
    S = jax.ShapeDtypeStruct
    V = pltpu.VMEM
    mat_shapes = [(rows, cols) for rows, cols, _, _ in MATRICES]
    any_spec = pl.BlockSpec(memory_space=pl.ANY)
    vmem_spec = pl.BlockSpec(memory_space=V)
    small_shapes = [(9, 256)] * 3 + [(1, 1024)] * 3 + [(7, 256)] * 3
    return pl.pallas_call(
        adam_kernel,
        out_shape=tuple(
            S(shape, kind) for shape in mat_shapes for kind in (f32, f32, f32, bf16)
        )
        + tuple(S(shape, f32) for shape in small_shapes),
        in_specs=[vmem_spec] * 2 + [any_spec] * 12 + [vmem_spec] * 9,
        out_specs=[any_spec] * 16 + [vmem_spec] * 9,
        scratch_shapes=[V(shape, f32) for shape in mat_shapes for _ in range(3)]
        + [V(shape, bf16) for shape in mat_shapes]
        + [pltpu.SemaphoreType.DMA((4, 4, 3)), pltpu.SemaphoreType.DMA((4, 4, 4))],
        compiler_params=pltpu.CompilerParams(vmem_limit_bytes=48 * 1024 * 1024),
    )(full, small_sum, *mats, *smalls)


CHUNKS = (
    (DOWN, 1024), (DOWN + 1024, 1024), (UP, 1024), (UP + 1024, 1024), (OUT, 512),
    (IN + 1024, 512), (IN + 512, 512), (IN, 512),
)
D0, D1, U0, U1, O0, V0, K0, G0 = range(8)
SLOTS = 12
PLAN = {
    "D0": ((D0, 0),),
    "D1": ((D1, 0), (D0, 1)),
    "U0": ((U0, 0), (D1, 1)),
    "U1": ((U1, 0), (U0, 1)),
    "O": ((O0, 0), (U1, 1)),
    0: ((O0, 1),),
    1: ((D0, 2),),
    2: (),
    3: ((D0, 3),),
    "A2": ((V0, 0),),
    "A1": ((K0, 0), (V0, 1)),
    "A0": ((G0, 0), (K0, 1)),
    4: ((G0, 1), (D1, 2), (D0, 4)),
    5: (),
    6: ((D0, 5), (D1, 3)),
    7: ((U0, 2), (D0, 6), (D1, 4)),
    "B2": ((V0, 2),),
    "B1": ((K0, 2),),
    "B0": ((G0, 2),),
}
TAIL = (
    ((D0, 7), (D1, 5), (U0, 3), (U1, 2)),
    ((D1, 6), (U0, 4), (U1, 3), (O0, 2)),
    ((D1, 7), (U0, 5), (U1, 4), (O0, 3), (V0, 3)),
    ((U0, 6), (U1, 5), (O0, 4), (V0, 4), (K0, 3)),
    ((U0, 7), (U1, 6), (O0, 5), (V0, 5), (K0, 4), (G0, 3)),
    ((U1, 7), (O0, 6), (V0, 6), (K0, 5), (G0, 4)),
    ((O0, 7), (V0, 7), (K0, 6), (G0, 5)),
    ((V0, 8), (K0, 7), (G0, 6)),
    ((K0, 8), (G0, 7)),
    ((G0, 8),),
)


class Traffic:
    def __init__(self, images, refs):
        (self.tok, self.cot, self.w_in, self.w_out, self.w_up, self.w_down, self.own_small,
         self.out, self.gin, self.full, self.small_sum,
         self.gin_v, self.grads, self.gsmall, self.wi, self.wo, self.wu, self.wd, self.small,
         self.at_s, self.af_s, self.da_s, self.gp_s, self.mf_s, self.nb_s, self.lb_s, self.out_v,
         self.cores, self.xs, self.ys, self.zs, self.firsts,
         self.small_in, self.small_z, self.send, self.recv, self.ssend, self.srecv,
         self.wsend, self.wrecv, self.load, self.save) = refs
        self.images = images
        dp, x = lax.axis_index("dp"), lax.axis_index("tensor")
        core, y, z = lax.rem(dp, 2), lax.rem(dp // 2, 2), dp // 4

        def at(zz, yy, cc, xx):
            return ((zz * 2 + yy) * 2 + cc, xx)

        self.x, self.core, self.y, self.z = x, core, y, z
        self.core_mate = at(z, y, 1 - core, x)
        self.x_mate = at(z, y, core, 1 - x)
        self.y_mate = at(z, 1 - y, core, x)
        self.z_others = [lax.rem(z + k, 4) for k in range(1, 4)]
        self.z_mates = [at(o, y, core, x) for o in self.z_others]
        self.loads = [
            pltpu.make_async_copy(src, dst, self.load.at[i])
            for i, (src, dst) in enumerate(
                (
                    (self.w_in.at[:, 0:256], self.mf_s.at[0, 0:512, :]),
                    (self.w_in.at[:, 256:512], self.mf_s.at[1, 0:512, :]),
                    (self.w_in.at[:, 512:768], self.gp_s.at[0, 0:512, :]),
                    (self.w_out, self.da_s.at[512:768, :]),
                    (self.w_up.at[:, 0:512], self.da_s.at[0:512, :]),
                    (self.w_up.at[:, 512:1024], self.af_s.at[0:512, :]),
                    (self.w_down.at[0:512, :], self.gin_v.at[0:512, :]),
                    (self.w_down.at[512:896, :], self.af_s.at[512:896, :]),
                    (self.w_down.at[896:1024, :], self.da_s.at[768:896, :]),
                    (self.tok, self.nb_s.at[0 : images * WIN, :]),
                    (self.cot, self.lb_s.at[0 : images * WIN, :]),
                )
            )
        ]


    def weight_copy(self, src, dst, item, slot, mate):
        return pltpu.make_async_remote_copy(
            src_ref=src,
            dst_ref=dst,
            send_sem=self.wsend.at[item, slot],
            recv_sem=self.wrecv.at[item, slot],
            device_id=mate,
            device_id_type=MESH,
        )

    def view(self, item, half, yy, cc):
        quarter = yy * 2 + cc
        if item == 0:
            return self.wi.at[half, :, aligned(quarter * 128, 128), :]
        ref, size = ((self.wo, 64), (self.wu, 128), (self.wd, 256))[item - 1]
        return ref.at[half, aligned(quarter * size, size), :]

    def crossing(self, item):
        if item == 4:
            own = self.small.at[self.x]
        else:
            own = self.view(item, self.x, self.y, self.core)
        return self.weight_copy(own, own, item, 0, self.x_mate)

    def inward(self, item):
        got = self.view(item, 1 - self.x, self.y, self.core)
        return self.weight_copy(got, got, item, 1, self.core_mate)

    def aside(self, item):
        got = self.view(item, 1 - self.x, self.y, self.core)
        return self.weight_copy(got, got, item, 2, self.y_mate)

    def onward(self, item):
        got = self.view(item, 1 - self.x, 1 - self.y, self.core)
        return self.weight_copy(got, got, item, 3, self.core_mate)

    def cast(self, rows, size, source, target):
        def body(first, tile):
            here = pl.ds(first, tile)
            target[here, :] = source[here, :].astype(bf16)

        tile_loop(rows, size, body)

    def begin(self):
        for go in self.loads:
            go.start()
        barrier = pltpu.get_barrier_semaphore()
        for mate in (self.core_mate, self.x_mate, self.y_mate, *self.z_mates):
            pl.semaphore_signal(barrier, inc=1, device_id=mate, device_id_type=MESH)
        x = self.x
        self.small[x] = self.own_small[...]
        for go in self.loads[0:3]:
            go.wait()
        spreads = [spread(part, True) for part in range(3)]

        def body(first, tile):
            rows = pl.ds(first, tile)
            low = jnp.concatenate(
                [self.mf_s[0, rows, :], self.mf_s[1, rows, :], self.gp_s[0, rows, :]], axis=1
            ).astype(bf16)
            for part in range(3):
                self.wi[x, part, rows, :] = nn(low, spreads[part]).astype(bf16)

        tile_loop(512, 128, body)
        pl.semaphore_wait(barrier, 6)
        self.crossing(0).start()
        self.crossing(4).start()
        for go in self.loads[3:9]:
            go.wait()
        self.cast(256, 64, self.da_s.at[512:768, :], self.wo.at[x])
        self.crossing(1).start()
        self.cast(512, 64, self.da_s.at[0:512, :], self.wu.at[x, :, 0:512])
        self.cast(512, 64, self.af_s.at[0:512, :], self.wu.at[x, :, 512:1024])
        self.crossing(2).start()
        self.cast(512, 64, self.gin_v.at[0:512, :], self.wd.at[x, 0:512, :])
        self.cast(384, 64, self.af_s.at[512:896, :], self.wd.at[x, 512:896, :])
        self.cast(128, 64, self.da_s.at[768:896, :], self.wd.at[x, 896:1024, :])
        self.crossing(3).start()

    def tokens(self):
        self.loads[9].wait()

    def weights(self):
        pass

    def fore(self, i):
        def passed(item):
            self.crossing(item).wait()
            self.inward(item).start()
            self.aside(item).start()

        def turned(item):
            self.aside(item).wait()
            self.onward(item).start()

        def done(item):
            self.inward(item).wait()
            self.onward(item).wait()

        last = self.images - 1

        @pl.when(i == 1)
        def _():
            passed(0)

        @pl.when(i == 2)
        def _():
            passed(1)

        @pl.when(i == last)
        def _():
            turned(0)
            self.crossing(4).wait()
            done(0)

        @pl.when(i == last + 1)
        def _():
            passed(2)
            turned(1)

        @pl.when(i == last + 3)
        def _():
            passed(3)
            turned(2)

        @pl.when(i == last + 4)
        def _():
            turned(3)
            done(1)

    def cotangent(self):
        self.loads[10].wait()

    def arrived(self):
        for item in (2, 3):
            self.inward(item).wait()
            self.onward(item).wait()


    def output(self):
        self.out_v[...] = self.gin_v[...].astype(bf16)
        self.saving(0).start()

    def saving(self, i):
        src, dst = (
            (self.out_v, self.out),
            (self.gin_v, self.gin),
            (self.grads.at[0], self.full),
        )[i]
        return pltpu.make_async_copy(src, dst, self.save.at[i])

    def finished(self):
        self.saving(1).start()


    def copy(self, src, dst, chunk, slot, mate):
        return pltpu.make_async_remote_copy(
            src_ref=src,
            dst_ref=dst,
            send_sem=self.send.at[chunk, slot],
            recv_sem=self.recv.at[chunk, slot],
            device_id=mate,
            device_id_type=MESH,
        )

    def flights(self, c, s):
        base, R = CHUNKS[c]
        half, quarter, piece = R // 2, R // 4, R // 16
        x, y, z, core, grads = self.x, self.y, self.z, self.core, self.grads
        mine = base + core * half
        theirs = aligned(base + (1 - core) * half, half)
        if c >= V0:
            if s == 0:
                src = grads.at[1 - x, theirs, :]
                return [self.copy(src, self.firsts[c - V0], c, 11, self.core_mate)]
            if s == 1:
                return [self.copy(self.firsts[c - V0], self.xs[c], c, 1, self.x_mate)]
            if s == 2:
                return [self.copy(grads.at[x, theirs, :], self.cores[c], c, 0, self.core_mate)]
            s -= 1
        else:
            if s == 0:
                return [self.copy(grads.at[:, theirs, :], self.cores[c], c, 0, self.core_mate)]
            if s == 1:
                return [self.copy(self.cores[c].at[1 - x], self.xs[c], c, 1, self.x_mate)]
        if s == 2:
            src = self.xs[c].at[aligned((1 - y) * quarter, quarter), :]
            return [self.copy(src, self.ys[c], c, 2, self.y_mate)]
        if s == 3:
            return [
                self.copy(
                    self.ys[c].at[aligned(self.z_others[k] * piece, piece), :],
                    self.zs[c].at[k],
                    c,
                    3 + k,
                    self.z_mates[k],
                )
                for k in range(3)
            ]
        if s == 4:
            own = grads.at[0, aligned(mine + y * quarter + z * piece, piece), :]
            return [self.copy(own, own, c, 6 + k, self.z_mates[k]) for k in range(3)]
        if s == 5:
            own = grads.at[0, aligned(mine + y * quarter, quarter), :]
            return [self.copy(own, own, c, 9, self.y_mate)]
        if s == 6:
            own = grads.at[0, aligned(mine, half), :]
            return [self.copy(own, own, c, 10, self.core_mate)]
        return []

    def stage(self, c, s):
        base, R = CHUNKS[c]
        half, quarter, piece = R // 2, R // 4, R // 16
        x, y, z, core, grads = self.x, self.y, self.z, self.core, self.grads
        mine = base + core * half
        late = c >= V0
        if s > 0 and not (late and s == 2):
            for flight in self.flights(c, s - 1):
                flight.wait()
        if late and s == 3:
            self.flights(c, 1)[0].wait()

        def total(target, *parts):
            out = None
            for part in parts:
                part = part.astype(f32)
                out = part if out is None else out + part
            return out.astype(bf16)

        cores, xs, ys, zs = self.cores[c], self.xs[c], self.ys[c], self.zs[c]
        step = s - 1 if late else s
        if late and s == 1:
            first = self.firsts[c - V0]

            def body(i, size):
                rows, own = pl.ds(i, size), aligned(mine + i, size)
                first[rows, :] = total(None, grads[1 - x, own, :], first[rows, :])

            tile_loop(half, 128, body)
        elif late and s == 3:

            def body(i, size):
                rows, own = pl.ds(i, size), aligned(mine + i, size)
                xs[rows, :] = total(None, grads[x, own, :], cores[rows, :], xs[rows, :])

            tile_loop(half, 128, body)
        elif not late and s == 1:

            def body(i, size):
                rows, own = pl.ds(i, size), aligned(mine + i, size)
                for t in range(2):
                    cores[t, rows, :] = total(None, grads[t, own, :], cores[t, rows, :])

            tile_loop(half, 128, body)
        elif not late and s == 2:

            def body(i, size):
                rows = pl.ds(i, size)
                xs[rows, :] = total(None, cores[x, rows, :], xs[rows, :])

            tile_loop(half, 128, body)
        elif step == 3:

            def body(i, size):
                rows, own = pl.ds(i, size), aligned(y * quarter + i, size)
                ys[rows, :] = total(None, xs[own, :], ys[rows, :])

            tile_loop(quarter, 128, body)
        elif step == 4:
            own = aligned(z * piece, piece)
            grads[0, aligned(mine + y * quarter + z * piece, piece), :] = total(
                None, ys[own, :], zs[0], zs[1], zs[2]
            )
        for flight in self.flights(c, s):
            flight.start()

    def small_flights(self, s):
        def small_copy(src, dst, slot, mate):
            return pltpu.make_async_remote_copy(
                src_ref=src,
                dst_ref=dst,
                send_sem=self.ssend.at[slot],
                recv_sem=self.srecv.at[slot],
                device_id=mate,
                device_id_type=MESH,
            )

        if s < 3:
            mate = (self.core_mate, self.x_mate, self.y_mate)[s]
            return [small_copy(self.small_z.at[s], self.small_in.at[s], s, mate)]
        return [
            small_copy(self.small_z.at[3], self.small_z.at[4 + self.z], 3 + k, self.z_mates[k])
            for k in range(3)
        ]

    def small_stage(self, s):
        small_z = self.small_z
        if s > 0:
            for flight in self.small_flights(s - 1):
                flight.wait()
        if s == 0:
            small_z[0] = self.gsmall[...]
        elif s <= 3:
            small_z[s] = small_z[s - 1] + self.small_in[s - 1]
        else:
            self.small_sum[...] = (small_z[4] + small_z[5]) + (small_z[6] + small_z[7])
            return
        if s == 3:
            small_z[4 + self.z] = small_z[3]
        for flight in self.small_flights(s):
            flight.start()

    def point(self, name):
        for c, s in PLAN[name]:
            self.stage(c, s)

    def back(self, i):
        for k in range(2 * self.images):
            if PLAN[k]:

                @pl.when(i == k)
                def _(k=k):
                    self.point(k)

    def end(self):
        self.small_stage(0)
        for k, wave in enumerate(TAIL):
            for c, s in wave:
                self.stage(c, s)
            if k < 4:
                self.small_stage(k + 1)
        self.saving(2).start()
        for i in range(3):
            self.saving(i).wait()


def main_kernel(images, counts, tok, cot, w_in, w_out, w_up, w_down, own_small, vecs,
                out, gin, full, small_sum, *scratch):
    n = len(block_scratch(images))
    inner, rest = scratch[:n], scratch[n:]
    gin_v, grads, gsmall, wi, wo, wu, wd, small = rest[:8]
    rest = rest[8:]
    cores, xs, ys, zs = (rest[8 * i : 8 * i + 8] for i in range(4))
    firsts = rest[32:35]
    x_s, co_s, at_s, af_s, da_s, gp_s, mf_s, na_s, nb_s, lb_s = inner[:10]
    traffic = Traffic(
        images,
        (tok, cot, w_in, w_out, w_up, w_down, own_small, out, gin, full, small_sum,
         gin_v, grads, gsmall, wi, wo, wu, wd, small,
         at_s, af_s, da_s, gp_s, mf_s, nb_s, lb_s, co_s.at[0 : images * WIN, :],
         cores, xs, ys, zs, firsts, *rest[35:]),
    )
    x = lax.axis_index("tensor")
    limit = counts[lax.axis_index("dp")] - x * images
    traffic.begin()
    block_body(
        images, limit, x, traffic, wi, wo, wu, wd, small, vecs, gin_v, grads, gsmall, *inner
    )
    traffic.end()


def main_call(counts, tok, cot, w_in, w_out, w_up, w_down, own_small, vecs):
    images = tok.shape[0] // WIN
    S = jax.ShapeDtypeStruct
    V = pltpu.VMEM
    away = pl.BlockSpec(memory_space=pl.ANY)
    here = pl.BlockSpec(memory_space=V)
    sizes = [R for _, R in CHUNKS]
    dma = pltpu.SemaphoreType.DMA
    return pl.pallas_call(
        functools.partial(main_kernel, images),
        out_shape=(
            S(tok.shape, bf16),
            S(tok.shape, f32),
            S((GROWS, 256), bf16),
            S((24, D), f32),
        ),
        in_specs=[pl.BlockSpec(memory_space=pltpu.SMEM)] + [away] * 6 + [here] * 2,
        out_specs=[away] * 3 + [here],
        scratch_shapes=block_scratch(images)
        + [
            V(tok.shape, f32),
            V((2, GROWS, 256), bf16),
            V((24, D), f32),
            V((2, 3, D, 256), bf16),
            V((2, 256, D), bf16),
            V((2, D, 1024), bf16),
            V((2, 1024, D), bf16),
            V((2, 16, 256), f32),
        ]
        + [V((2, R // 2, 256), bf16) for R in sizes[:5]]
        + [V((R // 2, 256), bf16) for R in sizes[5:]]
        + [V((R // 2, 256), bf16) for R in sizes]
        + [V((R // 4, 256), bf16) for R in sizes]
        + [V((3, R // 16, 256), bf16) for R in sizes]
        + [V((R // 2, 256), bf16) for R in sizes[5:]]
        + [
            V((3, 24, D), f32),
            V((8, 24, D), f32),
            dma((8, SLOTS)),
            dma((8, SLOTS)),
            dma((6,)),
            dma((6,)),
            dma((5, 4)),
            dma((5, 4)),
            dma((11,)),
            dma((3,)),
        ],
        compiler_params=pltpu.CompilerParams(
            collective_id=1, has_side_effects=True, vmem_limit_bytes=63 * 1024 * 1024
        ),
    )(counts, tok, cot, w_in, w_out, w_up, w_down, own_small, vecs)


def local(
    tokens, cotangent, image_counts,
    w_in, m_in, v_in, w_out, m_out, v_out, w_up, m_up, v_up, w_down, m_down, v_down,
    kernel, m_kernel, v_kernel, up_bias, m_bias, v_bias, vectors, m_vectors, v_vectors,
):
    own_small = jnp.concatenate(
        [kernel, up_bias.reshape(4, 256), jnp.zeros((3, 256), f32)], axis=0
    )
    out, grad_in, full, small_sum = main_call(
        image_counts, tokens, cotangent, w_in, w_out, w_up, w_down, own_small, vectors
    )
    new = adam_step(
        full,
        small_sum,
        (w_down, m_down, v_down, w_up, m_up, v_up, w_out, m_out, v_out, w_in, m_in, v_in),
        (kernel, m_kernel, v_kernel)
        + tuple(a.reshape(1, -1) for a in (up_bias, m_bias, v_bias))
        + (vectors, m_vectors, v_vectors),
    )
    down, up, mid, first = new[:4], new[4:8], new[8:12], new[12:16]
    bias = tuple(a.reshape(-1) for a in new[19:22])
    return (out, grad_in, *first, *mid, *up, *down, *new[16:19], *bias, *new[22:25])


def general(
    tokens, cotangent, image_counts,
    w_in, m_in, v_in, w_out, m_out, v_out, w_up, m_up, v_up, w_down, m_down, v_down,
    kernel, m_kernel, v_kernel, up_bias, m_bias, v_bias, vectors, m_vectors, v_vectors,
):
    images = tokens.shape[0] // WIN
    place = lax.axis_index("tensor")
    live = image_counts[lax.axis_index("dp")] - place * images

    def whole(a, axis):
        return lax.all_gather(a, "tensor", axis=axis, tiled=True)

    wi = whole(w_in.astype(bf16), 1).reshape(D, 2, 8, 3, HD).transpose(1, 3, 0, 2, 4)
    wi = wi.reshape(2, 3, D, 256)
    wo = whole(w_out.astype(bf16), 0).reshape(2, 256, D)
    wd = whole(w_down.astype(bf16), 0).reshape(2, 1024, D)
    wu = whole(w_up.astype(bf16), 1).reshape(D, 2, 1024).transpose(1, 0, 2)
    small = jnp.concatenate(
        [
            whole(kernel, 1).reshape(9, 2, 256).transpose(1, 0, 2),
            whole(up_bias, 0).reshape(2, 4, 256),
            jnp.zeros((2, 3, 256), f32),
        ],
        axis=1,
    )
    out, grad_in, grads, gs = block(
        live.reshape(1), tokens, cotangent, wi, wo, wu, wd, small, vectors
    )
    grads = grads.astype(f32)

    def columns(first, rows, count):
        part = grads[:, first : first + rows * count].reshape(2, count, rows, 256)
        return part

    g_down = grads[:, DOWN:UP].reshape(2, 2, 2, 512, 256).transpose(0, 1, 3, 2, 4).reshape(FF, D)
    g_up = columns(UP, 512, 4).transpose(2, 0, 1, 3).reshape(D, FF)
    g_out = columns(OUT, 256, 2).transpose(0, 2, 1, 3).reshape(D, D)
    g_in = columns(IN, 512, 3).reshape(2, 3, D, 8, HD).transpose(2, 0, 3, 1, 4).reshape(D, 3 * D)

    def owned(a, axis):
        return lax.psum(lax.psum_scatter(a, "tensor", scatter_dimension=axis, tiled=True), "dp")

    g_in, g_out, g_up, g_down = owned(g_in, 1), owned(g_out, 0), owned(g_up, 1), owned(g_down, 0)
    g_kernel, g_bias, g_vectors = owned(gs[0:9], 1), owned(gs[16:20].reshape(-1), 0), owned(gs[9:16], 1)
    vector_width = m_vectors.shape[1]
    own_vectors = lax.dynamic_slice_in_dim(vectors, place * vector_width, vector_width, 1)
    results = [out, grad_in]
    for w, m, v, g, rate in (
        (w_in, m_in, v_in, g_in, D**-0.5),
        (w_out, m_out, v_out, g_out, (D // HD) ** -0.5),
        (w_up, m_up, v_up, g_up, D**-0.5),
        (w_down, m_down, v_down, g_down, FF**-0.5),
    ):
        new = adam(w, m, v, g, rate, 0.05)
        results += [*new, new[0].astype(bf16)]
    results += adam(kernel, m_kernel, v_kernel, g_kernel, 2.0, 0.05)
    results += adam(up_bias, m_bias, v_bias, g_bias, 0.3, 0.0)
    results += adam(own_vectors, m_vectors, v_vectors, g_vectors, 0.3, 0.0)
    return tuple(results)


def solution(mesh):
    rows, columns = P("tensor", None), P(None, "tensor")
    tokens = P(("dp", "tensor"), None)
    mats = (columns,) * 3 + (rows,) * 3 + (columns,) * 3 + (rows,) * 3
    news = (columns,) * 4 + (rows,) * 4 + (columns,) * 4 + (rows,) * 4
    pairs = mesh.shape["dp"] == 16 and mesh.shape["tensor"] == 2
    return jax.shard_map(
        local if pairs else general,
        mesh=mesh,
        in_specs=(tokens, tokens, P(), *mats)
        + (columns,) * 3
        + (P("tensor"),) * 3
        + (P(), columns, columns),
        out_specs=(tokens, tokens, *news) + (columns,) * 3 + (P("tensor"),) * 3 + (columns,) * 3,
        check_vma=False,
    )
```

time: 218 us -> 169 us (0.78)
  Pallas kernels: 200 us -> 157 us
  local copies, waits for them, and re-layouts: 15.3 us -> 9.36 us
    pallas_call x3 -> x1, Pallas kernels: 178 us -> 136 us  [main_call(): pl.pallas_call(functools.partial(main_kernel, images), out_shape=(S(tok.s...]
    unnamed x50 -> x36, local copies, waits for them, and re-layouts: 13.3 us -> 8.59 us
where the time goes in v2:
time: 169 us
  Pallas kernels  157 us (93%)
  local copies, waits for them, and re-layouts  9.36 us (6%)
    pallas_call x1, Pallas kernels, main_call(): pl.pallas_call(functools.partial(main_kernel, images), out_shape=(S(tok.s...  136 us
    pallas_call x1, Pallas kernels, adam_step(): pl.pallas_call(adam_kernel, out_shape=tuple((S(shape, kind) for shape in...  21.7 us
    unnamed x36, local copies, waits for them, and re-layouts  8.59 us

profile of v2, /device:TPU:0, one launch (start us, length us, event | category | flops | bytes accessed | tf_op | source)
XLA Modules:
  0.0 168.9 jit_solution(4414012000412894115)
XLA Ops:
  0.7 0.1 pad.2.clone
  0.8 0.7 reshape.75
  1.4 1.4 maximum_maximum_fusion.own_small
  2.8 0.0 copy-start.1
  2.8 0.0 copy-start.5
  2.8 0.0 copy-start.6
  2.8 0.0 copy-start.8
  2.9 0.0 copy-start.9
  2.9 0.0 copy-start.10
  2.9 0.0 copy-start.11
  2.9 0.0 copy-start.12
  2.9 0.0 copy-start.13
  2.9 0.0 copy-start.14
  2.9 135.7 %shard_map.439 = (bf16[784,512]{1,0:T(8,128)(2,1)}, f32[784,512]{1,0:T(8,128)}, bf16[6144,256]{1,0:T(8,128)(2,1)}, f32[24,512]{1,0:T(8,128)}) custom-call(s32[16]{0:T(128)} %counts.1, bf16[784,512]{1,0:T(8,128)(2,1)} %tok.1, bf16[784,512]{1,0:T(8,128)(2,1)} %cot.1, f32[512,768]{1,0:T(8,128)} %refs_11_.1, f32[256,512]{1,0:T(8,128)} %refs_8_.1, ...), custom_call_target="tpu_custom_call" | custom-call | tf_op jit(solution)/shard_map/pallas_call | solution.py:1087
  138.6 0.0 copy-done.1
  138.6 0.0 copy-done.5
  138.6 0.0 copy-done.6
  138.6 0.0 copy-done.8
  138.6 0.0 copy-done.9
  138.6 0.0 copy-done.10
  138.7 0.0 copy-done.11
  138.7 0.0 copy-done.12
  138.7 0.0 copy-done.13
  138.7 0.0 copy-done.14
  138.7 0.0 copy-start
  138.7 1.4 copy-done
  140.1 0.0 copy-start.2
  140.1 1.4 copy-done.2
  141.5 0.0 copy-start.3
  141.5 1.0 copy-done.3
  142.6 0.0 copy-start.4
  142.6 1.0 copy-done.4
  143.6 0.0 copy-start.7
  143.6 0.8 copy-done.7
  144.4 0.0 copy-start.16
  144.4 21.7 %shard_map.440 = (f32[1024,512]{1,0:T(8,128)}, f32[1024,512]{1,0:T(8,128)}, f32[1024,512]{1,0:T(8,128)}, bf16[1024,512]{1,0:T(8,128)(2,1)}, f32[512,1024]{1,0:T(...) custom-call(bf16[6144,256]{1,0:T(8,128)(2,1)} %get-tuple-element.58., ...), custom_call_target="tpu_custom_call" | custom-call | tf_op jit(solution)/shard_map/pallas_call | solution.py:620
  166.1 0.0 copy-start.15
  166.1 0.0 copy-done.16
  166.1 0.9 copy.53
  167.0 0.8 copy-done.15
  167.8 1.2 copy.54
  (1 shorter events, 0.0 us)
Async XLA Ops:
  2.8 135.8 %copy-start.1 = (f32[256,512]{1,0:T(8,128)S(1)}, f32[256,512]{1,0:T(8,128)}, u32[]{:S(2)}) copy-start(f32[256,512]{1,0:T(8,128)} %refs_8_.1) | copy-start | bytes 1572868
  2.8 135.8 %copy-start.5 = (f32[7,512]{1,0:T(8,128)S(1)}, f32[7,512]{1,0:T(8,128)}, u32[]{:S(2)}) copy-start(f32[7,512]{1,0:T(8,128)} %refs_20_.1) | copy-start | bytes 43012
  2.8 135.8 %copy-start.6 = (f32[9,256]{1,0:T(8,128)S(1)}, f32[9,256]{1,0:T(8,128)}, u32[]{:S(2)}) copy-start(f32[9,256]{1,0:T(8,128)} %refs_14_.1) | copy-start | bytes 27652
  2.8 135.8 %copy-start.8 = (f32[9,256]{1,0:T(8,128)S(1)}, f32[9,256]{1,0:T(8,128)}, u32[]{:S(2)}) copy-start(f32[9,256]{1,0:T(8,128)} %refs_15_.1) | copy-start | bytes 27652
  2.9 135.8 %copy-start.9 = (f32[9,256]{1,0:T(8,128)S(1)}, f32[9,256]{1,0:T(8,128)}, u32[]{:S(2)}) copy-start(f32[9,256]{1,0:T(8,128)} %refs_16_.1) | copy-start | bytes 27652
  2.9 135.8 %copy-start.10 = (f32[1024]{0:T(1024)S(1)}, f32[1024]{0:T(1024)}, u32[]{:S(2)}) copy-start(f32[1024]{0:T(1024)} %param.42) | copy-start | bytes 12292
  2.9 135.8 %copy-start.11 = (f32[7,256]{1,0:T(8,128)S(1)}, f32[7,256]{1,0:T(8,128)}, u32[]{:S(2)}) copy-start(f32[7,256]{1,0:T(8,128)} %refs_21_.1) | copy-start | bytes 21508
  2.9 135.8 %copy-start.12 = (f32[7,256]{1,0:T(8,128)S(1)}, f32[7,256]{1,0:T(8,128)}, u32[]{:S(2)}) copy-start(f32[7,256]{1,0:T(8,128)} %refs_22_.1) | copy-start | bytes 21508
  2.9 135.8 %copy-start.13 = (f32[1024]{0:T(1024)S(1)}, f32[1024]{0:T(1024)}, u32[]{:S(2)}) copy-start(f32[1024]{0:T(1024)} %param.43) | copy-start | bytes 12292
  2.9 135.8 %copy-start.14 = (f32[1024]{0:T(1024)S(1)}, f32[1024]{0:T(1024)}, u32[]{:S(2)}) copy-start(f32[1024]{0:T(1024)} %param.44) | copy-start | bytes 12292
  138.7 1.4 copy-start
  140.1 1.4 copy-start.2
  141.5 1.0 copy-start.3
  142.6 1.0 copy-start.4
  143.6 0.8 copy-start.7
  144.4 21.7 %copy-start.16 = (bf16[784,512]{1,0:T(8,128)(2,1)S(1)}, bf16[784,512]{1,0:T(8,128)(2,1)}, u32[]{:S(2)}) copy-start(bf16[784,512]{1,0:T(8,128)(2,1)} %get-tuple-element.112) | copy-start | bytes 2408452
  166.1 1.7 %copy-start.15 = (f32[784,512]{1,0:T(8,128)S(1)}, f32[784,512]{1,0:T(8,128)}, u32[]{:S(2)}) copy-start(f32[784,512]{1,0:T(8,128)} %get-tuple-element.113) | copy-start | bytes 4816900

commit v3 on v2

--- a/solution.py
+++ b/solution.py
@@ -184,42 +184,38 @@
         af_s[rows, :] = after
         xhat, _ = normed(after)
         nb_s[rows, :] = (xhat * gain_b + shift_b).astype(bf16)
+        lb_s[rows, :] = (scale_f * co_s[rows, :].astype(f32)).astype(bf16)
         return carry
 
-    def feed(n, carry):
+    def feed(u, n):
         rows = padded(n)
+        lb = lb_s[rows, :]
+        nb = nb_s[rows, :]
+        us = slice(u * 512, (u + 1) * 512)
+        for t in range(2):
+            c = 2 * t + u
+            cs = slice(c * 512, (c + 1) * 512)
+            unit_bias = jnp.concatenate(
+                [small[t, 9 + 2 * u + j : 10 + 2 * u + j, :] for j in range(2)], axis=1
+            )
+            value, slope = gelu_pair(nn(nb, wu[t, :, us]) + unit_bias)
+            hd_s[rows, cs] = value.astype(bf16)
+            d_pre = slope * nt(lb, wd[t, us, :])
+            gsmall[16 + c : 17 + c, :] += row_sum(d_pre)
+            dp_s[rows, cs] = d_pre.astype(bf16)
+
+    def digest(n, carry):
+        rows = padded(n)
+        branch = nn(hd_s[rows, 0:1024], wd[0]) + nn(hd_s[rows, 1024:2048], wd[1])
+        d_nb = nt(dp_s[rows, 0:1024], wu[0]) + nt(dp_s[rows, 1024:2048], wu[1])
         co = co_s[rows, :].astype(f32)
-        d_branch = scale_f * co
-        lb = d_branch.astype(bf16)
-        lb_s[rows, :] = lb
-        nb = nb_s[rows, :]
-        branch = None
-        for c in range(4):
-            cs = slice(c * 512, (c + 1) * 512)
-            us = slice((c % 2) * 512, (c % 2 + 1) * 512)
-            unit_bias = jnp.concatenate(
-                [small[c // 2, 9 + (c % 2) * 2 + j : 10 + (c % 2) * 2 + j, :] for j in range(2)],
-                axis=1,
-            )
-            pre = nn(nb, wu[c // 2, :, us]) + unit_bias
-            value, slope = gelu_pair(pre)
-            hid = value.astype(bf16)
-            hd_s[rows, cs] = hid
-            br = nn(hid, wd[c // 2, us, :])
-            d_pre = slope * nt(lb, wd[c // 2, us, :])
-            gsmall[16 + c : 17 + c, :] += row_sum(d_pre)
-            dp = d_pre.astype(bf16)
-            dp_s[rows, cs] = dp
-            dn = nt(dp, wu[c // 2, :, us])
-            branch = br if branch is None else branch + br
-            d_nb = dn if c == 0 else d_nb + dn
         after = af_s[rows, :]
         xhat, r = normed(after)
         moved = branch + bias_f
         live = (n < limit).astype(f32)
         af_s[rows, :] = (after + scale_f * moved) * live
         gsmall[14:15, :] += row_sum(co * moved)
-        gsmall[15:16, :] += row_sum(d_branch)
+        gsmall[15:16, :] += scale_f * row_sum(co)
         gsmall[11:12, :] += row_sum(d_nb * xhat)
         gsmall[12:13, :] += row_sum(d_nb)
         d_after = co + norm_back(gain_b * d_nb, xhat, r)
@@ -229,6 +225,7 @@
         la_s[rows, :] = la
         for t in range(2):
             dm_s[t, held(n), :] = nt(la, wo[t]).astype(bf16)
+        hooks.turn("d", n, images)
         return carry
 
     pick_row = lax.broadcasted_iota(jnp.int32, (256, 128), 0)
@@ -252,7 +249,7 @@
         jnp.where((lane == h) | (lane == h + 4), -1.0, 0.0).astype(bf16) for h in range(4)
     ]
 
-    def recede(t, n):
+    def recede(t, n, turn):
         rows = padded(n)
         for g in range(2):
             ls = slice(g * 128, (g + 1) * 128)
@@ -301,6 +298,7 @@
                     d_cols[b] = term if d_cols[b] is None else d_cols[b] + term
             d_field = roll1(d_cols[0], -1) + d_cols[1] + roll1(d_cols[2], 1)
             pj_s[t, 0, rows, ls] = jnp.where(inside, slope * d_field, 0.0).astype(bf16)
+            hooks.turn("r", turn + g, 4 * images)
         d_na = None
         for part in range(3):
             term = nt(pj_s[t, part, rows, :], wi[t, part])
@@ -347,21 +345,24 @@
         first = IN + part * 512
         grads[t, first : first + 512, :] = tn(na_s[...], pj_s[t, part]).astype(bf16)
 
-    def widen(source, temp, spare, target, scaled):
+    def widen(source, spares, target, scaled):
+        temp = at_s
         temp[0 : images * WIN, :] = source[0 : images * WIN, :].astype(f32)
-        pad = jnp.zeros((WIDE - SIDE, D), f32)
-        for n in range(images):
-            for i in range(n * SIDE, (n + 1) * SIDE):
-                cells = temp[i * SIDE : (i + 1) * SIDE, :]
-                if scaled:
-                    cells = cells * (n < limit).astype(f32)
-                spare[i * WIDE : i * WIDE + SIDE, :] = cells
-                spare[i * WIDE + SIDE : (i + 1) * WIDE, :] = pad
-        target[...] = spare[...].astype(bf16)
+        for first, width, spare in spares:
+            cs = slice(first, first + width)
+            pad = jnp.zeros((WIDE - SIDE, width), f32)
+            for n in range(images):
+                for i in range(n * SIDE, (n + 1) * SIDE):
+                    cells = temp[i * SIDE : (i + 1) * SIDE, cs]
+                    if scaled:
+                        cells = cells * (n < limit).astype(f32)
+                    spare[i * WIDE : i * WIDE + SIDE, :] = cells
+                    spare[i * WIDE + SIDE : (i + 1) * WIDE, :] = pad
+            target[:, cs] = spare[...].astype(bf16)
 
     loop = lax.fori_loop
     hooks.tokens()
-    widen(nb_s, at_s, af_s, x_s, False)
+    widen(nb_s, [(t * 256, 256, gp_s.at[t]) for t in range(2)], x_s, False)
     loop(0, images, prepare, 0)
     hooks.weights()
     other_half = 1 - first_half
@@ -374,24 +375,38 @@
 
     loop(0, 2 * images, fore, 0)
     hooks.cotangent()
-    widen(lb_s, at_s, da_s, co_s, True)
+    widen(lb_s, [(0, D, da_s)], co_s, True)
     loop(0, images, finish, 0)
     hooks.arrived()
-    loop(0, images, feed, 0)
+
+    def feed_first(n, carry):
+        feed(0, n)
+        return carry
+
+    def feed_second(n, carry):
+        feed(1, n)
+        hooks.turn("f", n, images)
+        return carry
+
+    loop(0, images, feed_first, 0)
+    store_down(0)
+    hooks.point("D0")
+    store_up(0)
+    hooks.point("U0")
+    loop(0, images, feed_second, 0)
+    store_down(1)
+    hooks.point("D1")
+    store_up(1)
+    hooks.point("U1")
+    loop(0, images, digest, 0)
+    store_out()
+    hooks.point("O")
     narrow_rows(gin, af_s)
     hooks.output()
-    for u in range(2):
-        store_down(u)
-        hooks.point("D%d" % u)
-    for u in range(2):
-        store_up(u)
-        hooks.point("U%d" % u)
-    store_out()
-    hooks.point("O")
+    hooks.point("N")
 
     def aft(n, carry):
-        dn_s[padded(n), :] = recede(other_half, n)
-        hooks.back(n)
+        dn_s[padded(n), :] = recede(other_half, n, 2 * n)
         return carry
 
     loop(0, images, aft, 0)
@@ -400,8 +415,7 @@
         hooks.point("A%d" % part)
 
     def aft2(n, carry):
-        dn_s[padded(n), :] += recede(first_half, n)
-        hooks.back(images + n)
+        dn_s[padded(n), :] += recede(first_half, n, 2 * (images + n))
         return carry
 
     loop(0, images, aft2, 0)
@@ -413,6 +427,7 @@
     for t in range(2):
         gsmall[0:9, t * 256 : (t + 1) * 256] = gtaps[t, 0:9, :]
     hooks.finished()
+    hooks.point("R")
 
 
 class Quiet:
@@ -432,7 +447,10 @@
     def point(self, name):
         pass
 
-    back = fore = point
+    def turn(self, name, i, count):
+        pass
+
+    fore = point
 
     def weights(self):
         pass
@@ -501,41 +519,62 @@
     return pl.ds(pl.multiple_of(first, 16), size)
 
 
-def spread(part, transposed):
-    shape = (768, 256) if transposed else (256, 768)
-    narrow_side, wide_side = (1, 0) if transposed else (0, 1)
-    a = lax.broadcasted_iota(jnp.int32, shape, narrow_side)
-    b = lax.broadcasted_iota(jnp.int32, shape, wide_side)
+def spread_four(part):
+    a = lax.broadcasted_iota(jnp.int32, (384, 128), 1)
+    b = lax.broadcasted_iota(jnp.int32, (384, 128), 0)
     return jnp.where(b == (a // HD) * (3 * HD) + part * HD + lax.rem(a, HD), 1.0, 0.0).astype(bf16)
 
 
+def spread(part):
+    a = lax.broadcasted_iota(jnp.int32, (256, 768), 0)
+    b = lax.broadcasted_iota(jnp.int32, (256, 768), 1)
+    return jnp.where(b == (a // HD) * (3 * HD) + part * HD + lax.rem(a, HD), 1.0, 0.0).astype(bf16)
+
+
 def adam(w, m, v, g, rate, decay):
-    m = 0.5 * m + 0.5 * g
-    v = 0.5 * v + 0.5 * g * g
+    half = 0.5 * g
+    m = 0.5 * m + half
+    v = 0.5 * v + half * g
     scale = 1.0 / (1.0 - 0.5**STEP)
-    w = w - rate * ((m * scale) / (jnp.sqrt(v * scale) + 1e-08) + decay * w)
+    w = w - ((rate * scale) * m / (jnp.sqrt(v * scale) + 1e-08) + (rate * decay) * w)
     return w, m, v
 
 
+def adam_tile(w, m, v, g, rate, decay):
+    half = 0.5 * g
+    m = 0.5 * m + half
+    v = 0.5 * v + half * g
+    scale = 1.0 / (1.0 - 0.5**STEP)
+    seen = v * scale
+    below = seen * lax.rsqrt(seen) + 1e-08
+    inverse = pl.reciprocal(below, approx=True)
+    inverse = inverse * (2.0 - below * inverse)
+    w = w - ((rate * scale) * m * inverse + (rate * decay) * w)
+    return w, m, v
+
+
 MATRICES = (
-    (1024, 512, FF**-0.5, 4),
-    (512, 1024, D**-0.5, 4),
-    (256, 512, (D // HD) ** -0.5, 1),
-    (512, 768, D**-0.5, 2),
+    (1024, 512, FF**-0.5, 4, 64),
+    (512, 1024, D**-0.5, 4, 32),
+    (256, 512, (D // HD) ** -0.5, 1, 64),
+    (512, 768, D**-0.5, 4, 64),
 )
 
 
 def adam_kernel(*refs):
-    full, small_sum = refs[:2]
-    mats = refs[2:14]
-    smalls = refs[14:23]
-    outs = refs[23:39]
-    small_outs = refs[39:48]
-    bufs = refs[48:60]
-    lows = refs[60:64]
-    in_sem, out_sem = refs[64:]
+    full, small_sum, raw_out, raw_gin = refs[:4]
+    mats = refs[4:16]
+    smalls = refs[16:25]
+    outs = refs[25:41]
+    small_outs = refs[41:50]
+    out, gin = refs[50:52]
+    bufs = refs[52:64]
+    lows = refs[64:68]
+    g_vm, out_vm, gin_vm, in_sem, out_sem, more_sem = refs[68:]
+    g_load = pltpu.make_async_copy(full, g_vm, more_sem.at[2])
+    g_load.start()
     loads = {}
-    for i, (rows, cols, rate, pieces) in enumerate(MATRICES):
+    for i, (rows, cols, rate, pieces, tile) in enumerate(MATRICES):
         size = rows // pieces
         for p in range(pieces):
             rs = pl.ds(p * size, size)
@@ -545,41 +584,53 @@
                 )
                 go.start()
                 loads[i, p, j] = go
+    passing = [
+        pltpu.make_async_copy(raw_out, out_vm, more_sem.at[0]),
+        pltpu.make_async_copy(raw_gin, gin_vm, more_sem.at[1]),
+    ]
+    moves = [
+        pltpu.make_async_copy(out_vm, out, more_sem.at[3]),
+        pltpu.make_async_copy(gin_vm, gin, more_sem.at[4]),
+    ]
+    for go in passing:
+        go.start()
     stores = []
-    for i, (rows, cols, rate, pieces) in enumerate(MATRICES):
+    g_load.wait()
+    for i, (rows, cols, rate, pieces, tile) in enumerate(MATRICES):
         size = rows // pieces
         bw, bm, bv = bufs[3 * i : 3 * i + 3]
         low = lows[i]
+        spreads = [spread(part) for part in range(3)] if i == 3 else None
         for p in range(pieces):
             for j in range(3):
                 loads[i, p, j].wait()
 
-            def body(first, tile, i=i, p=p, bw=bw, bm=bm, bv=bv, low=low, rate=rate, size=size):
+            def body(first, tile, i=i, p=p, bw=bw, bm=bm, bv=bv, low=low, rate=rate, size=size, spreads=spreads):
                 rs = pl.ds(p * size + first, tile)
                 if i == 0:
                     g = [
-                        full[pl.ds(DOWN + (p // 2 * 2 + j) * 512 + p % 2 * size + first, tile), :]
+                        g_vm[pl.ds(DOWN + (p // 2 * 2 + j) * 512 + p % 2 * size + first, tile), :]
                         for j in range(2)
                     ]
                 elif i == 1:
-                    g = [full[pl.ds(UP + j * 512 + p * size + first, tile), :] for j in range(4)]
+                    g = [g_vm[pl.ds(UP + j * 512 + p * size + first, tile), :] for j in range(4)]
                 elif i == 2:
-                    g = [full[pl.ds(OUT + j * 256 + p * size + first, tile), :] for j in range(2)]
+                    g = [g_vm[pl.ds(OUT + j * 256 + p * size + first, tile), :] for j in range(2)]
                 else:
                     g = None
                     for part in range(3):
-                        own = full[pl.ds(IN + part * 512 + p * size + first, tile), :]
-                        term = nn(own, spread(part, False))
+                        own = g_vm[pl.ds(IN + part * 512 + p * size + first, tile), :]
+                        term = nn(own, spreads[part])
                         g = term if g is None else g + term
                 if i < 3:
                     g = jnp.concatenate(g, axis=1).astype(f32)
-                w, m, v = adam(bw[rs, :], bm[rs, :], bv[rs, :], g, rate, 0.05)
+                w, m, v = adam_tile(bw[rs, :], bm[rs, :], bv[rs, :], g, rate, 0.05)
                 bw[rs, :] = w
                 bm[rs, :] = m
                 bv[rs, :] = v
                 low[rs, :] = w.astype(bf16)
 
-            tile_loop(size, 32, body)
+            tile_loop(size, tile, body)
             rs = pl.ds(p * size, size)
             for j, src in enumerate((bw, bm, bv, low)):
                 go = pltpu.make_async_copy(
@@ -587,6 +638,10 @@
                 )
                 go.start()
                 stores.append(go)
+        if i == 0:
+            for come, go in zip(passing, moves):
+                come.wait()
+                go.start()
     x = lax.axis_index("tensor")
     mine = pl.ds(pl.multiple_of(x * 256, 256), 256)
     g_small = small_sum[:, mine]
@@ -606,14 +661,14 @@
         new = adam(w, smalls[3 * i + 1][...], smalls[3 * i + 2][...], g, rate, decay)
         for j in range(3):
             small_outs[3 * i + j][...] = new[j]
-    for go in stores:
+    for go in stores + moves:
         go.wait()
 
 
-def adam_step(full, small_sum, mats, smalls):
+def adam_step(full, small_sum, raw_out, raw_gin, mats, smalls):
     S = jax.ShapeDtypeStruct
     V = pltpu.VMEM
-    mat_shapes = [(rows, cols) for rows, cols, _, _ in MATRICES]
+    mat_shapes = [shape[:2] for shape in MATRICES]
     any_spec = pl.BlockSpec(memory_space=pl.ANY)
     vmem_spec = pl.BlockSpec(memory_space=V)
     small_shapes = [(9, 256)] * 3 + [(1, 1024)] * 3 + [(7, 256)] * 3
@@ -622,60 +677,77 @@
         out_shape=tuple(
             S(shape, kind) for shape in mat_shapes for kind in (f32, f32, f32, bf16)
         )
-        + tuple(S(shape, f32) for shape in small_shapes),
-        in_specs=[vmem_spec] * 2 + [any_spec] * 12 + [vmem_spec] * 9,
-        out_specs=[any_spec] * 16 + [vmem_spec] * 9,
+        + tuple(S(shape, f32) for shape in small_shapes)
+        + (S(raw_out.shape, bf16), S(raw_gin.shape, f32)),
+        in_specs=[any_spec, vmem_spec, any_spec, any_spec] + [any_spec] * 12 + [vmem_spec] * 9,
+        out_specs=[any_spec] * 16 + [vmem_spec] * 9 + [any_spec] * 2,
         scratch_shapes=[V(shape, f32) for shape in mat_shapes for _ in range(3)]
         + [V(shape, bf16) for shape in mat_shapes]
-        + [pltpu.SemaphoreType.DMA((4, 4, 3)), pltpu.SemaphoreType.DMA((4, 4, 4))],
-        compiler_params=pltpu.CompilerParams(vmem_limit_bytes=48 * 1024 * 1024),
-    )(full, small_sum, *mats, *smalls)
+        + [
+            V((GROWS, 256), bf16),
+            V(raw_out.shape, bf16),
+            V(raw_gin.shape, f32),
+            pltpu.SemaphoreType.DMA((4, 4, 3)),
+            pltpu.SemaphoreType.DMA((4, 4, 4)),
+            pltpu.SemaphoreType.DMA((5,)),
+        ],
+        compiler_params=pltpu.CompilerParams(vmem_limit_bytes=62 * 1024 * 1024),
+    )(full, small_sum, raw_out, raw_gin, *mats, *smalls)
 
 
 CHUNKS = (
-    (DOWN, 1024), (DOWN + 1024, 1024), (UP, 1024), (UP + 1024, 1024), (OUT, 512),
-    (IN + 1024, 512), (IN + 512, 512), (IN, 512),
+    (0, 1024),
+    (2048, 1024),
+    (1024, 1024),
+    (3072, 1024),
+    (4096, 512),
+    (5632, 512),
+    (5120, 512),
+    (4608, 512),
 )
-D0, D1, U0, U1, O0, V0, K0, G0 = range(8)
+LATE = 5
 SLOTS = 12
 PLAN = {
-    "D0": ((D0, 0),),
-    "D1": ((D1, 0), (D0, 1)),
-    "U0": ((U0, 0), (D1, 1)),
-    "U1": ((U1, 0), (U0, 1)),
-    "O": ((O0, 0), (U1, 1)),
-    0: ((O0, 1),),
-    1: ((D0, 2),),
-    2: (),
-    3: ((D0, 3),),
-    "A2": ((V0, 0),),
-    "A1": ((K0, 0), (V0, 1)),
-    "A0": ((G0, 0), (K0, 1)),
-    4: ((G0, 1), (D1, 2), (D0, 4)),
-    5: (),
-    6: ((D0, 5), (D1, 3)),
-    7: ((U0, 2), (D0, 6), (D1, 4)),
-    "B2": ((V0, 2),),
-    "B1": ((K0, 2),),
-    "B0": ((G0, 2),),
+    'D0': ((0, 0),),
+    'U0': ((1, 0),),
+    'f0': ((0, 1),),
+    'f1': ((1, 1),),
+    'D1': ((2, 0),),
+    'U1': ((3, 0),),
+    'd0': ((2, 1), (3, 1), (0, 2),),
+    'd3': ((1, 2), (0, 3),),
+    'O': ((4, 0),),
+    'r0': ((4, 1),),
+    'r1': ((1, 3), (2, 2),),
+    'r2': ((0, 4),),
+    'r5': ((2, 3), (1, 4), (3, 2),),
+    'r7': ((0, 5), (4, 2),),
+    'A2': ((5, 0),),
+    'A1': ((6, 0), (3, 3), (5, 1), (2, 4), (6, 1),),
+    'A0': ((7, 0),),
+    'r8': ((7, 1), (0, 6),),
+    'r9': ((4, 3), (1, 5), (0, 7),),
+    'r10': ((3, 4),),
+    'r13': ((2, 5), (1, 6), (4, 4),),
+    'r14': ((1, 7),),
+    'B2': ((5, 2), (3, 5),),
+    'B1': ((6, 2), (5, 3), (4, 5), (2, 6),),
+    'B0': ((7, 2), (6, 3),),
+    'R': ((7, 3), (3, 6), (2, 7),),
 }
 TAIL = (
-    ((D0, 7), (D1, 5), (U0, 3), (U1, 2)),
-    ((D1, 6), (U0, 4), (U1, 3), (O0, 2)),
-    ((D1, 7), (U0, 5), (U1, 4), (O0, 3), (V0, 3)),
-    ((U0, 6), (U1, 5), (O0, 4), (V0, 4), (K0, 3)),
-    ((U0, 7), (U1, 6), (O0, 5), (V0, 5), (K0, 4), (G0, 3)),
-    ((U1, 7), (O0, 6), (V0, 6), (K0, 5), (G0, 4)),
-    ((O0, 7), (V0, 7), (K0, 6), (G0, 5)),
-    ((V0, 8), (K0, 7), (G0, 6)),
-    ((K0, 8), (G0, 7)),
-    ((G0, 8),),
+    (3, 7), (5, 4), (4, 6), (4, 7), (6, 4), (5, 5),
+    (7, 4), (6, 5), (5, 6), (7, 5), (6, 6), (5, 7),
+    (5, 8), (7, 6), (6, 7), (6, 8), (7, 7), (7, 8),
 )
+
+
+ITEMS = ((0, 0, 64), (0, 64, 64), (1, 0, 64), (2, 0, 64), (2, 64, 64), (3, 0, 128), (3, 128, 128))
 
 
 class Traffic:
     def __init__(self, images, refs):
-        (self.tok, self.cot, self.w_in, self.w_out, self.w_up, self.w_down, self.own_small,
+        (self.tok, self.cot, self.w_in, self.w_out, self.w_up, self.w_down, self.taps, self.bias,
          self.out, self.gin, self.full, self.small_sum,
          self.gin_v, self.grads, self.gsmall, self.wi, self.wo, self.wu, self.wd, self.small,
          self.at_s, self.af_s, self.da_s, self.gp_s, self.mf_s, self.nb_s, self.lb_s, self.out_v,
@@ -695,23 +767,42 @@
         self.y_mate = at(z, 1 - y, core, x)
         self.z_others = [lax.rem(z + k, 4) for k in range(1, 4)]
         self.z_mates = [at(o, y, core, x) for o in self.z_others]
-        self.loads = [
-            pltpu.make_async_copy(src, dst, self.load.at[i])
-            for i, (src, dst) in enumerate(
-                (
-                    (self.w_in.at[:, 0:256], self.mf_s.at[0, 0:512, :]),
-                    (self.w_in.at[:, 256:512], self.mf_s.at[1, 0:512, :]),
-                    (self.w_in.at[:, 512:768], self.gp_s.at[0, 0:512, :]),
-                    (self.w_out, self.da_s.at[512:768, :]),
-                    (self.w_up.at[:, 0:512], self.da_s.at[0:512, :]),
-                    (self.w_up.at[:, 512:1024], self.af_s.at[0:512, :]),
-                    (self.w_down.at[0:512, :], self.gin_v.at[0:512, :]),
-                    (self.w_down.at[512:896, :], self.af_s.at[512:896, :]),
-                    (self.w_down.at[896:1024, :], self.da_s.at[768:896, :]),
-                    (self.tok, self.nb_s.at[0 : images * WIN, :]),
-                    (self.cot, self.lb_s.at[0 : images * WIN, :]),
-                )
-            )
+        quarter = y * 2 + core
+        self.quarter = quarter
+
+        def load(i, src, dst):
+            return pltpu.make_async_copy(src, dst, self.load.at[i])
+
+        w_in, w_out, w_up, w_down = self.w_in, self.w_out, self.w_up, self.w_down
+        at_s, af_s, da_s, mf_s, gin = self.at_s, self.af_s, self.da_s, self.mf_s, self.gin_v
+        q_in, q_out = aligned(quarter * 128, 128), aligned(quarter * 64, 64)
+        q_down = aligned(quarter * 256, 256)
+        self.early = [
+            load(0, w_in.at[q_in, 0:256], at_s.at[0:128, 0:256]),
+            load(1, w_in.at[q_in, 256:512], at_s.at[0:128, 256:512]),
+            load(2, w_in.at[q_in, 512:768], at_s.at[128:256, 0:256]),
+            load(3, w_out.at[q_out, :], at_s.at[256:320, :]),
+            load(4, w_up.at[q_in, 0:512], at_s.at[320:448, :]),
+            load(5, w_up.at[q_in, 512:1024], at_s.at[448:576, :]),
+            load(6, w_down.at[q_down, :], at_s.at[576:832, :]),
+        ]
+        self.own_in = [
+            load(7, w_in.at[:, 0:256], mf_s.at[0, 0:512, :]),
+            load(8, w_in.at[:, 256:512], mf_s.at[1, 0:512, :]),
+            load(9, w_in.at[:, 512:768], gin.at[0:512, 0:256]),
+        ]
+        self.tok_load = load(10, self.tok, self.nb_s.at[0 : images * WIN, :])
+        self.cot_load = load(11, self.cot, self.lb_s.at[0 : images * WIN, :])
+        self.own_rest = [
+            load(12, w_out.at[:, 0:256], gin.at[0:256, 256:512]),
+            load(13, w_out.at[:, 256:512], gin.at[256:512, 256:512]),
+            load(14, w_up.at[:, 0:512], da_s.at[0:512, :]),
+            load(15, w_up.at[:, 512:1024], af_s.at[0:512, :]),
+            load(16, w_down.at[0:256, :], da_s.at[512:768, :]),
+            load(17, w_down.at[256:512, :], af_s.at[512:768, :]),
+            load(18, w_down.at[512:768, :], gin.at[512:768, :]),
+            load(19, w_down.at[768:896, :], da_s.at[768:896, :]),
+            load(20, w_down.at[896:1024, :], af_s.at[768:896, :]),
         ]
 
 
@@ -726,14 +817,15 @@
         )
 
     def view(self, item, half, yy, cc):
+        kind, first, size = ITEMS[item]
         quarter = yy * 2 + cc
-        if item == 0:
-            return self.wi.at[half, :, aligned(quarter * 128, 128), :]
-        ref, size = ((self.wo, 64), (self.wu, 128), (self.wd, 256))[item - 1]
-        return ref.at[half, aligned(quarter * size, size), :]
+        if kind == 0:
+            return self.wi.at[half, :, aligned(quarter * 128 + first, size), :]
+        ref, rows = ((self.wo, 64), (self.wu, 128), (self.wd, 256))[kind - 1]
+        return ref.at[half, aligned(quarter * rows + first, size), :]
 
     def crossing(self, item):
-        if item == 4:
+        if item == len(ITEMS):
             own = self.small.at[self.x]
         else:
             own = self.view(item, self.x, self.y, self.core)
@@ -751,107 +843,137 @@
         got = self.view(item, 1 - self.x, 1 - self.y, self.core)
         return self.weight_copy(got, got, item, 3, self.core_mate)
 
-    def cast(self, rows, size, source, target):
-        def body(first, tile):
-            here = pl.ds(first, tile)
-            target[here, :] = source[here, :].astype(bf16)
-
-        tile_loop(rows, size, body)
+    def permuted(self, pieces, rows):
+        low = jnp.concatenate(pieces, axis=1).astype(bf16)
+        for part in range(3):
+            for j in range(2):
+                four = nn(low[:, j * 384 : (j + 1) * 384], spread_four(part))
+                self.wi[self.x, part, rows, j * 128 : (j + 1) * 128] = four.astype(bf16)
 
     def begin(self):
-        for go in self.loads:
+        for go in self.early:
             go.start()
         barrier = pltpu.get_barrier_semaphore()
         for mate in (self.core_mate, self.x_mate, self.y_mate, *self.z_mates):
             pl.semaphore_signal(barrier, inc=1, device_id=mate, device_id_type=MESH)
-        x = self.x
-        self.small[x] = self.own_small[...]
-        for go in self.loads[0:3]:
+        for go in self.own_in:
+            go.start()
+        self.tok_load.start()
+        x, quarter, at_s = self.x, self.quarter, self.at_s
+        self.small[x, 0:9, :] = self.taps[...]
+        for j in range(4):
+            self.small[x, 9 + j : 10 + j, :] = self.bias[:, j * 256 : (j + 1) * 256]
+        for go in self.early[0:3]:
             go.wait()
-        spreads = [spread(part, True) for part in range(3)]
-
-        def body(first, tile):
-            rows = pl.ds(first, tile)
-            low = jnp.concatenate(
-                [self.mf_s[0, rows, :], self.mf_s[1, rows, :], self.gp_s[0, rows, :]], axis=1
-            ).astype(bf16)
-            for part in range(3):
-                self.wi[x, part, rows, :] = nn(low, spreads[part]).astype(bf16)
-
-        tile_loop(512, 128, body)
+        self.permuted(
+            [at_s[0:128, 0:256], at_s[0:128, 256:512], at_s[128:256, 0:256]],
+            aligned(quarter * 128, 128),
+        )
         pl.semaphore_wait(barrier, 6)
         self.crossing(0).start()
+        self.crossing(1).start()
+        self.crossing(len(ITEMS)).start()
+        self.early[3].wait()
+        self.wo[x, aligned(quarter * 64, 64), :] = at_s[256:320, :].astype(bf16)
+        self.crossing(2).start()
+        for go in self.early[4:6]:
+            go.wait()
+        rows = aligned(quarter * 128, 128)
+        self.wu[x, rows, 0:512] = at_s[320:448, :].astype(bf16)
+        self.wu[x, rows, 512:1024] = at_s[448:576, :].astype(bf16)
+        self.crossing(3).start()
         self.crossing(4).start()
-        for go in self.loads[3:9]:
+        self.early[6].wait()
+        self.wd[x, aligned(quarter * 256, 256), :] = at_s[576:832, :].astype(bf16)
+        self.crossing(5).start()
+        self.crossing(6).start()
+        self.cot_load.start()
+        for go in self.own_rest:
+            go.start()
+
+    def tokens(self):
+        self.tok_load.wait()
+
+    def others(self, body):
+        for j in range(4):
+
+            @pl.when(self.quarter != j)
+            def _(j=j):
+                body(j)
+
+    def weights(self):
+        for go in self.own_in:
             go.wait()
-        self.cast(256, 64, self.da_s.at[512:768, :], self.wo.at[x])
-        self.crossing(1).start()
-        self.cast(512, 64, self.da_s.at[0:512, :], self.wu.at[x, :, 0:512])
-        self.cast(512, 64, self.af_s.at[0:512, :], self.wu.at[x, :, 512:1024])
-        self.crossing(2).start()
-        self.cast(512, 64, self.gin_v.at[0:512, :], self.wd.at[x, 0:512, :])
-        self.cast(384, 64, self.af_s.at[512:896, :], self.wd.at[x, 512:896, :])
-        self.cast(128, 64, self.da_s.at[768:896, :], self.wd.at[x, 896:1024, :])
-        self.crossing(3).start()
-
-    def tokens(self):
-        self.loads[9].wait()
-
-    def weights(self):
-        pass
-
-    def fore(self, i):
-        def passed(item):
+        mf_s, gin = self.mf_s, self.gin_v
+
+        def body(j):
+            rows = slice(j * 128, (j + 1) * 128)
+            self.permuted([mf_s[0, rows, :], mf_s[1, rows, :], gin[rows, 0:256]], rows)
+
+        self.others(body)
+
+    def passed(self, *items):
+        for item in items:
             self.crossing(item).wait()
             self.inward(item).start()
             self.aside(item).start()
 
-        def turned(item):
+    def turned(self, *items):
+        for item in items:
             self.aside(item).wait()
             self.onward(item).start()
 
-        def done(item):
+    def done(self, *items):
+        for item in items:
             self.inward(item).wait()
             self.onward(item).wait()
 
+    def fore(self, i):
         last = self.images - 1
-
-        @pl.when(i == 1)
-        def _():
-            passed(0)
-
-        @pl.when(i == 2)
-        def _():
-            passed(1)
-
-        @pl.when(i == last)
-        def _():
-            turned(0)
-            self.crossing(4).wait()
-            done(0)
-
-        @pl.when(i == last + 1)
-        def _():
-            passed(2)
-            turned(1)
-
-        @pl.when(i == last + 3)
-        def _():
-            passed(3)
-            turned(2)
-
-        @pl.when(i == last + 4)
-        def _():
-            turned(3)
-            done(1)
+        for k, steps in {
+            0: (("passed", 0), ("passed", 1)),
+            1: (("turned", 0), ("passed", 2)),
+            2: (("turned", 1),),
+            last: (("done", 0), ("done", 1), ("passed", 3)),
+            last + 1: (("turned", 2), ("passed", 4)),
+            last + 2: (("turned", 3),),
+            last + 3: (("passed", 5),),
+            last + 4: (("turned", 4), ("passed", 6)),
+        }.items():
+
+            @pl.when(i == k)
+            def _(k=k, steps=steps):
+                for name, item in steps:
+                    {"passed": self.passed, "turned": self.turned, "done": self.done}[name](item)
+                if k == last:
+                    self.crossing(len(ITEMS)).wait()
 
     def cotangent(self):
-        self.loads[10].wait()
+        self.done(2)
+        for go in self.own_rest:
+            go.wait()
+        x, gin, da_s, af_s = self.x, self.gin_v, self.da_s, self.af_s
+
+        def body(j):
+            rows = slice(j * 64, (j + 1) * 64)
+            self.wo[x, rows, 0:256] = gin[rows, 256:512].astype(bf16)
+            self.wo[x, rows, 256:512] = gin[j * 64 + 256 : (j + 1) * 64 + 256, 256:512].astype(bf16)
+            rows = slice(j * 128, (j + 1) * 128)
+            self.wu[x, rows, 0:512] = da_s[rows, :].astype(bf16)
+            self.wu[x, rows, 512:1024] = af_s[rows, :].astype(bf16)
+            rows = slice(j * 256, (j + 1) * 256)
+            if j < 3:
+                self.wd[x, rows, :] = (da_s, af_s, gin)[j][512:768, :].astype(bf16)
+            else:
+                self.wd[x, 768:896, :] = da_s[768:896, :].astype(bf16)
+                self.wd[x, 896:1024, :] = af_s[768:896, :].astype(bf16)
+
+        self.others(body)
+        self.cot_load.wait()
 
     def arrived(self):
-        for item in (2, 3):
-            self.inward(item).wait()
-            self.onward(item).wait()
+        self.turned(5, 6)
+        self.done(3, 4, 5, 6)
 
 
     def output(self):
@@ -886,12 +1008,12 @@
         x, y, z, core, grads = self.x, self.y, self.z, self.core, self.grads
         mine = base + core * half
         theirs = aligned(base + (1 - core) * half, half)
-        if c >= V0:
+        if c >= LATE:
             if s == 0:
                 src = grads.at[1 - x, theirs, :]
-                return [self.copy(src, self.firsts[c - V0], c, 11, self.core_mate)]
+                return [self.copy(src, self.firsts[c - LATE], c, 11, self.core_mate)]
             if s == 1:
-                return [self.copy(self.firsts[c - V0], self.xs[c], c, 1, self.x_mate)]
+                return [self.copy(self.firsts[c - LATE], self.xs[c], c, 1, self.x_mate)]
             if s == 2:
                 return [self.copy(grads.at[x, theirs, :], self.cores[c], c, 0, self.core_mate)]
             s -= 1
@@ -930,14 +1052,14 @@
         half, quarter, piece = R // 2, R // 4, R // 16
         x, y, z, core, grads = self.x, self.y, self.z, self.core, self.grads
         mine = base + core * half
-        late = c >= V0
+        late = c >= LATE
         if s > 0 and not (late and s == 2):
             for flight in self.flights(c, s - 1):
                 flight.wait()
         if late and s == 3:
             self.flights(c, 1)[0].wait()
 
-        def total(target, *parts):
+        def total(*parts):
             out = None
             for part in parts:
                 part = part.astype(f32)
@@ -947,18 +1069,18 @@
         cores, xs, ys, zs = self.cores[c], self.xs[c], self.ys[c], self.zs[c]
         step = s - 1 if late else s
         if late and s == 1:
-            first = self.firsts[c - V0]
+            first = self.firsts[c - LATE]
 
             def body(i, size):
                 rows, own = pl.ds(i, size), aligned(mine + i, size)
-                first[rows, :] = total(None, grads[1 - x, own, :], first[rows, :])
+                first[rows, :] = total(grads[1 - x, own, :], first[rows, :])
 
             tile_loop(half, 128, body)
         elif late and s == 3:
 
             def body(i, size):
                 rows, own = pl.ds(i, size), aligned(mine + i, size)
-                xs[rows, :] = total(None, grads[x, own, :], cores[rows, :], xs[rows, :])
+                xs[rows, :] = total(grads[x, own, :], cores[rows, :], xs[rows, :])
 
             tile_loop(half, 128, body)
         elif not late and s == 1:
@@ -966,27 +1088,27 @@
             def body(i, size):
                 rows, own = pl.ds(i, size), aligned(mine + i, size)
                 for t in range(2):
-                    cores[t, rows, :] = total(None, grads[t, own, :], cores[t, rows, :])
+                    cores[t, rows, :] = total(grads[t, own, :], cores[t, rows, :])
 
             tile_loop(half, 128, body)
         elif not late and s == 2:
 
             def body(i, size):
                 rows = pl.ds(i, size)
-                xs[rows, :] = total(None, cores[x, rows, :], xs[rows, :])
+                xs[rows, :] = total(cores[x, rows, :], xs[rows, :])
 
             tile_loop(half, 128, body)
         elif step == 3:
 
             def body(i, size):
                 rows, own = pl.ds(i, size), aligned(y * quarter + i, size)
-                ys[rows, :] = total(None, xs[own, :], ys[rows, :])
+                ys[rows, :] = total(xs[own, :], ys[rows, :])
 
             tile_loop(quarter, 128, body)
         elif step == 4:
             own = aligned(z * piece, piece)
             grads[0, aligned(mine + y * quarter + z * piece, piece), :] = total(
-                None, ys[own, :], zs[0], zs[1], zs[2]
+                ys[own, :], zs[0], zs[1], zs[2]
             )
         for flight in self.flights(c, s):
             flight.start()
@@ -1028,44 +1150,46 @@
             flight.start()
 
     def point(self, name):
-        for c, s in PLAN[name]:
+        for c, s in PLAN.get(name, ()):
             self.stage(c, s)
 
-    def back(self, i):
-        for k in range(2 * self.images):
-            if PLAN[k]:
+    def turn(self, name, i, count):
+        for k in range(count):
+            if name + str(k) in PLAN:
 
                 @pl.when(i == k)
                 def _(k=k):
-                    self.point(k)
+                    self.point(name + str(k))
 
     def end(self):
         self.small_stage(0)
-        for k, wave in enumerate(TAIL):
-            for c, s in wave:
-                self.stage(c, s)
-            if k < 4:
-                self.small_stage(k + 1)
+        gap = len(TAIL) // 6
+        for k, (c, s) in enumerate(TAIL):
+            self.stage(c, s)
+            if k % gap == gap - 1 and k // gap < 4:
+                self.small_stage(k // gap + 1)
         self.saving(2).start()
         for i in range(3):
             self.saving(i).wait()
 
 
-def main_kernel(images, counts, tok, cot, w_in, w_out, w_up, w_down, own_small, vecs,
+def main_kernel(images, counts, tok, cot, w_in, w_out, w_up, w_down, taps, bias, vecs,
                 out, gin, full, small_sum, *scratch):
     n = len(block_scratch(images))
     inner, rest = scratch[:n], scratch[n:]
     gin_v, grads, gsmall, wi, wo, wu, wd, small = rest[:8]
     rest = rest[8:]
-    cores, xs, ys, zs = (rest[8 * i : 8 * i + 8] for i in range(4))
-    firsts = rest[32:35]
+    count = len(CHUNKS)
+    cores, xs, ys, zs = (rest[count * i : count * (i + 1)] for i in range(4))
+    rest = rest[4 * count :]
+    firsts, rest = rest[: count - LATE], rest[count - LATE :]
     x_s, co_s, at_s, af_s, da_s, gp_s, mf_s, na_s, nb_s, lb_s = inner[:10]
     traffic = Traffic(
         images,
-        (tok, cot, w_in, w_out, w_up, w_down, own_small, out, gin, full, small_sum,
+        (tok, cot, w_in, w_out, w_up, w_down, taps, bias, out, gin, full, small_sum,
          gin_v, grads, gsmall, wi, wo, wu, wd, small,
          at_s, af_s, da_s, gp_s, mf_s, nb_s, lb_s, co_s.at[0 : images * WIN, :],
-         cores, xs, ys, zs, firsts, *rest[35:]),
+         cores, xs, ys, zs, firsts, *rest),
     )
     x = lax.axis_index("tensor")
     limit = counts[lax.axis_index("dp")] - x * images
@@ -1076,7 +1200,7 @@
     traffic.end()
 
 
-def main_call(counts, tok, cot, w_in, w_out, w_up, w_down, own_small, vecs):
+def main_call(counts, tok, cot, w_in, w_out, w_up, w_down, taps, bias, vecs):
     images = tok.shape[0] // WIN
     S = jax.ShapeDtypeStruct
     V = pltpu.VMEM
@@ -1092,7 +1216,7 @@
             S((GROWS, 256), bf16),
             S((24, D), f32),
         ),
-        in_specs=[pl.BlockSpec(memory_space=pltpu.SMEM)] + [away] * 6 + [here] * 2,
+        in_specs=[pl.BlockSpec(memory_space=pltpu.SMEM)] + [away] * 6 + [here] * 3,
         out_specs=[away] * 3 + [here],
         scratch_shapes=block_scratch(images)
         + [
@@ -1105,28 +1229,28 @@
             V((2, 1024, D), bf16),
             V((2, 16, 256), f32),
         ]
-        + [V((2, R // 2, 256), bf16) for R in sizes[:5]]
-        + [V((R // 2, 256), bf16) for R in sizes[5:]]
+        + [V((2, R // 2, 256), bf16) for R in sizes[:LATE]]
+        + [V((R // 2, 256), bf16) for R in sizes[LATE:]]
         + [V((R // 2, 256), bf16) for R in sizes]
         + [V((R // 4, 256), bf16) for R in sizes]
         + [V((3, R // 16, 256), bf16) for R in sizes]
-        + [V((R // 2, 256), bf16) for R in sizes[5:]]
+        + [V((R // 2, 256), bf16) for R in sizes[LATE:]]
         + [
             V((3, 24, D), f32),
             V((8, 24, D), f32),
-            dma((8, SLOTS)),
-            dma((8, SLOTS)),
+            dma((len(sizes), SLOTS)),
+            dma((len(sizes), SLOTS)),
             dma((6,)),
             dma((6,)),
-            dma((5, 4)),
-            dma((5, 4)),
-            dma((11,)),
+            dma((8, 4)),
+            dma((8, 4)),
+            dma((21,)),
             dma((3,)),
         ],
         compiler_params=pltpu.CompilerParams(
             collective_id=1, has_side_effects=True, vmem_limit_bytes=63 * 1024 * 1024
         ),
-    )(counts, tok, cot, w_in, w_out, w_up, w_down, own_small, vecs)
+    )(counts, tok, cot, w_in, w_out, w_up, w_down, taps, bias, vecs)
 
 
 def local(
@@ -1134,23 +1258,23 @@
     w_in, m_in, v_in, w_out, m_out, v_out, w_up, m_up, v_up, w_down, m_down, v_down,
     kernel, m_kernel, v_kernel, up_bias, m_bias, v_bias, vectors, m_vectors, v_vectors,
 ):
-    own_small = jnp.concatenate(
-        [kernel, up_bias.reshape(4, 256), jnp.zeros((3, 256), f32)], axis=0
-    )
-    out, grad_in, full, small_sum = main_call(
-        image_counts, tokens, cotangent, w_in, w_out, w_up, w_down, own_small, vectors
+    biases = tuple(a.reshape(1, -1) for a in (up_bias, m_bias, v_bias))
+    raw_out, raw_gin, full, small_sum = main_call(
+        image_counts, tokens, cotangent, w_in, w_out, w_up, w_down, kernel, biases[0], vectors
     )
     new = adam_step(
         full,
         small_sum,
+        raw_out,
+        raw_gin,
         (w_down, m_down, v_down, w_up, m_up, v_up, w_out, m_out, v_out, w_in, m_in, v_in),
         (kernel, m_kernel, v_kernel)
-        + tuple(a.reshape(1, -1) for a in (up_bias, m_bias, v_bias))
+        + biases
         + (vectors, m_vectors, v_vectors),
     )
     down, up, mid, first = new[:4], new[4:8], new[8:12], new[12:16]
     bias = tuple(a.reshape(-1) for a in new[19:22])
-    return (out, grad_in, *first, *mid, *up, *down, *new[16:19], *bias, *new[22:25])
+    return (*new[25:27], *first, *mid, *up, *down, *new[16:19], *bias, *new[22:25])
 
 
 def general(

time: 169 us -> 137 us (0.81)
  Pallas kernels: 157 us -> 136 us
  local copies, waits for them, and re-layouts: 9.36 us -> 0 us
    pallas_call x1, Pallas kernels: 136 us -> 118 us  [main_call(): pl.pallas_call(functools.partial(main_kernel, images), out_shape=(S(tok.s...]
    unnamed x36 -> x0, local copies, waits for them, and re-layouts: 8.59 us -> none
    pallas_call x1, Pallas kernels: 21.7 us -> 18.3 us  [adam_step(): pl.pallas_call(adam_kernel, out_shape=tuple((S(shape, kind) for shape in...]
where the time goes in v3:
time: 137 us
  Pallas kernels  136 us (99%)
    pallas_call x1, Pallas kernels, main_call(): pl.pallas_call(functools.partial(main_kernel, images), out_shape=(S(tok.s...  118 us
    pallas_call x1, Pallas kernels, adam_step(): pl.pallas_call(adam_kernel, out_shape=tuple((S(shape, kind) for shape in...  18.3 us

profile of v3, /device:TPU:0, one launch (start us, length us, event | category | flops | bytes accessed | tf_op | source)
XLA Modules:
  0.0 137.0 jit_solution(4786650031498737113)
XLA Ops:
  0.7 117.8 %shard_map.439 = (bf16[784,512]{1,0:T(8,128)(2,1)}, f32[784,512]{1,0:T(8,128)}, bf16[6144,256]{1,0:T(8,128)(2,1)}, f32[24,512]{1,0:T(8,128)}) custom-call(s32[16]{0:T(128)} %counts.1, bf16[784,512]{1,0:T(8,128)(2,1)} %tok.1, bf16[784,512]{1,0:T(8,128)(2,1)} %cot.1, f32[512,768]{1,0:T(8,128)} %refs_13_.1, f32[256,512]{1,0:T(8,128)} %refs_10_.1, ...), custom_call_target="tpu_custom_call" | custom-call | tf_op jit(solution)/shard_map/pallas_call | solution.py:1211
  118.5 18.3 %shard_map.440 = (f32[1024,512]{1,0:T(8,128)}, f32[1024,512]{1,0:T(8,128)}, f32[1024,512]{1,0:T(8,128)}, bf16[1024,512]{1,0:T(8,128)(2,1)}, f32[512,1024]{1,0:T(...) custom-call(bf16[6144,256]{1,0:T(8,128)(2,1)} %get-tuple-element.58., ...), custom_call_target="tpu_custom_call" | custom-call | tf_op jit(solution)/shard_map/pallas_call | solution.py:675

commit v4 on v3

--- a/solution.py
+++ b/solution.py
@@ -91,7 +91,6 @@
         vecs[i : i + 1, :] for i in range(7)
     )
     gsmall[...] = jnp.zeros_like(gsmall)
-    dn_s = at_s
     gtaps = taps_s
     gtaps[...] = jnp.zeros_like(gtaps)
     blank = jnp.zeros((KEYS - ROWS, 256), bf16)
@@ -187,22 +186,18 @@
         lb_s[rows, :] = (scale_f * co_s[rows, :].astype(f32)).astype(bf16)
         return carry
 
-    def feed(u, n):
+    def feed(t, u, n):
         rows = padded(n)
-        lb = lb_s[rows, :]
-        nb = nb_s[rows, :]
         us = slice(u * 512, (u + 1) * 512)
-        for t in range(2):
-            c = 2 * t + u
-            cs = slice(c * 512, (c + 1) * 512)
-            unit_bias = jnp.concatenate(
-                [small[t, 9 + 2 * u + j : 10 + 2 * u + j, :] for j in range(2)], axis=1
-            )
-            value, slope = gelu_pair(nn(nb, wu[t, :, us]) + unit_bias)
-            hd_s[rows, cs] = value.astype(bf16)
-            d_pre = slope * nt(lb, wd[t, us, :])
-            gsmall[16 + c : 17 + c, :] += row_sum(d_pre)
-            dp_s[rows, cs] = d_pre.astype(bf16)
+        cs = pl.ds(pl.multiple_of(t * 1024 + u * 512, 512), 512)
+        unit_bias = jnp.concatenate(
+            [small[t, 9 + 2 * u + j : 10 + 2 * u + j, :] for j in range(2)], axis=1
+        )
+        value, slope = gelu_pair(nn(nb_s[rows, :], wu[t, :, us]) + unit_bias)
+        hd_s[rows, cs] = value.astype(bf16)
+        d_pre = slope * nt(lb_s[rows, :], wd[t, us, :])
+        gsmall[pl.ds(16 + 2 * t + u, 1), :] += row_sum(d_pre)
+        dp_s[rows, cs] = d_pre.astype(bf16)
 
     def digest(n, carry):
         rows = padded(n)
@@ -299,19 +294,19 @@
             d_field = roll1(d_cols[0], -1) + d_cols[1] + roll1(d_cols[2], 1)
             pj_s[t, 0, rows, ls] = jnp.where(inside, slope * d_field, 0.0).astype(bf16)
             hooks.turn("r", turn + g, 4 * images)
-        d_na = None
-        for part in range(3):
-            term = nt(pj_s[t, part, rows, :], wi[t, part])
-            d_na = term if d_na is None else d_na + term
-        return d_na
 
     def rise(n, carry):
         rows = padded(n)
-        d_na = dn_s[rows, :]
+        d_na = None
+        for t in range(2):
+            for part in range(3):
+                term = nt(pj_s[t, part, rows, :], wi[t, part])
+                d_na = term if d_na is None else d_na + term
         xhat, r = normed(x_s[rows, :].astype(f32))
         gsmall[9:10, :] += row_sum(d_na * xhat)
         gsmall[10:11, :] += row_sum(d_na)
         da_s[rows, :] += norm_back(gain_a * d_na, xhat, r)
+        hooks.turn("s", n, images)
         return carry
 
     def narrow_rows(target, source):
@@ -377,17 +372,24 @@
     hooks.cotangent()
     widen(lb_s, [(0, D, da_s)], co_s, True)
     loop(0, images, finish, 0)
-    hooks.arrived()
+    hooks.near()
+
+    def feed_own(n, carry):
+        for u in range(2):
+            feed(first_half, u, n)
+        return carry
 
     def feed_first(n, carry):
-        feed(0, n)
+        feed(other_half, 0, n)
         return carry
 
     def feed_second(n, carry):
-        feed(1, n)
+        feed(other_half, 1, n)
         hooks.turn("f", n, images)
         return carry
 
+    loop(0, images, feed_own, 0)
+    hooks.arrived()
     loop(0, images, feed_first, 0)
     store_down(0)
     hooks.point("D0")
@@ -401,12 +403,9 @@
     loop(0, images, digest, 0)
     store_out()
     hooks.point("O")
-    narrow_rows(gin, af_s)
-    hooks.output()
-    hooks.point("N")
 
     def aft(n, carry):
-        dn_s[padded(n), :] = recede(other_half, n, 2 * n)
+        recede(other_half, n, 2 * n)
         return carry
 
     loop(0, images, aft, 0)
@@ -415,7 +414,7 @@
         hooks.point("A%d" % part)
 
     def aft2(n, carry):
-        dn_s[padded(n), :] += recede(first_half, n, 2 * (images + n))
+        recede(first_half, n, 2 * (images + n))
         return carry
 
     loop(0, images, aft2, 0)
@@ -423,9 +422,14 @@
         store_in(first_half, part)
         hooks.point("B%d" % part)
     loop(0, images, rise, 0)
-    narrow_rows(gin, da_s)
     for t in range(2):
         gsmall[0:9, t * 256 : (t + 1) * 256] = gtaps[t, 0:9, :]
+    hooks.sums(0)
+    narrow_rows(gin, af_s)
+    hooks.output()
+    hooks.sums(1)
+    hooks.point("N")
+    narrow_rows(gin, da_s)
     hooks.finished()
     hooks.point("R")
 
@@ -450,12 +454,12 @@
     def turn(self, name, i, count):
         pass
 
-    fore = point
+    sums = fore = point
 
     def weights(self):
         pass
 
-    cotangent = arrived = finished = weights
+    cotangent = near = arrived = finished = weights
 
 
 def block_kernel(images, lim, tok, cot, wi, wo, wu, wd, small, vecs, out, gin, grads, gsmall, *scratch):
@@ -708,37 +712,37 @@
 LATE = 5
 SLOTS = 12
 PLAN = {
-    'D0': ((0, 0),),
-    'U0': ((1, 0),),
-    'f0': ((0, 1),),
-    'f1': ((1, 1),),
-    'D1': ((2, 0),),
-    'U1': ((3, 0),),
-    'd0': ((2, 1), (3, 1), (0, 2),),
-    'd3': ((1, 2), (0, 3),),
-    'O': ((4, 0),),
-    'r0': ((4, 1),),
-    'r1': ((1, 3), (2, 2),),
-    'r2': ((0, 4),),
-    'r5': ((2, 3), (1, 4), (3, 2),),
-    'r7': ((0, 5), (4, 2),),
-    'A2': ((5, 0),),
-    'A1': ((6, 0), (3, 3), (5, 1), (2, 4), (6, 1),),
-    'A0': ((7, 0),),
-    'r8': ((7, 1), (0, 6),),
-    'r9': ((4, 3), (1, 5), (0, 7),),
-    'r10': ((3, 4),),
-    'r13': ((2, 5), (1, 6), (4, 4),),
-    'r14': ((1, 7),),
-    'B2': ((5, 2), (3, 5),),
-    'B1': ((6, 2), (5, 3), (4, 5), (2, 6),),
-    'B0': ((7, 2), (6, 3),),
-    'R': ((7, 3), (3, 6), (2, 7),),
+    'U0': ((0, 0),),
+    'f0': ((1, 0),),
+    'f3': ((0, 1),),
+    'D1': ((1, 1),),
+    'U1': ((2, 0),),
+    'd0': ((3, 0),),
+    'd1': ((2, 1), (3, 1),),
+    'd2': ((0, 2),),
+    'r0': ((4, 0),),
+    'r1': ((1, 2), (0, 3), (4, 1),),
+    'r5': ((1, 3),),
+    'r6': ((2, 2), (0, 4),),
+    'A1': ((5, 0),),
+    'A0': ((6, 0),),
+    'r8': ((7, 0), (5, 1), (6, 1), (3, 2), (2, 3), (1, 4), (7, 1),),
+    'r9': ((0, 5), (4, 2),),
+    'r12': ((3, 3), (2, 4),),
+    'r14': ((0, 6),),
+    'r15': ((4, 3), (1, 5), (0, 7),),
+    'B1': ((5, 2), (3, 4), (6, 2),),
+    's0': ((7, 2), (5, 3), (6, 3),),
+    's1': ((2, 5), (7, 3), (1, 6),),
+    's2': ((4, 4),),
+    's3': ((5, 4), (1, 7),),
+    'N': ((6, 4), (3, 5),),
 }
 TAIL = (
-    (3, 7), (5, 4), (4, 6), (4, 7), (6, 4), (5, 5),
-    (7, 4), (6, 5), (5, 6), (7, 5), (6, 6), (5, 7),
-    (5, 8), (7, 6), (6, 7), (6, 8), (7, 7), (7, 8),
+    (4, 5), (2, 6), (5, 5), (2, 7), (7, 4), (6, 5),
+    (3, 6), (5, 6), (3, 7), (4, 6), (7, 5), (4, 7),
+    (6, 6), (5, 7), (5, 8), (7, 6), (6, 7), (6, 8),
+    (7, 7), (7, 8),
 )
 
 
@@ -851,14 +855,16 @@
                 self.wi[self.x, part, rows, j * 128 : (j + 1) * 128] = four.astype(bf16)
 
     def begin(self):
-        for go in self.early:
+        for go in self.early[0:3]:
             go.start()
         barrier = pltpu.get_barrier_semaphore()
         for mate in (self.core_mate, self.x_mate, self.y_mate, *self.z_mates):
             pl.semaphore_signal(barrier, inc=1, device_id=mate, device_id_type=MESH)
+        for go in self.early[3:]:
+            go.start()
+        self.tok_load.start()
         for go in self.own_in:
             go.start()
-        self.tok_load.start()
         x, quarter, at_s = self.x, self.quarter, self.at_s
         self.small[x, 0:9, :] = self.taps[...]
         for j in range(4):
@@ -971,8 +977,10 @@
         self.others(body)
         self.cot_load.wait()
 
+    def near(self):
+        self.turned(5, 6)
+
     def arrived(self):
-        self.turned(5, 6)
         self.done(3, 4, 5, 6)
 
 
@@ -984,12 +992,18 @@
         src, dst = (
             (self.out_v, self.out),
             (self.gin_v, self.gin),
-            (self.grads.at[0], self.full),
         )[i]
         return pltpu.make_async_copy(src, dst, self.save.at[i])
 
     def finished(self):
         self.saving(1).start()
+
+    def keeping(self, c):
+        base, R = CHUNKS[c]
+        rows = pl.ds(base, R)
+        return pltpu.make_async_copy(
+            self.grads.at[0, rows, :], self.full.at[rows, :], self.save.at[2 + c]
+        )
 
 
     def copy(self, src, dst, chunk, slot, mate):
@@ -1110,6 +1124,8 @@
             grads[0, aligned(mine + y * quarter + z * piece, piece), :] = total(
                 ys[own, :], zs[0], zs[1], zs[2]
             )
+        if step == 7:
+            self.keeping(c).start()
         for flight in self.flights(c, s):
             flight.start()
 
@@ -1161,16 +1177,20 @@
                 def _(k=k):
                     self.point(name + str(k))
 
+    def sums(self, k):
+        self.small_stage(k)
+
     def end(self):
-        self.small_stage(0)
-        gap = len(TAIL) // 6
+        self.small_stage(2)
         for k, (c, s) in enumerate(TAIL):
             self.stage(c, s)
-            if k % gap == gap - 1 and k // gap < 4:
-                self.small_stage(k // gap + 1)
-        self.saving(2).start()
-        for i in range(3):
+            if k == len(TAIL) // 3:
+                self.small_stage(3)
+        self.small_stage(4)
+        for i in range(2):
             self.saving(i).wait()
+        for c in range(len(CHUNKS)):
+            self.keeping(c).wait()
 
 
 def main_kernel(images, counts, tok, cot, w_in, w_out, w_up, w_down, taps, bias, vecs,
@@ -1245,7 +1265,7 @@
             dma((8, 4)),
             dma((8, 4)),
             dma((21,)),
-            dma((3,)),
+            dma((2 + len(sizes),)),
         ],
         compiler_params=pltpu.CompilerParams(
             collective_id=1, has_side_effects=True, vmem_limit_bytes=63 * 1024 * 1024

time: 137 us -> 130 us (0.949)
  Pallas kernels: 136 us -> 129 us
    pallas_call x1, Pallas kernels: 118 us -> 110 us  [main_call(): pl.pallas_call(functools.partial(main_kernel, images), out_shape=(S(tok.s...]
where the time goes in v4:
time: 130 us
  Pallas kernels  129 us (99%)
    pallas_call x1, Pallas kernels, main_call(): pl.pallas_call(functools.partial(main_kernel, images), out_shape=(S(tok.s...  110 us
    pallas_call x1, Pallas kernels, adam_step(): pl.pallas_call(adam_kernel, out_shape=tuple((S(shape, kind) for shape in...  18.3 us

profile of v4, /device:TPU:0, one launch (start us, length us, event | category | flops | bytes accessed | tf_op | source)
XLA Modules:
  0.0 129.6 jit_solution(7487142187659876964)
XLA Ops:
  0.7 110.4 %shard_map.439 = (bf16[784,512]{1,0:T(8,128)(2,1)}, f32[784,512]{1,0:T(8,128)}, bf16[6144,256]{1,0:T(8,128)(2,1)}, f32[24,512]{1,0:T(8,128)}) custom-call(s32[16]{0:T(128)} %counts.1, bf16[784,512]{1,0:T(8,128)(2,1)} %tok.1, bf16[784,512]{1,0:T(8,128)(2,1)} %cot.1, f32[512,768]{1,0:T(8,128)} %refs_13_.1, f32[256,512]{1,0:T(8,128)} %refs_10_.1, ...), custom_call_target="tpu_custom_call" | custom-call | tf_op jit(solution)/shard_map/pallas_call | solution.py:1231
  111.1 18.3 %shard_map.440 = (f32[1024,512]{1,0:T(8,128)}, f32[1024,512]{1,0:T(8,128)}, f32[1024,512]{1,0:T(8,128)}, bf16[1024,512]{1,0:T(8,128)(2,1)}, f32[512,1024]{1,0:T(...) custom-call(bf16[6144,256]{1,0:T(8,128)(2,1)} %get-tuple-element.58., ...), custom_call_target="tpu_custom_call" | custom-call | tf_op jit(solution)/shard_map/pallas_call | solution.py:679

commit v5 on v4

--- a/solution.py
+++ b/solution.py
@@ -220,7 +220,7 @@
         la_s[rows, :] = la
         for t in range(2):
             dm_s[t, held(n), :] = nt(la, wo[t]).astype(bf16)
-        hooks.turn("d", n, images)
+        hooks.turn("d", n)
         return carry
 
     pick_row = lax.broadcasted_iota(jnp.int32, (256, 128), 0)
@@ -293,7 +293,7 @@
                     d_cols[b] = term if d_cols[b] is None else d_cols[b] + term
             d_field = roll1(d_cols[0], -1) + d_cols[1] + roll1(d_cols[2], 1)
             pj_s[t, 0, rows, ls] = jnp.where(inside, slope * d_field, 0.0).astype(bf16)
-            hooks.turn("r", turn + g, 4 * images)
+            hooks.turn("r", n, 2, turn + g)
 
     def rise(n, carry):
         rows = padded(n)
@@ -306,7 +306,7 @@
         gsmall[9:10, :] += row_sum(d_na * xhat)
         gsmall[10:11, :] += row_sum(d_na)
         da_s[rows, :] += norm_back(gain_a * d_na, xhat, r)
-        hooks.turn("s", n, images)
+        hooks.turn("s", n)
         return carry
 
     def narrow_rows(target, source):
@@ -385,7 +385,7 @@
 
     def feed_second(n, carry):
         feed(other_half, 1, n)
-        hooks.turn("f", n, images)
+        hooks.turn("f", n)
         return carry
 
     loop(0, images, feed_own, 0)
@@ -405,7 +405,7 @@
     hooks.point("O")
 
     def aft(n, carry):
-        recede(other_half, n, 2 * n)
+        recede(other_half, n, 0)
         return carry
 
     loop(0, images, aft, 0)
@@ -414,7 +414,7 @@
         hooks.point("A%d" % part)
 
     def aft2(n, carry):
-        recede(first_half, n, 2 * (images + n))
+        recede(first_half, n, 2 * images)
         return carry
 
     loop(0, images, aft2, 0)
@@ -451,7 +451,7 @@
     def point(self, name):
         pass
 
-    def turn(self, name, i, count):
+    def turn(self, name, n, stride=1, offset=0):
         pass
 
     sums = fore = point
@@ -715,34 +715,34 @@
     'U0': ((0, 0),),
     'f0': ((1, 0),),
     'f3': ((0, 1),),
-    'D1': ((1, 1),),
-    'U1': ((2, 0),),
-    'd0': ((3, 0),),
-    'd1': ((2, 1), (3, 1),),
+    'D1': ((1, 1), (2, 0),),
+    'd0': ((3, 0), (2, 1),),
+    'd1': ((3, 1),),
     'd2': ((0, 2),),
     'r0': ((4, 0),),
     'r1': ((1, 2), (0, 3), (4, 1),),
-    'r5': ((1, 3),),
-    'r6': ((2, 2), (0, 4),),
+    'r6': ((2, 2), (1, 3), (0, 4),),
     'A1': ((5, 0),),
     'A0': ((6, 0),),
-    'r8': ((7, 0), (5, 1), (6, 1), (3, 2), (2, 3), (1, 4), (7, 1),),
-    'r9': ((0, 5), (4, 2),),
-    'r12': ((3, 3), (2, 4),),
-    'r14': ((0, 6),),
-    'r15': ((4, 3), (1, 5), (0, 7),),
-    'B1': ((5, 2), (3, 4), (6, 2),),
-    's0': ((7, 2), (5, 3), (6, 3),),
-    's1': ((2, 5), (7, 3), (1, 6),),
-    's2': ((4, 4),),
-    's3': ((5, 4), (1, 7),),
-    'N': ((6, 4), (3, 5),),
+    'r8': ((7, 0), (5, 1), (6, 1), (3, 2), (2, 3),),
+    'r9': ((7, 1), (4, 2), (1, 4),),
+    'r10': ((0, 5),),
+    'r12': ((3, 3),),
+    'r13': ((4, 3), (2, 4),),
+    'r15': ((1, 5), (0, 6),),
+    'B1': ((5, 2),),
+    'B0': ((6, 2), (3, 4), (7, 2), (5, 3), (4, 4), (0, 7), (6, 3),),
+    's0': ((7, 3), (1, 6),),
+    's1': ((2, 5), (5, 4), (1, 7),),
+    's2': ((6, 4),),
+    's3': ((3, 5), (7, 4),),
+    'N': ((4, 5),),
+    'R': ((5, 5),),
 }
 TAIL = (
-    (4, 5), (2, 6), (5, 5), (2, 7), (7, 4), (6, 5),
-    (3, 6), (5, 6), (3, 7), (4, 6), (7, 5), (4, 7),
-    (6, 6), (5, 7), (5, 8), (7, 6), (6, 7), (6, 8),
-    (7, 7), (7, 8),
+    (2, 6), (6, 5), (2, 7), (7, 5), (3, 6), (4, 6),
+    (3, 7), (5, 6), (4, 7), (6, 6), (7, 6), (5, 7),
+    (5, 8), (6, 7), (6, 8), (7, 7), (7, 8),
 )
 
 
@@ -1169,13 +1169,14 @@
         for c, s in PLAN.get(name, ()):
             self.stage(c, s)
 
-    def turn(self, name, i, count):
-        for k in range(count):
-            if name + str(k) in PLAN:
-
-                @pl.when(i == k)
-                def _(k=k):
-                    self.point(name + str(k))
+    def turn(self, name, n, stride=1, offset=0):
+        for j in range(self.images):
+            key = name + str(j * stride + offset)
+            if key in PLAN:
+
+                @pl.when(n == j)
+                def _(key=key):
+                    self.point(key)
 
     def sums(self, k):
         self.small_stage(k)

time: 130 us -> 127 us (0.977)
  Pallas kernels: 129 us -> 126 us
    pallas_call x1, Pallas kernels: 110 us -> 107 us  [main_call(): pl.pallas_call(functools.partial(main_kernel, images), out_shape=(S(tok.s...]
where the time goes in v5:
time: 127 us
  Pallas kernels  126 us (99%)
    pallas_call x1, Pallas kernels, main_call(): pl.pallas_call(functools.partial(main_kernel, images), out_shape=(S(tok.s...  107 us
    pallas_call x1, Pallas kernels, adam_step(): pl.pallas_call(adam_kernel, out_shape=tuple((S(shape, kind) for shape in...  18.3 us

profile of v5, /device:TPU:0, one launch (start us, length us, event | category | flops | bytes accessed | tf_op | source)
XLA Modules:
  0.0 126.5 jit_solution(687781246924987895)
XLA Ops:
  0.7 107.3 %shard_map.439 = (bf16[784,512]{1,0:T(8,128)(2,1)}, f32[784,512]{1,0:T(8,128)}, bf16[6144,256]{1,0:T(8,128)(2,1)}, f32[24,512]{1,0:T(8,128)}) custom-call(s32[16]{0:T(128)} %counts.1, bf16[784,512]{1,0:T(8,128)(2,1)} %tok.1, bf16[784,512]{1,0:T(8,128)(2,1)} %cot.1, f32[512,768]{1,0:T(8,128)} %refs_13_.1, f32[256,512]{1,0:T(8,128)} %refs_10_.1, ...), custom_call_target="tpu_custom_call" | custom-call | tf_op jit(solution)/shard_map/pallas_call | solution.py:1232
  108.0 18.3 %shard_map.440 = (f32[1024,512]{1,0:T(8,128)}, f32[1024,512]{1,0:T(8,128)}, f32[1024,512]{1,0:T(8,128)}, bf16[1024,512]{1,0:T(8,128)(2,1)}, f32[512,1024]{1,0:T(...) custom-call(bf16[6144,256]{1,0:T(8,128)(2,1)} %get-tuple-element.58., ...), custom_call_target="tpu_custom_call" | custom-call | tf_op jit(solution)/shard_map/pallas_call | solution.py:679

commit v6 on v5

--- a/solution.py
+++ b/solution.py
@@ -715,34 +715,37 @@
     'U0': ((0, 0),),
     'f0': ((1, 0),),
     'f3': ((0, 1),),
-    'D1': ((1, 1), (2, 0),),
-    'd0': ((3, 0), (2, 1),),
-    'd1': ((3, 1),),
-    'd2': ((0, 2),),
+    'D1': ((1, 1),),
+    'U1': ((2, 0),),
+    'd0': ((3, 0),),
+    'd1': ((2, 1),),
+    'd2': ((3, 1), (0, 2),),
     'r0': ((4, 0),),
-    'r1': ((1, 2), (0, 3), (4, 1),),
-    'r6': ((2, 2), (1, 3), (0, 4),),
+    'r1': ((1, 2),),
+    'r2': ((4, 1), (0, 3),),
+    'r6': ((2, 2), (1, 3),),
+    'A2': ((0, 4),),
     'A1': ((5, 0),),
     'A0': ((6, 0),),
-    'r8': ((7, 0), (5, 1), (6, 1), (3, 2), (2, 3),),
-    'r9': ((7, 1), (4, 2), (1, 4),),
-    'r10': ((0, 5),),
+    'r8': ((7, 0), (5, 1), (3, 2), (6, 1), (2, 3),),
+    'r9': ((7, 1), (1, 4),),
+    'r10': ((4, 2),),
+    'r11': ((0, 5),),
     'r12': ((3, 3),),
     'r13': ((4, 3), (2, 4),),
     'r15': ((1, 5), (0, 6),),
     'B1': ((5, 2),),
-    'B0': ((6, 2), (3, 4), (7, 2), (5, 3), (4, 4), (0, 7), (6, 3),),
-    's0': ((7, 3), (1, 6),),
-    's1': ((2, 5), (5, 4), (1, 7),),
-    's2': ((6, 4),),
-    's3': ((3, 5), (7, 4),),
-    'N': ((4, 5),),
-    'R': ((5, 5),),
+    'B0': ((6, 2), (3, 4), (7, 2), (0, 7), (5, 3),),
+    's0': ((6, 3), (4, 4), (7, 3), (1, 6),),
+    's2': ((5, 4), (2, 5), (1, 7),),
+    's3': ((6, 4),),
+    'N': ((3, 5), (7, 4),),
+    'R': ((4, 5),),
 }
 TAIL = (
-    (2, 6), (6, 5), (2, 7), (7, 5), (3, 6), (4, 6),
-    (3, 7), (5, 6), (4, 7), (6, 6), (7, 6), (5, 7),
-    (5, 8), (6, 7), (6, 8), (7, 7), (7, 8),
+    (5, 5), (2, 6), (6, 5), (2, 7), (7, 5), (3, 6),
+    (4, 6), (5, 6), (3, 7), (4, 7), (6, 6), (7, 6),
+    (5, 7), (5, 8), (6, 7), (6, 8), (7, 7), (7, 8),
 )
 
 

time: 127 us -> 127 us (level)
  no operation moved by 1% of the time
where the time goes in v6:
time: 127 us; the launch traced here: 126 us
  Pallas kernels  125 us (98%)
    pallas_call x1, Pallas kernels, main_call(): pl.pallas_call(functools.partial(main_kernel, images), out_shape=(S(tok.s...  107 us
    pallas_call x1, Pallas kernels, adam_step(): pl.pallas_call(adam_kernel, out_shape=tuple((S(shape, kind) for shape in...  18.3 us

profile of v6, /device:TPU:0, one launch (start us, length us, event | category | flops | bytes accessed | tf_op | source)
XLA Modules:
  0.0 126.3 jit_solution(10651010619519251623)
XLA Ops:
  0.7 107.1 %shard_map.439 = (bf16[784,512]{1,0:T(8,128)(2,1)}, f32[784,512]{1,0:T(8,128)}, bf16[6144,256]{1,0:T(8,128)(2,1)}, f32[24,512]{1,0:T(8,128)}) custom-call(s32[16]{0:T(128)} %counts.1, bf16[784,512]{1,0:T(8,128)(2,1)} %tok.1, bf16[784,512]{1,0:T(8,128)(2,1)} %cot.1, f32[512,768]{1,0:T(8,128)} %refs_13_.1, f32[256,512]{1,0:T(8,128)} %refs_10_.1, ...), custom_call_target="tpu_custom_call" | custom-call | tf_op jit(solution)/shard_map/pallas_call | solution.py:1235
  107.7 18.3 %shard_map.440 = (f32[1024,512]{1,0:T(8,128)}, f32[1024,512]{1,0:T(8,128)}, f32[1024,512]{1,0:T(8,128)}, bf16[1024,512]{1,0:T(8,128)(2,1)}, f32[512,1024]{1,0:T(...) custom-call(bf16[6144,256]{1,0:T(8,128)(2,1)} %get-tuple-element.58., ...), custom_call_target="tpu_custom_call" | custom-call | tf_op jit(solution)/shard_map/pallas_call | solution.py:679
